TPU v7x, 128 devices: a whole 4x4x4 slice. The times are simulated.
128 devices in a mesh: row: 8 (over z, core), col: 16 (over x, y).
Axes of the slice: x: 4, y: 4, z: 4, core: 2. Of those that a mesh axis runs over, the one named last changes fastest.
Arguments:
- inputs: bfloat16 [1024, 12288], P('col', 'row'), may hold values from -6 to 6
- w_in: bfloat16 [12288, 24576], P('row', 'col'), may hold values from -0.0546875 to 0.0546875
- w_out: bfloat16 [24576, 12288], P('col', 'row'), may hold values from -0.0390625 to 0.0390625
- cotangent: bfloat16 [1024, 12288], P('col', 'row'), may hold values from -3 to 3
Outputs:
- output: bfloat16 [1024, 12288], P('col', 'row')
- grad_inputs: bfloat16 [1024, 12288], P('col', 'row')
- grad_w_in: bfloat16 [12288, 24576], P('row', 'col')
- grad_w_out: bfloat16 [24576, 12288], P('col', 'row')
All inputs are finite; a program needn't handle non-finite values.
Results may differ from a plain program's by a relative error of at most 0.005.
Values may be sent and summed in bfloat16 or wider, within the bound.
No kernel may reach another device: no remote copies, remote signals or barrier semaphores. Data moves between devices by JAX's collectives and lax.ppermute only.
A program may use at most 128 MiB of HBM per device.

v0:
```python
import jax
import jax.numpy as jnp
from jax import lax
from jax.sharding import PartitionSpec as P


def gelu_form(value):
    return jax.nn.gelu(value, approximate=True)


def gelu_backward(value, grad):
    return jax.vjp(gelu_form, value)[1](grad)[0]


def times_transposed(left, right):
    return lax.dot_general(
        left, right, (((1,), (1,)), ((), ())), preferred_element_type=jnp.float32
    )


def transposed_times(left, right):
    return lax.dot_general(
        left, right, (((0,), (0,)), ((), ())), preferred_element_type=jnp.float32
    )


def gather_tokens(block):
    return lax.all_gather(block, "col", axis=0, tiled=True)


def gather_hidden(block):
    return lax.all_gather(block, "row", axis=0, tiled=True)


def scatter_hidden(term, count):
    return lax.psum_scatter(
        term(jnp.int32(0), lax.axis_size("row") * count), "row", scatter_dimension=0, tiled=True
    )


def scatter_features(term, count):
    return lax.psum_scatter(
        term(jnp.int32(0), lax.axis_size("col") * count), "col", scatter_dimension=0, tiled=True
    )


def local(inputs, w_in, w_out, cotangent):
    full_inputs = gather_tokens(inputs)
    tokens = full_inputs.shape[0]
    hidden_count = tokens // lax.axis_size("row")
    feature_count = inputs.shape[0]

    def hidden_term(start, count):
        return jnp.dot(full_inputs, w_in, preferred_element_type=jnp.float32)

    hidden = scatter_hidden(hidden_term, hidden_count)
    activated_all = gather_hidden(gelu_form(hidden).astype(jnp.bfloat16))

    def output_term(start, count):
        return jnp.dot(activated_all, w_out, preferred_element_type=jnp.float32)

    output = scatter_features(output_term, feature_count).astype(jnp.bfloat16)
    full_cotangent = gather_tokens(cotangent)
    grad_w_out = transposed_times(activated_all, full_cotangent).astype(jnp.bfloat16)

    def grad_term(start, count):
        return times_transposed(full_cotangent, w_out)

    grad_activated = scatter_hidden(grad_term, hidden_count)
    grad_hidden_all = gather_hidden(gelu_backward(hidden, grad_activated).astype(jnp.bfloat16))
    grad_w_in = transposed_times(full_inputs, grad_hidden_all).astype(jnp.bfloat16)

    def input_term(start, count):
        return times_transposed(grad_hidden_all, w_in)

    grad_inputs = scatter_features(input_term, feature_count).astype(jnp.bfloat16)
    return (output, grad_inputs, grad_w_in, grad_w_out)


def solution(mesh):
    in_specs = (P("col", "row"), P("row", "col"), P("col", "row"), P("col", "row"))
    out_specs = (P("col", "row"), P("col", "row"), P("row", "col"), P("col", "row"))
    return jax.shard_map(local, mesh=mesh, in_specs=in_specs, out_specs=out_specs, check_vma=False)
```

profile of v0, /device:TPU:1, one launch (start us, length us, event | category | flops | bytes accessed | tf_op | source)
XLA Modules:
  0.0 435.6 jit_solution(15179679156619263174)
XLA Ops:
  7.2 0.0 all-gather.5.cloned.1.call-start
  7.2 0.7 all-gather.5.cloned.1.call-update
  7.9 0.0 all-gather.9.cloned.1.call-start
  7.9 0.7 all-gather.9.cloned.1.call-update
  8.6 0.0 reduce-scatter.5.cloned.1.call-start
  8.7 52.2 %all-gather.5.cloned.1.call-done = bf16[1024,1536]{1,0:T(8,128)(2,1)} async-done(((bf16[64,1536]{1,0:T(8,128)(2,1)}), bf16[1024,1536]{1,0:T(8,128)(2,1)}) %all-gather.5.cloned.1.call-update) | async-done | bytes 3145744 | tf_op jit(solution)/shard_map/all_gather | solution.py:28
  60.9 9.7 %fusion.8 = f32[1024,1536]{1,0:T(8,128)} fusion(bf16[1024,1536]{1,0:T(8,128)(2,1)} %all-gather.5.cloned.1.call-done, bf16[1536,1536]{1,0:T(8,128)(2,1)} %param.5), kind=kOutput, calls=%fused_computation.13 | convolution fusion | flops 4831838208 | bytes 14155776 | tf_op jit(solution)/shard_map/dot_general | solution.py:54
  70.6 0.0 reduce-scatter.5.cloned.1.call-update
  70.7 0.0 reduce-scatter.9.cloned.1.call-start
  70.7 39.2 %all-gather.9.cloned.1.call-done = bf16[1024,1536]{1,0:T(8,128)(2,1)} async-done(((bf16[64,1536]{1,0:T(8,128)(2,1)}), bf16[1024,1536]{1,0:T(8,128)(2,1)}) %all-gather.9.cloned.1.call-update) | async-done | bytes 3145744 | tf_op jit(solution)/shard_map/all_gather | solution.py:28
  109.9 9.7 %fusion.10 = f32[1024,1536]{1,0:T(8,128)} fusion(bf16[1024,1536]{1,0:T(8,128)(2,1)} %all-gather.9.cloned.1.call-done, bf16[1536,1536]{1,0:T(8,128)(2,1)} %param.6), kind=kOutput, calls=%fused_computation.15 | convolution fusion | flops 4831838208 | bytes 14155776 | tf_op jit(solution)/shard_map/dot_general | solution.py:16
  119.7 0.0 reduce-scatter.9.cloned.1.call-update
  119.7 0.0 all-gather.7.cloned.1.call-start
  119.7 33.9 %reduce-scatter.5.cloned.1.call-done = f32[128,1536]{1,0:T(8,128)} async-done(((f32[1024,1536]{1,0:T(8,128)}), f32[128,1536]{1,0:T(8,128)}) %reduce-scatter.5.cloned.1.call-update) | async-done | bytes 786448 | tf_op jit(solution)/shard_map/reduce_scatter | solution.py:36
  153.6 44.6 %reduce-scatter.9.cloned.1.call-done = f32[128,1536]{1,0:T(8,128)} async-done(((f32[1024,1536]{1,0:T(8,128)}), f32[128,1536]{1,0:T(8,128)}) %reduce-scatter.9.cloned.1.call-update) | async-done | bytes 786448 | tf_op jit(solution)/shard_map/reduce_scatter | solution.py:36
  198.2 2.8 fusion.7
  201.0 0.0 all-gather.7.cloned.1.call-update
  201.0 0.0 all-gather.11.cloned.1.call-start
  201.1 0.5 all-gather.11.cloned.1.call-update
  201.6 0.0 reduce-scatter.7.cloned.1.call-start
  201.6 28.2 %all-gather.7.cloned.1.call-done = bf16[1024,1536]{1,0:T(8,128)(2,1)} async-done(((bf16[128,1536]{1,0:T(8,128)(2,1)}), bf16[1024,1536]{1,0:T(8,128)(2,1)}) %all-gather.7.cloned.1.call-update) | async-done | bytes 3145744 | tf_op jit(solution)/shard_map/all_gather | solution.py:32
  229.8 9.7 %fusion.9 = f32[1024,1536]{1,0:T(8,128)} fusion(bf16[1024,1536]{1,0:T(8,128)(2,1)} %all-gather.7.cloned.1.call-done, bf16[1536,1536]{1,0:T(8,128)(2,1)} %param.6), kind=kOutput, calls=%fused_computation.14 | convolution fusion | flops 4831838208 | bytes 14155776 | tf_op jit(solution)/shard_map/dot_general | solution.py:60
  239.5 0.0 reduce-scatter.7.cloned.1.call-update
  239.6 0.2 reduce-scatter.11.cloned.1.call-start
  239.8 20.0 %all-gather.11.cloned.1.call-done = bf16[1024,1536]{1,0:T(8,128)(2,1)} async-done(((bf16[128,1536]{1,0:T(8,128)(2,1)}), bf16[1024,1536]{1,0:T(8,128)(2,1)}) %all-gather.11.cloned.1.call-update) | async-done | bytes 3145744 | tf_op jit(solution)/shard_map/all_gather | solution.py:32
  259.8 9.7 %fusion.11 = f32[1024,1536]{1,0:T(8,128)} fusion(bf16[1024,1536]{1,0:T(8,128)(2,1)} %all-gather.11.cloned.1.call-done, bf16[1536,1536]{1,0:T(8,128)(2,1)} %param.5), kind=kOutput, calls=%fused_computation.16 | convolution fusion | flops 4831838208 | bytes 14155776 | tf_op jit(solution)/shard_map/dot_general | solution.py:16
  269.6 0.0 copy-start
  269.6 0.0 reduce-scatter.11.cloned.1.call-update
  269.6 1.9 copy-done
  271.5 8.9 %fusion = bf16[1536,1536]{0,1:T(8,128)(2,1)} fusion(bf16[1024,1536]{1,0:T(8,128)(2,1)} %all-gather.11.cloned.1.call-done, bf16[1024,1536]{1,0:T(8,128)(2,1)S(1)} %copy-done), kind=kOutput, calls=%fused_computation.2 | convolution fusion | flops 4834197504 | bytes 11010048 | tf_op jit(solution)/shard_map/dot_general | solution.py:22
  280.4 0.0 copy-start.1
  280.4 6.9 %copy.8 = bf16[1536,1536]{1,0:T(8,128)(2,1)} copy(bf16[1536,1536]{0,1:T(8,128)(2,1)} %fusion) | data formatting | bytes 9437184
  287.3 0.0 copy-done.1
  287.3 8.7 %convolution_convert_fusion = bf16[1536,1536]{1,0:T(8,128)(2,1)} fusion(bf16[1024,1536]{1,0:T(8,128)(2,1)} %all-gather.7.cloned.1.call-done, bf16[1024,1536]{1,0:T(8,128)(2,1)S(1)} %copy-done.1), kind=kOutput, calls=%fused_computation | convolution fusion | flops 4834197504 | bytes 11010048 | tf_op jit(solution)/shard_map/dot_general | solution.py:22
  296.0 47.1 %reduce-scatter.7.cloned.1.call-done = f32[64,1536]{1,0:T(8,128)} async-done(((f32[1024,1536]{1,0:T(8,128)}), f32[64,1536]{1,0:T(8,128)}) %reduce-scatter.7.cloned.1.call-update) | async-done | bytes 393232 | tf_op jit(solution)/shard_map/reduce_scatter | solution.py:42
  343.0 1.7 convert_element_type.22
  344.7 82.4 %reduce-scatter.11.cloned.1.call-done = f32[64,1536]{1,0:T(8,128)} async-done(((f32[1024,1536]{1,0:T(8,128)}), f32[64,1536]{1,0:T(8,128)}) %reduce-scatter.11.cloned.1.call-update) | async-done | bytes 393232 | tf_op jit(solution)/shard_map/reduce_scatter | solution.py:42
  427.1 1.7 convert_element_type.24
Async XLA Ops:
  7.2 53.8 %all-gather.5.cloned.1.call-start = ((), (), s32[]{:S(2)}) async-start(), calls=%async_computation.4 | async-start | bytes 3342336 | tf_op jit(solution)/shard_map/all_gather | solution.py:28
  7.9 102.0 %all-gather.9.cloned.1.call-start = ((), (), s32[]{:S(2)}) async-start(), calls=%async_computation.8 | async-start | bytes 3342336 | tf_op jit(solution)/shard_map/all_gather | solution.py:28
  8.6 145.0 %reduce-scatter.5.cloned.1.call-start = ((), (), s32[]{:S(2)}) async-start(), calls=%async_computation.5 | async-start | bytes 7077888 | tf_op jit(solution)/shard_map/reduce_scatter | solution.py:36
  70.7 127.5 %reduce-scatter.9.cloned.1.call-start = ((), (), s32[]{:S(2)}) async-start(), calls=%async_computation.9 | async-start | bytes 7077888 | tf_op jit(solution)/shard_map/reduce_scatter | solution.py:36
  119.7 110.1 %all-gather.7.cloned.1.call-start = ((), (), s32[]{:S(2)}) async-start(), calls=%async_computation.6 | async-start | bytes 3538944 | tf_op jit(solution)/shard_map/all_gather | solution.py:32
  201.0 58.8 %all-gather.11.cloned.1.call-start = ((), (), s32[]{:S(2)}) async-start(), calls=%async_computation.10 | async-start | bytes 3538944 | tf_op jit(solution)/shard_map/all_gather | solution.py:32
  201.6 141.5 %reduce-scatter.7.cloned.1.call-start = ((), (), s32[]{:S(2)}) async-start(), calls=%async_computation.7 | async-start | bytes 6684672 | tf_op jit(solution)/shard_map/reduce_scatter | solution.py:42
  239.6 187.5 %reduce-scatter.11.cloned.1.call-start = ((), (), s32[]{:S(2)}) async-start(), calls=%async_computation.11 | async-start | bytes 6684672 | tf_op jit(solution)/shard_map/reduce_scatter | solution.py:42
  269.6 1.9 copy-start
  280.4 6.9 %copy-start.1 = (bf16[1024,1536]{1,0:T(8,128)(2,1)S(1)}, bf16[1024,1536]{1,0:T(8,128)(2,1)}, u32[]{:S(2)}) copy-start(bf16[1024,1536]{1,0:T(8,128)(2,1)} %all-gather.9.cloned.1.call-done) | copy-start | bytes 9437188
Sparse Core Ops, SparseCore 0:
  10.2 50.7 all-gather.4
  63.1 46.7 all-gather.8
  112.3 41.2 reduce-scatter.4
  155.9 42.2 reduce-scatter.8
  201.1 28.6 all-gather.6
  231.9 27.8 all-gather.10
  263.3 79.7 reduce-scatter.6
  346.5 80.5 reduce-scatter.10
where the time goes:
time: 436 us
  waiting for transfers between devices  350 us (80%)
  matrix products  56.6 us (13%)
  between operations  14.1 us (3%)
  local copies, waits for them, and re-layouts  8.72 us (2%)
  other arithmetic  6.19 us (1%)
    reduce_scatter x2, waiting for transfers between devices, scatter_features(): lax.psum_scatter(term(jnp.int32(0), lax.axis_size('col') * count), 'col',...  129 us
    all_gather x2, waiting for transfers between devices, gather_tokens(): return lax.all_gather(block, 'col', axis=0, tiled=True)  91.4 us
    reduce_scatter x2, waiting for transfers between devices, scatter_hidden(): lax.psum_scatter(term(jnp.int32(0), lax.axis_size('row') * count), 'row',...  78.4 us
    all_gather x2, waiting for transfers between devices, gather_hidden(): return lax.all_gather(block, 'row', axis=0, tiled=True)  48.2 us
    dot_general x2, matrix products, times_transposed(): lax.dot_general(left, right, (((1,), (1,)), ((), ())), preferred_element_...  19.5 us
    dot_general x2, matrix products, transposed_times(): lax.dot_general(left, right, (((0,), (0,)), ((), ())), preferred_element_...  17.7 us
    dot_general x1, matrix products, output_term(): return jnp.dot(activated_all, w_out, preferred_element_type=jnp.float32)  9.71 us
    dot_general x1, matrix products, hidden_term(): return jnp.dot(full_inputs, w_in, preferred_element_type=jnp.float32)  9.71 us
  transfers between devices with their start and end apart: 8, of which 8 were waited for; matrix products, arithmetic and copies ran while one was open for 15% of the time, Pallas kernels for 0%

commit v1 on v0

v1 whole, which is shorter than its diff:
```python
import functools

import jax
import jax.numpy as jnp
from jax import lax
from jax.experimental import pallas as pl
from jax.experimental.pallas import tpu as pltpu
from jax.sharding import PartitionSpec as P

BF16 = jnp.bfloat16
F32 = jnp.float32
AXES = ("row", "col")
RING = 4
TILE = 256
LIMIT = 40 * 1024 * 1024


def gelu_form(value):
    return jax.nn.gelu(value, approximate=True)


def gelu_backward(value, grad):
    return jax.vjp(gelu_form, value)[1](grad)[0]


def permutation(first=0, second=0, up=0, other=0):
    pairs = []
    for z in range(RING):
        for core in range(2):
            for x in range(RING):
                for y in range(RING):
                    step_x, step_y = (first, second) if core == 0 else (second, first)
                    to_row = ((z + up) % RING) * 2 + (core + other) % 2
                    to_col = ((x + step_x) % RING) * RING + (y + step_y) % RING
                    pairs.append(((z * 2 + core) * 16 + x * RING + y, to_row * 16 + to_col))
    return pairs


def send(block, **where):
    return lax.ppermute(block, AXES, permutation(**where))


def swap(block):
    return send(block, other=1)


def gather_ring(block, axis):
    return [block] + [send(block, **{axis: -step}) for step in range(1, RING)]


def scatter_ring(blocks, axis):
    got = [send(blocks[step], **{axis: step}) for step in range(1, RING)]
    total = blocks[0].astype(F32)
    for block in got:
        total = total + block.astype(F32)
    return total


def cost(rows, depth, columns, moved):
    return pl.CostEstimate(flops=2 * rows * depth * columns, bytes_accessed=moved, transcendentals=0)


def dot(left, right, transposed):
    return lax.dot_general(left, right, (((1,), (1 if transposed else 0,)), ((), ())), preferred_element_type=F32)


def up_kernel(transposed, place, p0, p1, p2, p3, w_own, w_other, h0, h1, h2, h3, own, other, scratch):
    rows = p0.shape[0]
    depth = own.shape[1]

    @pl.when(pl.program_id(0) == 0)
    def _():
        for index, piece in enumerate((p0, p1, p2, p3)):
            own[index * rows : (index + 1) * rows, :] = piece[:, :depth]
            other[index * rows : (index + 1) * rows, :] = piece[:, depth:]

    total = dot(own[...], w_own[...], transposed) + dot(other[...], w_other[...], transposed)
    scratch[...] = total.astype(BF16)
    for index, out in enumerate((h0, h1, h2, h3)):
        start = pl.multiple_of(lax.rem(place[0] + index, RING) * rows, rows)
        out[...] = scratch[pl.ds(start, rows), :]


def project_up(place, pieces, w_own, w_other, transposed):
    rows, width = pieces[0].shape
    depth = width // 2
    columns = w_own.shape[0 if transposed else 1]
    tile = min(TILE, columns)
    whole = pl.BlockSpec((rows, width), lambda n: (0, 0))
    if transposed:
        weight = pl.BlockSpec((tile, depth), lambda n: (n, 0))
    else:
        weight = pl.BlockSpec((depth, tile), lambda n: (0, n))
    kept = pl.BlockSpec((RING * rows, depth), lambda n: (0, 0))
    outs = pl.pallas_call(
        functools.partial(up_kernel, transposed),
        grid=(columns // tile,),
        in_specs=[pl.BlockSpec(memory_space=pltpu.SMEM)] + [whole] * RING + [weight] * 2,
        out_specs=[pl.BlockSpec((rows, tile), lambda n: (0, n))] * RING + [kept] * 2,
        out_shape=[jax.ShapeDtypeStruct((rows, columns), BF16)] * RING
        + [jax.ShapeDtypeStruct((RING * rows, depth), BF16)] * 2,
        scratch_shapes=[pltpu.VMEM((RING * rows, tile), BF16)],
        compiler_params=pltpu.CompilerParams(vmem_limit_bytes=LIMIT),
        cost_estimate=cost(RING * rows, width, columns, 2 * (width * columns + 2 * RING * rows * width)),
    )(place, *pieces, w_own, w_other)
    return outs[:RING], outs[RING], outs[RING + 1]


def down_kernel(transposed, place, p0, p1, p2, p3, w_own, w_other, y0, y1, y2, y3, kept):
    rows = p0.shape[0]
    depth = p0.shape[1]
    step = pl.program_id(0)
    half = pl.num_programs(0) // 2

    @pl.when(step == 0)
    def _():
        for index, piece in enumerate((p0, p1, p2, p3)):
            start = pl.multiple_of(lax.rem(place[0] + index, RING) * rows, rows)
            kept[pl.ds(start, rows), :] = piece[...]

    def finish(weight):
        total = dot(kept[...], weight[...], transposed).astype(BF16)
        for index, out in enumerate((y0, y1, y2, y3)):
            out[...] = total[index * rows : (index + 1) * rows, :]

    @pl.when(step < half)
    def _():
        finish(w_own)

    @pl.when(step >= half)
    def _():
        finish(w_other)


def project_down(place, pieces, w_own, w_other, transposed):
    rows, depth = pieces[0].shape
    columns = w_own.shape[0 if transposed else 1]
    tile = min(TILE, columns)
    half = columns // tile
    whole = pl.BlockSpec((rows, depth), lambda n: (0, 0))
    if transposed:
        own = pl.BlockSpec((tile, depth), lambda n: (jnp.minimum(n, half - 1), 0))
        other = pl.BlockSpec((tile, depth), lambda n: (jnp.maximum(n - half, 0), 0))
    else:
        own = pl.BlockSpec((depth, tile), lambda n: (0, jnp.minimum(n, half - 1)))
        other = pl.BlockSpec((depth, tile), lambda n: (0, jnp.maximum(n - half, 0)))
    outs = pl.pallas_call(
        functools.partial(down_kernel, transposed),
        grid=(2 * half,),
        in_specs=[pl.BlockSpec(memory_space=pltpu.SMEM)] + [whole] * RING + [own, other],
        out_specs=[pl.BlockSpec((rows, tile), lambda n: (0, n))] * RING
        + [pl.BlockSpec((RING * rows, depth), lambda n: (0, 0))],
        out_shape=[jax.ShapeDtypeStruct((rows, 2 * columns), BF16)] * RING
        + [jax.ShapeDtypeStruct((RING * rows, depth), BF16)],
        compiler_params=pltpu.CompilerParams(vmem_limit_bytes=LIMIT),
        cost_estimate=cost(
            RING * rows, depth, 2 * columns, 2 * (2 * depth * columns + 2 * RING * rows * (depth + columns))
        ),
    )(place, *pieces, w_own, w_other)
    return outs[:RING], outs[RING]


def weight_kernel(l_own, l_other, r_own, r_other, out):
    dims = (((0,), (0,)), ((), ()))
    total = lax.dot_general(l_own[...], r_own[...], dims, preferred_element_type=F32)
    total = total + lax.dot_general(l_other[...], r_other[...], dims, preferred_element_type=F32)
    out[...] = total.astype(BF16)


def weight_grad(l_own, l_other, r_own, r_other):
    tokens, rows = l_own.shape
    columns = r_own.shape[1]
    tile = min(TILE, rows)
    left = pl.BlockSpec((tokens, tile), lambda m: (0, m))
    right = pl.BlockSpec((tokens, columns), lambda m: (0, 0))
    return pl.pallas_call(
        weight_kernel,
        grid=(rows // tile,),
        in_specs=[left, left, right, right],
        out_specs=pl.BlockSpec((tile, columns), lambda m: (m, 0)),
        out_shape=jax.ShapeDtypeStruct((rows, columns), BF16),
        compiler_params=pltpu.CompilerParams(vmem_limit_bytes=LIMIT),
        cost_estimate=cost(rows, 2 * tokens, columns, 2 * (rows * columns + 2 * tokens * (rows + columns))),
    )(l_own, l_other, r_own, r_other)


def gather_tokens(block):
    return gather_ring(jnp.concatenate(gather_ring(block, "first"), axis=0), "second")


def scatter_features(pieces):
    total = scatter_ring(pieces, "second")
    rows = total.shape[0] // RING
    blocks = [total[i * rows : (i + 1) * rows].astype(BF16) for i in range(RING)]
    return scatter_ring(blocks, "first").astype(BF16)


def local(inputs, w_in, w_out, cotangent):
    row = lax.axis_index("row")
    core = lax.rem(row, 2)
    place = jnp.reshape(lax.div(row, 2), (1,)).astype(jnp.int32)
    half, width = inputs.shape[0] // 2, inputs.shape[1]

    both = jnp.stack([inputs, cotangent]).reshape(2, 2, half, width)
    mine = lax.dynamic_index_in_dim(both, core, 1, keepdims=False)
    theirs = lax.dynamic_index_in_dim(both, 1 - core, 1, keepdims=False)
    chip = jnp.concatenate([mine, swap(theirs)], axis=2)
    w_in_other = swap(w_in)
    w_out_other = swap(w_out)

    input_pieces = gather_tokens(chip[0])
    cotangent_pieces = gather_tokens(chip[1])

    hidden_parts, input_own, input_sent = project_up(place, input_pieces, w_in, w_in_other, False)
    hidden = scatter_ring(hidden_parts, "up")
    grad_parts, cotangent_own, cotangent_sent = project_up(place, cotangent_pieces, w_out, w_out_other, True)

    activated = gather_ring(gelu_form(hidden).astype(BF16), "up")
    grad_activated = scatter_ring(grad_parts, "up")

    output_parts, activated_own = project_down(place, activated, w_out, w_out_other, False)
    grad_hidden = gather_ring(gelu_backward(hidden, grad_activated).astype(BF16), "up")
    output_half = scatter_features(output_parts)

    input_parts, grad_hidden_own = project_down(place, grad_hidden, w_in, w_in_other, True)
    grad_inputs_half = scatter_features(input_parts)

    grad_w_out = weight_grad(activated_own, swap(activated_own), cotangent_own, swap(cotangent_sent))
    grad_w_in = weight_grad(input_own, swap(input_sent), grad_hidden_own, swap(grad_hidden_own))

    def whole(part):
        kept, got = part[:, :width], swap(part[:, width:])
        return jnp.where(core == 0, jnp.concatenate([kept, got]), jnp.concatenate([got, kept]))

    return (whole(output_half), whole(grad_inputs_half), grad_w_in, grad_w_out)


def solution(mesh):
    in_specs = (P("col", "row"), P("row", "col"), P("col", "row"), P("col", "row"))
    out_specs = (P("col", "row"), P("col", "row"), P("row", "col"), P("col", "row"))
    return jax.shard_map(local, mesh=mesh, in_specs=in_specs, out_specs=out_specs, check_vma=False)
```

time: 436 us -> 231 us (0.53)
  waiting for transfers between devices: 350 us -> 73.1 us
  starting transfers between devices: 0.5 us -> 78.6 us
  matrix products: 56.6 us -> 0 us
  Pallas kernels: 0 us -> 53.8 us
  between operations: 14.1 us -> 0.87 us
  local copies, waits for them, and re-layouts: 8.72 us -> 17.3 us
    reduce_scatter x4 -> x0, waiting for transfers between devices: 208 us -> none  [the longest x2 129 us: scatter_features(): lax.psum_scatter(term(jnp.int32(0), lax.axis_size('col') * count), 'col',...]
    all_gather x4 -> x0, waiting for transfers between devices: 140 us -> none  [the longest x2 91.4 us: gather_tokens(): return lax.all_gather(block, 'col', axis=0, tiled=True)]
    ppermute x0 -> x45, starting transfers between devices: none -> 78.6 us  [send(): return lax.ppermute(block, AXES, permutation(**where))]
    ppermute x0 -> x45, waiting for transfers between devices: none -> 73.1 us  [send(): return lax.ppermute(block, AXES, permutation(**where))]
    dot_general x6 -> x0, matrix products: 56.6 us -> none  [the longest x2 19.5 us: times_transposed(): lax.dot_general(left, right, (((1,), (1,)), ((), ())), preferred_element_...]
    pallas_call x0 -> x6, Pallas kernels: none -> 53.8 us  [the longest x2 22.4 us: project_down(): pl.pallas_call(functools.partial(down_kernel, transposed), grid=(2 * half...]
    unnamed x5 -> x38, local copies, waits for them, and re-layouts: 8.72 us -> 17.2 us
    convert_element_type x3, other arithmetic: 6.19 us -> 1.12 us  [the longest x1 0.92 us: local(): gelu_backward(hidden, grad_activated).astype(BF16)]
  transfers between devices with their start and end apart: 8 -> 45, of which waited for: 8 -> 18; matrix products, arithmetic and copies ran while one was open for 15% -> 2% of each run, Pallas kernels for 0% -> 20%
where the time goes in v1:
time: 231 us; the launch traced here: 230 us
  starting transfers between devices  78.6 us (34%)
  waiting for transfers between devices  73.1 us (32%)
  Pallas kernels  53.8 us (23%)
  local copies, waits for them, and re-layouts  17.3 us (7%)
  other arithmetic  6.33 us (3%)
    ppermute x45, starting transfers between devices, send(): return lax.ppermute(block, AXES, permutation(**where))  78.6 us
    ppermute x45, waiting for transfers between devices, send(): return lax.ppermute(block, AXES, permutation(**where))  73.1 us
    pallas_call x2, Pallas kernels, project_down(): pl.pallas_call(functools.partial(down_kernel, transposed), grid=(2 * half...  22.4 us
    unnamed x38, local copies, waits for them, and re-layouts  17.2 us
    pallas_call x2, Pallas kernels, project_up(): pl.pallas_call(functools.partial(up_kernel, transposed), grid=(columns //...  17 us
    pallas_call x2, Pallas kernels, weight_grad(): pl.pallas_call(weight_kernel, grid=(rows // tile,), in_specs=[left, left,...  14.4 us
  transfers between devices with their start and end apart: 45, of which 18 were waited for; matrix products, arithmetic and copies ran while one was open for 2% of the time, Pallas kernels for 20%

profile of v1, /device:TPU:1, one launch (start us, length us, event | category | flops | bytes accessed | tf_op | source)
XLA Modules:
  0.0 230.0 jit_solution(4551729648457924869)
XLA Ops:
  0.6 1.5 collective-permute-start.7
  2.2 1.1 fusion.10
  3.8 6.4 %collective-permute-done = bf16[2,32,1536]{2,1,0:T(8,128)(2,1)S(1)} collective-permute-done((bf16[2,32,1536]{2,1,0:T(8,128)(2,1)S(1)}, bf16[2,32,1536]{2,1,0:T(8,128)(2,1)S(1)}, u32[]{:S(2)}, u32[]{:S(2)}) %collective-permute-start) | collective-permute-done | bytes 196640 | tf_op jit(solution)/shard_map/ppermute | solution.py:40
  10.3 1.4 collective-permute-start.3
  11.7 2.6 %collective-permute-start.2 = (bf16[32,3072]{1,0:T(8,128)(2,1)S(1)}, bf16[32,3072]{1,0:T(8,128)(2,1)S(1)}, u32[]{:S(2)}, u32[]{:S(2)}) collective-permute-start(bf16[32,3072]{1,0:T(8,128)(2,1)S(1)} %get-tuple-element.57), channel_id=1, source_target_pairs={{0,8},{1,9},{2,10},{3,11},{4,12},{5,13},{6,14},{7,15},{8,0},{9,1},... | collective-permute-start | bytes 589832 | tf_op jit(solution)/shard_map/ppermute | solution.py:40
  14.3 1.1 collective-permute-start.1
  15.4 1.1 collective-permute-done.3
  16.5 3.3 %collective-permute-done.2 = bf16[32,3072]{1,0:T(8,128)(2,1)S(1)} collective-permute-done((bf16[32,3072]{1,0:T(8,128)(2,1)S(1)}, bf16[32,3072]{1,0:T(8,128)(2,1)S(1)}, u32[]{:S(2)}, u32[]{:S(2)}) %collective-permute-start.2) | collective-permute-done | bytes 196640 | tf_op jit(solution)/shard_map/ppermute | solution.py:40
  20.4 1.3 collective-permute-start.22
  23.1 3.0 %collective-permute-done.23 = bf16[32,3072]{1,0:T(8,128)(2,1)S(1)} collective-permute-done((bf16[32,3072]{1,0:T(8,128)(2,1)S(1)}, bf16[32,3072]{1,0:T(8,128)(2,1)S(1)}, u32[]{:S(2)}, u32[]{:S(2)}) %collective-permute-start.23) | collective-permute-done | bytes 196640 | tf_op jit(solution)/shard_map/ppermute | solution.py:40
  26.1 2.2 collective-permute-start.5
  28.3 0.9 collective-permute-start.4
  29.2 6.8 %collective-permute-done.6.p3 = bf16[128,3072]{1,0:T(8,128)(2,1)S(1)} collective-permute-done((bf16[128,3072]{1,0:T(8,128)(2,1)S(1)}, bf16[128,3072]{1,0:T(8,128)(2,1)S(1)}, u32[]{:S(2)}, u32[]{:S(2)}) %collective-permute-start.6) | collective-permute-done | bytes 786464 | tf_op jit(solution)/shard_map/ppermute | solution.py:40
  36.0 1.0 copy-done.7
  36.9 7.5 %collective-permute-done.5.p2 = bf16[128,3072]{1,0:T(8,128)(2,1)S(1)} collective-permute-done((bf16[128,3072]{1,0:T(8,128)(2,1)S(1)}, bf16[128,3072]{1,0:T(8,128)(2,1)S(1)}, u32[]{:S(2)}, u32[]{:S(2)}) %collective-permute-start.5) | collective-permute-done | bytes 786464 | tf_op jit(solution)/shard_map/ppermute | solution.py:40
  44.4 0.9 copy-done.9
  45.3 1.1 collective-permute-start.26
  46.8 0.9 copy-done.11
  47.7 2.3 %collective-permute-start.25 = (bf16[128,3072]{1,0:T(8,128)(2,1)S(1)}, bf16[128,3072]{1,0:T(8,128)(2,1)}, u32[]{:S(2)}, u32[]{:S(2)}) collective-permute-start(bf16[128,3072]{1,0:T(8,128)(2,1)S(1)} %pad_maximum_fusion.1.p0), channel_id=1, source_target_pairs={{0,3},{1,0},{2,1},{3,2},{4,7},{5,4},{6,5},{7,6},{8,11},{9,8},{10,9... | collective-permute-start | bytes 2359304 | tf_op jit(solution)/shard_map/ppermute | solution.py:40
  50.1 2.3 %copy-done.2 = bf16[1536,1536]{1,0:T(8,128)(2,1)S(1)} copy-done((bf16[1536,1536]{1,0:T(8,128)(2,1)S(1)}, bf16[1536,1536]{1,0:T(8,128)(2,1)}, u32[]{:S(2)}) %copy-start.2) | copy-done | bytes 4718616
  52.4 1.1 copy-done.8
  53.5 1.1 copy-done.10
  54.7 1.1 copy-done.12
  55.8 8.1 %shard_map.75 = (bf16[128,1536]{1,0:T(8,128)(2,1)S(1)}, bf16[128,1536]{1,0:T(8,128)(2,1)S(1)}, bf16[128,1536]{1,0:T(8,128)(2,1)S(1)}, bf16[128,1536]{1,0:T(8,128...) custom-call(s32[1]{0:T(128)} %bitcast.place, bf16[128,3072]{1,0:T(8,128)(2,1)S(1)} %pad_maximum_fusion.p0, ...), custom_call_target="tpu_custom_call" | custom-call | flops 4831838208 | bytes 15728640 | tf_op jit(solution)/shard_map/pallas_call | solution.py:95
  63.9 1.1 copy-done.15
  65.1 1.6 collective-permute-start.8
  66.7 3.3 %collective-permute-start.9 = (bf16[128,1536]{1,0:T(8,128)(2,1)S(1)}, bf16[128,1536]{1,0:T(8,128)(2,1)S(1)}, u32[]{:S(2)}, u32[]{:S(2)}) collective-permute-start(bf16[128,1536]{1,0:T(8,128)(2,1)S(1)} %get-tuple-element.28), channel_id=1, source_target_pairs={{0,64},{1,65},{2,66},{3,67},{4,68},{5,69},{6,70},{7,71},{8,72},{9,... | collective-permute-start | bytes 1179656 | tf_op jit(solution)/shard_map/ppermute | solution.py:40
  70.8 2.3 %copy-done = bf16[1536,1536]{1,0:T(8,128)(2,1)S(1)} copy-done((bf16[1536,1536]{1,0:T(8,128)(2,1)S(1)}, bf16[1536,1536]{1,0:T(8,128)(2,1)}, u32[]{:S(2)}) %copy-start) | copy-done | bytes 4718616
  73.1 8.9 %shard_map.77 = (bf16[128,1536]{1,0:T(8,128)(2,1)S(1)}, bf16[128,1536]{1,0:T(8,128)(2,1)S(1)}, bf16[128,1536]{1,0:T(8,128)(2,1)S(1)}, bf16[128,1536]{1,0:T(8,128...) custom-call(s32[1]{0:T(128)} %bitcast.place, bf16[128,3072]{1,0:T(8,128)(2,1)S(1)} %pad_maximum_fusion.1.p0, ...), custom_call_target="tpu_custom_call" | custom-call | flops 4831838208 | bytes 15728640 | tf_op jit(solution)/shard_map/pallas_call | solution.py:95
  82.0 0.8 collective-permute-start.28
  83.3 2.0 collective-permute-start.30
  85.4 7.4 %collective-permute-done.28 = bf16[128,1536]{1,0:T(8,128)(2,1)S(1)} collective-permute-done((bf16[128,1536]{1,0:T(8,128)(2,1)S(1)}, bf16[128,1536]{1,0:T(8,128)(2,1)S(1)}, u32[]{:S(2)}, u32[]{:S(2)}) %collective-permute-start.28) | collective-permute-done | bytes 393248 | tf_op jit(solution)/shard_map/ppermute | solution.py:40
  92.7 8.8 %collective-permute-done.29 = bf16[128,1536]{1,0:T(8,128)(2,1)S(1)} collective-permute-done((bf16[128,1536]{1,0:T(8,128)(2,1)S(1)}, bf16[128,1536]{1,0:T(8,128)(2,1)S(1)}, u32[]{:S(2)}, u32[]{:S(2)}) %collective-permute-start.29) | collective-permute-done | bytes 393248 | tf_op jit(solution)/shard_map/ppermute | solution.py:40
  101.5 0.9 fusion.6
  102.5 2.6 %collective-permute-start.13 = (bf16[128,1536]{1,0:T(8,128)(2,1)S(1)}, bf16[128,1536]{1,0:T(8,128)(2,1)S(1)}, u32[]{:S(2)}, u32[]{:S(2)}) collective-permute-start(bf16[128,1536]{1,0:T(8,128)(2,1)S(1)} %get-tuple-element.49.p0), channel_id=1, source_target_pairs={{0,32},{1,33},{2,34},{3,35},{4,36},{5,37},{6,38},{7,39},{8,40},{9,... | collective-permute-start | bytes 1179656 | tf_op jit(solution)/shard_map/ppermute | solution.py:40
  105.0 1.5 collective-permute-start.12
  106.5 1.0 collective-permute-start.11
  108.0 1.5 collective-permute-start.32
  109.5 1.8 collective-permute-done.13.p3
  111.2 1.9 collective-permute-start.31
  113.2 8.2 %collective-permute-done.12.p2 = bf16[128,1536]{1,0:T(8,128)(2,1)S(1)} collective-permute-done((bf16[128,1536]{1,0:T(8,128)(2,1)S(1)}, bf16[128,1536]{1,0:T(8,128)(2,1)S(1)}, u32[]{:S(2)}, u32[]{:S(2)}) %collective-permute-start.12) | collective-permute-done | bytes 393248 | tf_op jit(solution)/shard_map/ppermute | solution.py:40
  121.3 3.7 %collective-permute-done.11.p1 = bf16[128,1536]{1,0:T(8,128)(2,1)S(1)} collective-permute-done((bf16[128,1536]{1,0:T(8,128)(2,1)S(1)}, bf16[128,1536]{1,0:T(8,128)(2,1)S(1)}, u32[]{:S(2)}, u32[]{:S(2)}) %collective-permute-start.11) | collective-permute-done | bytes 393248 | tf_op jit(solution)/shard_map/ppermute | solution.py:40
  125.1 11.4 %shard_map.76 = (bf16[128,3072]{1,0:T(8,128)(2,1)S(1)}, bf16[128,3072]{1,0:T(8,128)(2,1)}, bf16[128,3072]{1,0:T(8,128)(2,1)}, bf16[128,3072]{1,0:T(8,128)(2,1)S(1)}, bf16[512,1536]{1,0:T(8,128)(2,1)S(1)}) custom-call(s32[1]{0:T(128)} %bitcast.place, bf16[128,1536]{1,0:T(8,128)(2,1)S(1)} %get-tuple-element.49.p0, ...), custom_call_target="tpu_custom_call" | custom-call | flops 4831838208 | bytes 15728640 | tf_op jit(solution)/shard_map/pallas_call | solution.py:147
  136.5 1.1 copy-done.5
  137.6 3.6 %collective-permute-start.16 = (bf16[128,3072]{1,0:T(8,128)(2,1)}, bf16[128,3072]{1,0:T(8,128)(2,1)}, u32[]{:S(2)}, u32[]{:S(2)}) collective-permute-start(bf16[128,3072]{1,0:T(8,128)(2,1)} %get-tuple-element.32), channel_id=1, source_target_pairs={{0,2},{1,3},{2,0},{3,1},{4,6},{5,7},{6,4},{7,5},{8,10},{9,11},{10,... | collective-permute-start | bytes 2359304 | tf_op jit(solution)/shard_map/ppermute | solution.py:40
  142.0 5.0 %collective-permute-start.41 = (bf16[512,1536]{1,0:T(8,128)(2,1)S(1)}, bf16[512,1536]{1,0:T(8,128)(2,1)S(1)}, u32[]{:S(2)}, u32[]{:S(2)}) collective-permute-start(bf16[512,1536]{1,0:T(8,128)(2,1)S(1)} %get-tuple-element.43), channel_id=1, source_target_pairs={{0,16},{1,17},{2,18},{3,19},{4,20},{5,21},{6,22},{7,23},{8,24},{9,... | collective-permute-start | bytes 4718600 | tf_op jit(solution)/shard_map/ppermute | solution.py:40
  147.1 2.3 %copy-done.3 = bf16[1536,1536]{1,0:T(8,128)(2,1)S(1)} copy-done((bf16[1536,1536]{1,0:T(8,128)(2,1)S(1)}, bf16[1536,1536]{1,0:T(8,128)(2,1)}, u32[]{:S(2)}) %copy-start.3) | copy-done | bytes 4718616
  149.4 1.0 copy-done.14
  150.4 11.0 %shard_map.78 = (bf16[128,3072]{1,0:T(8,128)(2,1)S(1)}, bf16[128,3072]{1,0:T(8,128)(2,1)S(1)}, bf16[128,3072]{1,0:T(8,128)(2,1)S(1)}, bf16[128,3072]{1,0:T(8,128)(2,1)S(1)}, bf16[512,1536]{1,0:T(8,128)(2,1)S(1)}) custom-call(s32[1]{0:T(128)} %bitcast.place, bf16[128,1536]{1,0:T(8,128)(2,1)S(1)} %get-tuple-element.48.p0, ...), custom_call_target="tpu_custom_call" | custom-call | flops 4831838208 | bytes 15728640 | tf_op jit(solution)/shard_map/pallas_call | solution.py:147
  161.4 7.1 %collective-permute-start.34 = (bf16[128,3072]{1,0:T(8,128)(2,1)S(1)}, bf16[128,3072]{1,0:T(8,128)(2,1)S(1)}, u32[]{:S(2)}, u32[]{:S(2)}) collective-permute-start(bf16[128,3072]{1,0:T(8,128)(2,1)S(1)} %get-tuple-element.39), channel_id=1, source_target_pairs={{0,1},{1,2},{2,3},{3,0},{4,5},{5,6},{6,7},{7,4},{8,9},{9,10},{10,1... | collective-permute-start | bytes 2359304 | tf_op jit(solution)/shard_map/ppermute | solution.py:40
  168.5 2.5 %collective-permute-start.36 = (bf16[128,3072]{1,0:T(8,128)(2,1)S(1)}, bf16[128,3072]{1,0:T(8,128)(2,1)S(1)}, u32[]{:S(2)}, u32[]{:S(2)}) collective-permute-start(bf16[128,3072]{1,0:T(8,128)(2,1)S(1)} %get-tuple-element.41), channel_id=1, source_target_pairs={{0,3},{1,0},{2,1},{3,2},{4,7},{5,4},{6,5},{7,6},{8,11},{9,8},{10,9... | collective-permute-start | bytes 2359304 | tf_op jit(solution)/shard_map/ppermute | solution.py:40
  171.0 2.1 add_convert_fusion.1
  173.1 9.1 %collective-permute-done.34 = bf16[128,3072]{1,0:T(8,128)(2,1)S(1)} collective-permute-done((bf16[128,3072]{1,0:T(8,128)(2,1)S(1)}, bf16[128,3072]{1,0:T(8,128)(2,1)S(1)}, u32[]{:S(2)}, u32[]{:S(2)}) %collective-permute-start.34) | collective-permute-done | bytes 786464 | tf_op jit(solution)/shard_map/ppermute | solution.py:40
  182.3 3.6 %collective-permute-done.35 = bf16[128,3072]{1,0:T(8,128)(2,1)S(1)} collective-permute-done((bf16[128,3072]{1,0:T(8,128)(2,1)S(1)}, bf16[128,3072]{1,0:T(8,128)(2,1)S(1)}, u32[]{:S(2)}, u32[]{:S(2)}) %collective-permute-start.35) | collective-permute-done | bytes 786464 | tf_op jit(solution)/shard_map/ppermute | solution.py:40
  186.4 4.2 %collective-permute-start.19 = (bf16[32,3072]{1,0:T(8,128)(2,1)S(1)}, bf16[32,3072]{1,0:T(8,128)(2,1)S(1)}, u32[]{:S(2)}, u32[]{:S(2)}) collective-permute-start(bf16[32,3072]{1,0:T(8,128)(2,1)S(1)} %get-tuple-element.55), channel_id=1, source_target_pairs={{0,8},{1,9},{2,10},{3,11},{4,12},{5,13},{6,14},{7,15},{8,0},{9,1},... | collective-permute-start | bytes 589832 | tf_op jit(solution)/shard_map/ppermute | solution.py:40
  191.2 0.9 collective-permute-start.37
  192.1 1.8 collective-permute-start.39
  193.9 2.8 %collective-permute-start.38 = (bf16[32,3072]{1,0:T(8,128)(2,1)S(1)}, bf16[32,3072]{1,0:T(8,128)(2,1)S(1)}, u32[]{:S(2)}, u32[]{:S(2)}) collective-permute-start(bf16[32,3072]{1,0:T(8,128)(2,1)S(1)} %get-tuple-element.52), channel_id=1, source_target_pairs={{0,8},{1,9},{2,10},{3,11},{4,12},{5,13},{6,14},{7,15},{8,0},{9,1},... | collective-permute-start | bytes 589832 | tf_op jit(solution)/shard_map/ppermute | solution.py:40
  197.0 11.1 %collective-permute-start.43 = (bf16[512,1536]{1,0:T(8,128)(2,1)S(1)}, bf16[512,1536]{1,0:T(8,128)(2,1)S(1)}, u32[]{:S(2)}, u32[]{:S(2)}) collective-permute-start(bf16[512,1536]{1,0:T(8,128)(2,1)S(1)} %copy-done.6), channel_id=1, source_target_pairs={{0,16},{1,17},{2,18},{3,19},{4,20},{5,21},{6,22},{7,23},{8,24},{9,... | collective-permute-start | bytes 4718600 | tf_op jit(solution)/shard_map/ppermute | solution.py:40
  208.1 1.3 collective-permute-start.42
  209.4 3.1 %collective-permute-start.21 = (bf16[32,1536]{1,0:T(8,128)(2,1)S(1)}, bf16[32,1536]{1,0:T(8,128)(2,1)S(1)}, u32[]{:S(2)}, u32[]{:S(2)}) collective-permute-start(bf16[32,1536]{1,0:T(8,128)(2,1)S(1)} %get-tuple-element.63), channel_id=1, source_target_pairs={{0,16},{1,17},{2,18},{3,19},{4,20},{5,21},{6,22},{7,23},{8,24},{9,... | collective-permute-start | bytes 294920 | tf_op jit(solution)/shard_map/ppermute | solution.py:40
  212.6 0.9 collective-permute-done.21
  215.6 7.2 %shard_map.79 = bf16[1536,1536]{1,0:T(8,128)(2,1)} custom-call(bf16[512,1536]{1,0:T(8,128)(2,1)S(1)} %copy-done.16, bf16[512,1536]{1,0:T(8,128)(2,1)S(1)} %collective-permute-done.41.l_other, bf16[512,1536]{1,0:T(8,128)(2,1)S(1)} %get-tuple-element.44.r_own, bf16[512,1536]{1,0:T(8,128)(2,1)S(1)} %collective-permute-done.42.r_other), custom_call_target="tpu_custom_call" | custom-call | flops 4831838208 | bytes 11010048 | tf_op jit(solution)/shard_map/pallas_call | solution.py:176
  222.8 7.2 %shard_map.80 = bf16[1536,1536]{1,0:T(8,128)(2,1)} custom-call(bf16[512,1536]{1,0:T(8,128)(2,1)S(1)} %copy-done.6, bf16[512,1536]{1,0:T(8,128)(2,1)S(1)} %collective-permute-done.43.l_other, bf16[512,1536]{1,0:T(8,128)(2,1)S(1)} %copy-done.18, bf16[512,1536]{1,0:T(8,128)(2,1)S(1)} %collective-permute-done.44.r_other), custom_call_target="tpu_custom_call" | custom-call | flops 4831838208 | bytes 11010048 | tf_op jit(solution)/shard_map/pallas_call | solution.py:176
  (85 shorter events, 9.3 us)
Async XLA Ops:
  0.6 49.4 %collective-permute-start.7 = (bf16[1536,1536]{1,0:T(8,128)(2,1)}, bf16[1536,1536]{1,0:T(8,128)(2,1)}, u32[]{:S(2)}, u32[]{:S(2)}) collective-permute-start(bf16[1536,1536]{1,0:T(8,128)(2,1)} %w_own.7), channel_id=1, source_target_pairs={{0,16},{1,17},{2,18},{3,19},{4,20},{5,21},{6,22},{7,23},{8,24},{9,... | collective-permute-start | bytes 14155784 | tf_op jit(solution)/shard_map/ppermute | solution.py:40
  2.1 68.6 %collective-permute-start.14 = (bf16[1536,1536]{1,0:T(8,128)(2,1)}, bf16[1536,1536]{1,0:T(8,128)(2,1)}, u32[]{:S(2)}, u32[]{:S(2)}) collective-permute-start(bf16[1536,1536]{1,0:T(8,128)(2,1)} %w_own.6), channel_id=1, source_target_pairs={{0,16},{1,17},{2,18},{3,19},{4,20},{5,21},{6,22},{7,23},{8,24},{9,... | collective-permute-start | bytes 14155784 | tf_op jit(solution)/shard_map/ppermute | solution.py:40
  3.3 6.9 %collective-permute-start = (bf16[2,32,1536]{2,1,0:T(8,128)(2,1)S(1)}, bf16[2,32,1536]{2,1,0:T(8,128)(2,1)S(1)}, u32[]{:S(2)}, u32[]{:S(2)}) collective-permute-start(bf16[2,32,1536]{2,1,0:T(8,128)(2,1)S(1)} %get-tuple-element.58), channel_id=1, source_target_pairs={{0,16},{1,17},{2,18},{3,19},{4,20},{5,21},{6,22},{7,23},{8,24},{9,... | collective-permute-start | bytes 589832 | tf_op jit(solution)/shard_map/ppermute | solution.py:40
  10.3 6.2 %collective-permute-start.3 = (bf16[32,3072]{1,0:T(8,128)(2,1)S(1)}, bf16[32,3072]{1,0:T(8,128)(2,1)S(1)}, u32[]{:S(2)}, u32[]{:S(2)}) collective-permute-start(bf16[32,3072]{1,0:T(8,128)(2,1)S(1)} %get-tuple-element.57), channel_id=1, source_target_pairs={{0,4},{1,5},{2,6},{3,7},{4,8},{5,9},{6,10},{7,11},{8,12},{9,13},{1... | collective-permute-start | bytes 589832 | tf_op jit(solution)/shard_map/ppermute | solution.py:40
  11.7 8.1 %collective-permute-start.2 = (bf16[32,3072]{1,0:T(8,128)(2,1)S(1)}, bf16[32,3072]{1,0:T(8,128)(2,1)S(1)}, u32[]{:S(2)}, u32[]{:S(2)}) collective-permute-start(bf16[32,3072]{1,0:T(8,128)(2,1)S(1)} %get-tuple-element.57), channel_id=1, source_target_pairs={{0,8},{1,9},{2,10},{3,11},{4,12},{5,13},{6,14},{7,15},{8,0},{9,1},... | collective-permute-start | bytes 589832 | tf_op jit(solution)/shard_map/ppermute | solution.py:40
  14.3 6.0 %collective-permute-start.1 = (bf16[32,3072]{1,0:T(8,128)(2,1)S(1)}, bf16[32,3072]{1,0:T(8,128)(2,1)S(1)}, u32[]{:S(2)}, u32[]{:S(2)}) collective-permute-start(bf16[32,3072]{1,0:T(8,128)(2,1)S(1)} %get-tuple-element.57), channel_id=1, source_target_pairs={{0,12},{1,13},{2,14},{3,15},{4,0},{5,1},{6,2},{7,3},{8,4},{9,5},{1... | collective-permute-start | bytes 589832 | tf_op jit(solution)/shard_map/ppermute | solution.py:40
  16.5 6.0 %collective-permute-start.24 = (bf16[32,3072]{1,0:T(8,128)(2,1)S(1)}, bf16[32,3072]{1,0:T(8,128)(2,1)S(1)}, u32[]{:S(2)}, u32[]{:S(2)}) collective-permute-start(bf16[32,3072]{1,0:T(8,128)(2,1)S(1)} %get-tuple-element.56), channel_id=1, source_target_pairs={{0,4},{1,5},{2,6},{3,7},{4,8},{5,9},{6,10},{7,11},{8,12},{9,13},{1... | collective-permute-start | bytes 589832 | tf_op jit(solution)/shard_map/ppermute | solution.py:40
  19.8 6.3 %collective-permute-start.23 = (bf16[32,3072]{1,0:T(8,128)(2,1)S(1)}, bf16[32,3072]{1,0:T(8,128)(2,1)S(1)}, u32[]{:S(2)}, u32[]{:S(2)}) collective-permute-start(bf16[32,3072]{1,0:T(8,128)(2,1)S(1)} %get-tuple-element.56), channel_id=1, source_target_pairs={{0,8},{1,9},{2,10},{3,11},{4,12},{5,13},{6,14},{7,15},{8,0},{9,1},... | collective-permute-start | bytes 589832 | tf_op jit(solution)/shard_map/ppermute | solution.py:40
  20.4 7.9 %collective-permute-start.22 = (bf16[32,3072]{1,0:T(8,128)(2,1)S(1)}, bf16[32,3072]{1,0:T(8,128)(2,1)S(1)}, u32[]{:S(2)}, u32[]{:S(2)}) collective-permute-start(bf16[32,3072]{1,0:T(8,128)(2,1)S(1)} %get-tuple-element.56), channel_id=1, source_target_pairs={{0,12},{1,13},{2,14},{3,15},{4,0},{5,1},{6,2},{7,3},{8,4},{9,5},{1... | collective-permute-start | bytes 589832 | tf_op jit(solution)/shard_map/ppermute | solution.py:40
  22.5 13.4 %collective-permute-start.6 = (bf16[128,3072]{1,0:T(8,128)(2,1)S(1)}, bf16[128,3072]{1,0:T(8,128)(2,1)S(1)}, u32[]{:S(2)}, u32[]{:S(2)}) collective-permute-start(bf16[128,3072]{1,0:T(8,128)(2,1)S(1)} %pad_maximum_fusion.p0), channel_id=1, source_target_pairs={{0,1},{1,2},{2,3},{3,0},{4,5},{5,6},{6,7},{7,4},{8,9},{9,10},{10,1... | collective-permute-start | bytes 2359304 | tf_op jit(solution)/shard_map/ppermute | solution.py:40
  26.1 18.3 %collective-permute-start.5 = (bf16[128,3072]{1,0:T(8,128)(2,1)S(1)}, bf16[128,3072]{1,0:T(8,128)(2,1)S(1)}, u32[]{:S(2)}, u32[]{:S(2)}) collective-permute-start(bf16[128,3072]{1,0:T(8,128)(2,1)S(1)} %pad_maximum_fusion.p0), channel_id=1, source_target_pairs={{0,2},{1,3},{2,0},{3,1},{4,6},{5,7},{6,4},{7,5},{8,10},{9,11},{10,... | collective-permute-start | bytes 2359304 | tf_op jit(solution)/shard_map/ppermute | solution.py:40
  28.3 18.6 %collective-permute-start.4 = (bf16[128,3072]{1,0:T(8,128)(2,1)S(1)}, bf16[128,3072]{1,0:T(8,128)(2,1)S(1)}, u32[]{:S(2)}, u32[]{:S(2)}) collective-permute-start(bf16[128,3072]{1,0:T(8,128)(2,1)S(1)} %pad_maximum_fusion.p0), channel_id=1, source_target_pairs={{0,3},{1,0},{2,1},{3,2},{4,7},{5,4},{6,5},{7,6},{8,11},{9,8},{10,9... | collective-permute-start | bytes 2359304 | tf_op jit(solution)/shard_map/ppermute | solution.py:40
  36.0 1.0 copy-start.7
  36.9 29.8 %collective-permute-start.27 = (bf16[128,3072]{1,0:T(8,128)(2,1)S(1)}, bf16[128,3072]{1,0:T(8,128)(2,1)}, u32[]{:S(2)}, u32[]{:S(2)}) collective-permute-start(bf16[128,3072]{1,0:T(8,128)(2,1)S(1)} %pad_maximum_fusion.1.p0), channel_id=1, source_target_pairs={{0,1},{1,2},{2,3},{3,0},{4,5},{5,6},{6,7},{7,4},{8,9},{9,10},{10,1... | collective-permute-start | bytes 2359304 | tf_op jit(solution)/shard_map/ppermute | solution.py:40
  44.4 0.9 copy-start.9
  45.3 24.7 %collective-permute-start.26 = (bf16[128,3072]{1,0:T(8,128)(2,1)S(1)}, bf16[128,3072]{1,0:T(8,128)(2,1)}, u32[]{:S(2)}, u32[]{:S(2)}) collective-permute-start(bf16[128,3072]{1,0:T(8,128)(2,1)S(1)} %pad_maximum_fusion.1.p0), channel_id=1, source_target_pairs={{0,2},{1,3},{2,0},{3,1},{4,6},{5,7},{6,4},{7,5},{8,10},{9,11},{10,... | collective-permute-start | bytes 2359304 | tf_op jit(solution)/shard_map/ppermute | solution.py:40
  46.8 0.9 copy-start.11
  47.7 23.1 %collective-permute-start.25 = (bf16[128,3072]{1,0:T(8,128)(2,1)S(1)}, bf16[128,3072]{1,0:T(8,128)(2,1)}, u32[]{:S(2)}, u32[]{:S(2)}) collective-permute-start(bf16[128,3072]{1,0:T(8,128)(2,1)S(1)} %pad_maximum_fusion.1.p0), channel_id=1, source_target_pairs={{0,3},{1,0},{2,1},{3,2},{4,7},{5,4},{6,5},{7,6},{8,11},{9,8},{10,9... | collective-permute-start | bytes 2359304 | tf_op jit(solution)/shard_map/ppermute | solution.py:40
  50.0 2.3 %copy-start.2 = (bf16[1536,1536]{1,0:T(8,128)(2,1)S(1)}, bf16[1536,1536]{1,0:T(8,128)(2,1)}, u32[]{:S(2)}) copy-start(bf16[1536,1536]{1,0:T(8,128)(2,1)} %w_own.7) | copy-start | bytes 14155780
  52.4 1.1 copy-start.8
  53.5 1.1 copy-start.10
  54.7 1.1 copy-start.12
  63.9 1.1 copy-start.15
  65.1 18.2 %collective-permute-start.8 = (bf16[128,1536]{1,0:T(8,128)(2,1)S(1)}, bf16[128,1536]{1,0:T(8,128)(2,1)S(1)}, u32[]{:S(2)}, u32[]{:S(2)}) collective-permute-start(bf16[128,1536]{1,0:T(8,128)(2,1)S(1)} %get-tuple-element.27), channel_id=1, source_target_pairs={{0,32},{1,33},{2,34},{3,35},{4,36},{5,37},{6,38},{7,39},{8,40},{9,... | collective-permute-start | bytes 1179656 | tf_op jit(solution)/shard_map/ppermute | solution.py:40
  66.7 18.6 %collective-permute-start.9 = (bf16[128,1536]{1,0:T(8,128)(2,1)S(1)}, bf16[128,1536]{1,0:T(8,128)(2,1)S(1)}, u32[]{:S(2)}, u32[]{:S(2)}) collective-permute-start(bf16[128,1536]{1,0:T(8,128)(2,1)S(1)} %get-tuple-element.28), channel_id=1, source_target_pairs={{0,64},{1,65},{2,66},{3,67},{4,68},{5,69},{6,70},{7,71},{8,72},{9,... | collective-permute-start | bytes 1179656 | tf_op jit(solution)/shard_map/ppermute | solution.py:40
  70.0 15.3 %collective-permute-start.10 = (bf16[128,1536]{1,0:T(8,128)(2,1)S(1)}, bf16[128,1536]{1,0:T(8,128)(2,1)S(1)}, u32[]{:S(2)}, u32[]{:S(2)}) collective-permute-start(bf16[128,1536]{1,0:T(8,128)(2,1)S(1)} %get-tuple-element.29), channel_id=1, source_target_pairs={{0,96},{1,97},{2,98},{3,99},{4,100},{5,101},{6,102},{7,103},{8,104... | collective-permute-start | bytes 1179656 | tf_op jit(solution)/shard_map/ppermute | solution.py:40
  70.8 2.3 %copy-start = (bf16[1536,1536]{1,0:T(8,128)(2,1)S(1)}, bf16[1536,1536]{1,0:T(8,128)(2,1)}, u32[]{:S(2)}) copy-start(bf16[1536,1536]{1,0:T(8,128)(2,1)} %w_own.6) | copy-start | bytes 14155780
  73.1 52.0 %copy-start.1 = (bf16[1536,1536]{1,0:T(8,128)(2,1)S(1)}, bf16[1536,1536]{1,0:T(8,128)(2,1)}, u32[]{:S(2)}) copy-start(bf16[1536,1536]{1,0:T(8,128)(2,1)} %w_own.6) | copy-start | bytes 14155780
  82.0 20.4 %copy-start.4 = (bf16[512,1536]{1,0:T(8,128)(2,1)}, bf16[512,1536]{1,0:T(8,128)(2,1)S(1)}, u32[]{:S(2)}) copy-start(bf16[512,1536]{1,0:T(8,128)(2,1)S(1)} %get-tuple-element.47) | copy-start | bytes 4718596
  82.0 20.4 %copy-start.17 = (bf16[512,1536]{1,0:T(8,128)(2,1)}, bf16[512,1536]{1,0:T(8,128)(2,1)S(1)}, u32[]{:S(2)}) copy-start(bf16[512,1536]{1,0:T(8,128)(2,1)S(1)} %get-tuple-element.46.r_own) | copy-start | bytes 4718596
  82.0 10.7 %collective-permute-start.28 = (bf16[128,1536]{1,0:T(8,128)(2,1)S(1)}, bf16[128,1536]{1,0:T(8,128)(2,1)S(1)}, u32[]{:S(2)}, u32[]{:S(2)}) collective-permute-start(bf16[128,1536]{1,0:T(8,128)(2,1)S(1)} %get-tuple-element.35), channel_id=1, source_target_pairs={{0,32},{1,33},{2,34},{3,35},{4,36},{5,37},{6,38},{7,39},{8,40},{9,... | collective-permute-start | bytes 1179656 | tf_op jit(solution)/shard_map/ppermute | solution.py:40
  82.9 18.6 %collective-permute-start.29 = (bf16[128,1536]{1,0:T(8,128)(2,1)S(1)}, bf16[128,1536]{1,0:T(8,128)(2,1)S(1)}, u32[]{:S(2)}, u32[]{:S(2)}) collective-permute-start(bf16[128,1536]{1,0:T(8,128)(2,1)S(1)} %get-tuple-element.36), channel_id=1, source_target_pairs={{0,64},{1,65},{2,66},{3,67},{4,68},{5,69},{6,70},{7,71},{8,72},{9,... | collective-permute-start | bytes 1179656 | tf_op jit(solution)/shard_map/ppermute | solution.py:40
  83.3 18.2 %collective-permute-start.30 = (bf16[128,1536]{1,0:T(8,128)(2,1)S(1)}, bf16[128,1536]{1,0:T(8,128)(2,1)S(1)}, u32[]{:S(2)}, u32[]{:S(2)}) collective-permute-start(bf16[128,1536]{1,0:T(8,128)(2,1)S(1)} %get-tuple-element.37), channel_id=1, source_target_pairs={{0,96},{1,97},{2,98},{3,99},{4,100},{5,101},{6,102},{7,103},{8,104... | collective-permute-start | bytes 1179656 | tf_op jit(solution)/shard_map/ppermute | solution.py:40
  102.5 8.8 %collective-permute-start.13 = (bf16[128,1536]{1,0:T(8,128)(2,1)S(1)}, bf16[128,1536]{1,0:T(8,128)(2,1)S(1)}, u32[]{:S(2)}, u32[]{:S(2)}) collective-permute-start(bf16[128,1536]{1,0:T(8,128)(2,1)S(1)} %get-tuple-element.49.p0), channel_id=1, source_target_pairs={{0,32},{1,33},{2,34},{3,35},{4,36},{5,37},{6,38},{7,39},{8,40},{9,... | collective-permute-start | bytes 1179656 | tf_op jit(solution)/shard_map/ppermute | solution.py:40
  105.0 16.3 %collective-permute-start.12 = (bf16[128,1536]{1,0:T(8,128)(2,1)S(1)}, bf16[128,1536]{1,0:T(8,128)(2,1)S(1)}, u32[]{:S(2)}, u32[]{:S(2)}) collective-permute-start(bf16[128,1536]{1,0:T(8,128)(2,1)S(1)} %get-tuple-element.49.p0), channel_id=1, source_target_pairs={{0,64},{1,65},{2,66},{3,67},{4,68},{5,69},{6,70},{7,71},{8,72},{9,... | collective-permute-start | bytes 1179656 | tf_op jit(solution)/shard_map/ppermute | solution.py:40
  106.5 18.5 %collective-permute-start.11 = (bf16[128,1536]{1,0:T(8,128)(2,1)S(1)}, bf16[128,1536]{1,0:T(8,128)(2,1)S(1)}, u32[]{:S(2)}, u32[]{:S(2)}) collective-permute-start(bf16[128,1536]{1,0:T(8,128)(2,1)S(1)} %get-tuple-element.49.p0), channel_id=1, source_target_pairs={{0,96},{1,97},{2,98},{3,99},{4,100},{5,101},{6,102},{7,103},{8,104... | collective-permute-start | bytes 1179656 | tf_op jit(solution)/shard_map/ppermute | solution.py:40
  107.5 33.7 %collective-permute-start.33 = (bf16[128,1536]{1,0:T(8,128)(2,1)S(1)}, bf16[128,1536]{1,0:T(8,128)(2,1)S(1)}, u32[]{:S(2)}, u32[]{:S(2)}) collective-permute-start(bf16[128,1536]{1,0:T(8,128)(2,1)S(1)} %get-tuple-element.48.p0), channel_id=1, source_target_pairs={{0,32},{1,33},{2,34},{3,35},{4,36},{5,37},{6,38},{7,39},{8,40},{9,... | collective-permute-start | bytes 1179656 | tf_op jit(solution)/shard_map/ppermute | solution.py:40
  108.0 34.0 %collective-permute-start.32 = (bf16[128,1536]{1,0:T(8,128)(2,1)S(1)}, bf16[128,1536]{1,0:T(8,128)(2,1)}, u32[]{:S(2)}, u32[]{:S(2)}) collective-permute-start(bf16[128,1536]{1,0:T(8,128)(2,1)S(1)} %get-tuple-element.48.p0), channel_id=1, source_target_pairs={{0,64},{1,65},{2,66},{3,67},{4,68},{5,69},{6,70},{7,71},{8,72},{9,... | collective-permute-start | bytes 1179656 | tf_op jit(solution)/shard_map/ppermute | solution.py:40
  111.2 35.8 %collective-permute-start.31 = (bf16[128,1536]{1,0:T(8,128)(2,1)S(1)}, bf16[128,1536]{1,0:T(8,128)(2,1)}, u32[]{:S(2)}, u32[]{:S(2)}) collective-permute-start(bf16[128,1536]{1,0:T(8,128)(2,1)S(1)} %get-tuple-element.48.p0), channel_id=1, source_target_pairs={{0,96},{1,97},{2,98},{3,99},{4,100},{5,101},{6,102},{7,103},{8,104... | collective-permute-start | bytes 1179656 | tf_op jit(solution)/shard_map/ppermute | solution.py:40
  136.5 1.1 copy-start.5
  137.6 23.8 %collective-permute-start.15 = (bf16[128,3072]{1,0:T(8,128)(2,1)}, bf16[128,3072]{1,0:T(8,128)(2,1)}, u32[]{:S(2)}, u32[]{:S(2)}) collective-permute-start(bf16[128,3072]{1,0:T(8,128)(2,1)} %get-tuple-element.31), channel_id=1, source_target_pairs={{0,1},{1,2},{2,3},{3,0},{4,5},{5,6},{6,7},{7,4},{8,9},{9,10},{10,1... | collective-permute-start | bytes 2359304 | tf_op jit(solution)/shard_map/ppermute | solution.py:40
  137.6 30.8 %collective-permute-start.16 = (bf16[128,3072]{1,0:T(8,128)(2,1)}, bf16[128,3072]{1,0:T(8,128)(2,1)}, u32[]{:S(2)}, u32[]{:S(2)}) collective-permute-start(bf16[128,3072]{1,0:T(8,128)(2,1)} %get-tuple-element.32), channel_id=1, source_target_pairs={{0,2},{1,3},{2,0},{3,1},{4,6},{5,7},{6,4},{7,5},{8,10},{9,11},{10,... | collective-permute-start | bytes 2359304 | tf_op jit(solution)/shard_map/ppermute | solution.py:40
  141.2 0.8 copy-start.13
  142.0 26.5 %collective-permute-start.17 = (bf16[128,3072]{1,0:T(8,128)(2,1)S(1)}, bf16[128,3072]{1,0:T(8,128)(2,1)}, u32[]{:S(2)}, u32[]{:S(2)}) collective-permute-start(bf16[128,3072]{1,0:T(8,128)(2,1)S(1)} %get-tuple-element.33), channel_id=1, source_target_pairs={{0,3},{1,0},{2,1},{3,2},{4,7},{5,4},{6,5},{7,6},{8,11},{9,8},{10,9... | collective-permute-start | bytes 2359304 | tf_op jit(solution)/shard_map/ppermute | solution.py:40
  142.0 73.6 %collective-permute-start.41 = (bf16[512,1536]{1,0:T(8,128)(2,1)S(1)}, bf16[512,1536]{1,0:T(8,128)(2,1)S(1)}, u32[]{:S(2)}, u32[]{:S(2)}) collective-permute-start(bf16[512,1536]{1,0:T(8,128)(2,1)S(1)} %get-tuple-element.43), channel_id=1, source_target_pairs={{0,16},{1,17},{2,18},{3,19},{4,20},{5,21},{6,22},{7,23},{8,24},{9,... | collective-permute-start | bytes 4718600 | tf_op jit(solution)/shard_map/ppermute | solution.py:40
  147.0 75.8 %collective-permute-start.44 = (bf16[512,1536]{1,0:T(8,128)(2,1)}, bf16[512,1536]{1,0:T(8,128)(2,1)S(1)}, u32[]{:S(2)}, u32[]{:S(2)}) collective-permute-start(bf16[512,1536]{1,0:T(8,128)(2,1)} %copy-done.4), channel_id=1, source_target_pairs={{0,16},{1,17},{2,18},{3,19},{4,20},{5,21},{6,22},{7,23},{8,24},{9,... | collective-permute-start | bytes 4718600 | tf_op jit(solution)/shard_map/ppermute | solution.py:40
  147.1 2.3 %copy-start.3 = (bf16[1536,1536]{1,0:T(8,128)(2,1)S(1)}, bf16[1536,1536]{1,0:T(8,128)(2,1)}, u32[]{:S(2)}) copy-start(bf16[1536,1536]{1,0:T(8,128)(2,1)} %w_own.7) | copy-start | bytes 14155780
  149.4 1.0 copy-start.14
  161.4 20.8 %collective-permute-start.34 = (bf16[128,3072]{1,0:T(8,128)(2,1)S(1)}, bf16[128,3072]{1,0:T(8,128)(2,1)S(1)}, u32[]{:S(2)}, u32[]{:S(2)}) collective-permute-start(bf16[128,3072]{1,0:T(8,128)(2,1)S(1)} %get-tuple-element.39), channel_id=1, source_target_pairs={{0,1},{1,2},{2,3},{3,0},{4,5},{5,6},{6,7},{7,4},{8,9},{9,10},{10,1... | collective-permute-start | bytes 2359304 | tf_op jit(solution)/shard_map/ppermute | solution.py:40
  168.5 17.4 %collective-permute-start.35 = (bf16[128,3072]{1,0:T(8,128)(2,1)S(1)}, bf16[128,3072]{1,0:T(8,128)(2,1)S(1)}, u32[]{:S(2)}, u32[]{:S(2)}) collective-permute-start(bf16[128,3072]{1,0:T(8,128)(2,1)S(1)} %get-tuple-element.40), channel_id=1, source_target_pairs={{0,2},{1,3},{2,0},{3,1},{4,6},{5,7},{6,4},{7,5},{8,10},{9,11},{10,... | collective-permute-start | bytes 2359304 | tf_op jit(solution)/shard_map/ppermute | solution.py:40
  168.5 17.9 %collective-permute-start.36 = (bf16[128,3072]{1,0:T(8,128)(2,1)S(1)}, bf16[128,3072]{1,0:T(8,128)(2,1)S(1)}, u32[]{:S(2)}, u32[]{:S(2)}) collective-permute-start(bf16[128,3072]{1,0:T(8,128)(2,1)S(1)} %get-tuple-element.41), channel_id=1, source_target_pairs={{0,3},{1,0},{2,1},{3,2},{4,7},{5,4},{6,5},{7,6},{8,11},{9,8},{10,9... | collective-permute-start | bytes 2359304 | tf_op jit(solution)/shard_map/ppermute | solution.py:40
  182.3 8.9 %collective-permute-start.18 = (bf16[32,3072]{1,0:T(8,128)(2,1)S(1)}, bf16[32,3072]{1,0:T(8,128)(2,1)S(1)}, u32[]{:S(2)}, u32[]{:S(2)}) collective-permute-start(bf16[32,3072]{1,0:T(8,128)(2,1)S(1)} %get-tuple-element.53), channel_id=1, source_target_pairs={{0,4},{1,5},{2,6},{3,7},{4,8},{5,9},{6,10},{7,11},{8,12},{9,13},{1... | collective-permute-start | bytes 589832 | tf_op jit(solution)/shard_map/ppermute | solution.py:40
  185.8 6.3 %collective-permute-start.20 = (bf16[32,3072]{1,0:T(8,128)(2,1)S(1)}, bf16[32,3072]{1,0:T(8,128)(2,1)S(1)}, u32[]{:S(2)}, u32[]{:S(2)}) collective-permute-start(bf16[32,3072]{1,0:T(8,128)(2,1)S(1)} %get-tuple-element.54), channel_id=1, source_target_pairs={{0,12},{1,13},{2,14},{3,15},{4,0},{5,1},{6,2},{7,3},{8,4},{9,5},{1... | collective-permute-start | bytes 589832 | tf_op jit(solution)/shard_map/ppermute | solution.py:40
  186.4 7.5 %collective-permute-start.19 = (bf16[32,3072]{1,0:T(8,128)(2,1)S(1)}, bf16[32,3072]{1,0:T(8,128)(2,1)S(1)}, u32[]{:S(2)}, u32[]{:S(2)}) collective-permute-start(bf16[32,3072]{1,0:T(8,128)(2,1)S(1)} %get-tuple-element.55), channel_id=1, source_target_pairs={{0,8},{1,9},{2,10},{3,11},{4,12},{5,13},{6,14},{7,15},{8,0},{9,1},... | collective-permute-start | bytes 589832 | tf_op jit(solution)/shard_map/ppermute | solution.py:40
  191.1 5.9 %copy-start.6 = (bf16[512,1536]{1,0:T(8,128)(2,1)S(1)}, bf16[512,1536]{1,0:T(8,128)(2,1)}, u32[]{:S(2)}) copy-start(bf16[512,1536]{1,0:T(8,128)(2,1)} %copy-done.5) | copy-start | bytes 4718596
  191.2 5.8 %collective-permute-start.37 = (bf16[32,3072]{1,0:T(8,128)(2,1)S(1)}, bf16[32,3072]{1,0:T(8,128)(2,1)S(1)}, u32[]{:S(2)}, u32[]{:S(2)}) collective-permute-start(bf16[32,3072]{1,0:T(8,128)(2,1)S(1)} %get-tuple-element.50), channel_id=1, source_target_pairs={{0,4},{1,5},{2,6},{3,7},{4,8},{5,9},{6,10},{7,11},{8,12},{9,13},{1... | collective-permute-start | bytes 589832 | tf_op jit(solution)/shard_map/ppermute | solution.py:40
  192.1 16.0 %collective-permute-start.39 = (bf16[32,3072]{1,0:T(8,128)(2,1)S(1)}, bf16[32,3072]{1,0:T(8,128)(2,1)S(1)}, u32[]{:S(2)}, u32[]{:S(2)}) collective-permute-start(bf16[32,3072]{1,0:T(8,128)(2,1)S(1)} %get-tuple-element.51), channel_id=1, source_target_pairs={{0,12},{1,13},{2,14},{3,15},{4,0},{5,1},{6,2},{7,3},{8,4},{9,5},{1... | collective-permute-start | bytes 589832 | tf_op jit(solution)/shard_map/ppermute | solution.py:40
  193.9 21.6 %copy-start.16 = (bf16[512,1536]{1,0:T(8,128)(2,1)S(1)}, bf16[512,1536]{1,0:T(8,128)(2,1)}, u32[]{:S(2)}) copy-start(bf16[512,1536]{1,0:T(8,128)(2,1)} %copy-done.15) | copy-start | bytes 4718596
  193.9 15.5 %collective-permute-start.38 = (bf16[32,3072]{1,0:T(8,128)(2,1)S(1)}, bf16[32,3072]{1,0:T(8,128)(2,1)S(1)}, u32[]{:S(2)}, u32[]{:S(2)}) collective-permute-start(bf16[32,3072]{1,0:T(8,128)(2,1)S(1)} %get-tuple-element.52), channel_id=1, source_target_pairs={{0,8},{1,9},{2,10},{3,11},{4,12},{5,13},{6,14},{7,15},{8,0},{9,1},... | collective-permute-start | bytes 589832 | tf_op jit(solution)/shard_map/ppermute | solution.py:40
  197.0 25.8 %collective-permute-start.43 = (bf16[512,1536]{1,0:T(8,128)(2,1)S(1)}, bf16[512,1536]{1,0:T(8,128)(2,1)S(1)}, u32[]{:S(2)}, u32[]{:S(2)}) collective-permute-start(bf16[512,1536]{1,0:T(8,128)(2,1)S(1)} %copy-done.6), channel_id=1, source_target_pairs={{0,16},{1,17},{2,18},{3,19},{4,20},{5,21},{6,22},{7,23},{8,24},{9,... | collective-permute-start | bytes 4718600 | tf_op jit(solution)/shard_map/ppermute | solution.py:40
  208.1 7.5 %collective-permute-start.42 = (bf16[512,1536]{1,0:T(8,128)(2,1)S(1)}, bf16[512,1536]{1,0:T(8,128)(2,1)S(1)}, u32[]{:S(2)}, u32[]{:S(2)}) collective-permute-start(bf16[512,1536]{1,0:T(8,128)(2,1)S(1)} %get-tuple-element.44.r_own), channel_id=1, source_target_pairs={{0,16},{1,17},{2,18},{3,19},{4,20},{5,21},{6,22},{7,23},{8,24},{9,... | collective-permute-start | bytes 4718600 | tf_op jit(solution)/shard_map/ppermute | solution.py:40
  209.4 4.2 %collective-permute-start.21 = (bf16[32,1536]{1,0:T(8,128)(2,1)S(1)}, bf16[32,1536]{1,0:T(8,128)(2,1)S(1)}, u32[]{:S(2)}, u32[]{:S(2)}) collective-permute-start(bf16[32,1536]{1,0:T(8,128)(2,1)S(1)} %get-tuple-element.63), channel_id=1, source_target_pairs={{0,16},{1,17},{2,18},{3,19},{4,20},{5,21},{6,22},{7,23},{8,24},{9,... | collective-permute-start | bytes 294920 | tf_op jit(solution)/shard_map/ppermute | solution.py:40
  213.5 1.3 collective-permute-start.40
  215.6 7.2 %copy-start.18 = (bf16[512,1536]{1,0:T(8,128)(2,1)S(1)}, bf16[512,1536]{1,0:T(8,128)(2,1)}, u32[]{:S(2)}) copy-start(bf16[512,1536]{1,0:T(8,128)(2,1)} %copy-done.17) | copy-start | bytes 4718596

commit v2 on v1

v2 whole, which is shorter than its diff:
```python
import functools

import jax
import jax.numpy as jnp
from jax import lax
from jax.experimental import pallas as pl
from jax.experimental.pallas import tpu as pltpu
from jax.sharding import PartitionSpec as P

BF16 = jnp.bfloat16
F32 = jnp.float32
AXES = ("row", "col")
FAR = (1, 3)
NEAR = (3, 1)
RING = 4
TILE = 512
LIMIT = 62 * 1024 * 1024
SMALL = 16 * 1024 * 1024
ANYWHERE = pl.BlockSpec(memory_space=pl.ANY)


def gelu_form(value):
    return jax.nn.gelu(value, approximate=True)


def gelu_backward(value, grad):
    return jax.vjp(gelu_form, value)[1](grad)[0]


def permutation(first=0, second=0, other=0, flip=(0, 0)):
    pairs = []
    for z in range(RING):
        for core in range(2):
            for x in range(RING):
                for y in range(RING):
                    step_x, step_y = (first, second) if core == 0 else (second, first)
                    to_row = (z ^ flip[core]) * 2 + (core + other) % 2
                    to_col = ((x + step_x) % RING) * RING + (y + step_y) % RING
                    pairs.append(((z * 2 + core) * 16 + x * RING + y, to_row * 16 + to_col))
    return pairs


def send(block, **where):
    return lax.ppermute(block, AXES, permutation(**where))


def swap(block):
    return send(block, other=1)


def gather_ring(block, axis):
    return [block] + [send(block, **{axis: -step}) for step in range(1, RING)]


def scatter_ring(blocks, axis):
    got = [send(blocks[step], **{axis: step}) for step in range(1, RING)]
    total = blocks[0].astype(F32)
    for block in got:
        total = total + block.astype(F32)
    return total


def cost(rows, depth, columns, moved):
    return pl.CostEstimate(flops=2 * rows * depth * columns, bytes_accessed=moved, transcendentals=0)


def dot(left, right, transposed):
    return lax.dot_general(left, right, (((1,), (1 if transposed else 0,)), ((), ())), preferred_element_type=F32)


def up_kernel(transposed, place, p0, p1, p2, p3, w_own, w_other, after, keep, give, own, other, scratch):
    rows = p0.shape[0]
    depth = own.shape[1]

    @pl.when(pl.program_id(0) == 0)
    def _():
        start = 0
        for piece in (p0, p1, p2, p3):
            stop = start + piece.shape[0]
            own[start:stop, :] = piece[:, :depth]
            other[start:stop, :] = piece[:, depth:]
            start = stop

    total = dot(own[...], w_own[...], transposed) + dot(other[...], w_other[...], transposed)
    scratch[...] = total
    for index in range(RING):
        part = scratch[pl.ds(pl.multiple_of(place[index] * rows, rows), rows), :]
        if index < 2:
            keep[index * rows : (index + 1) * rows, :] = part
        else:
            give[(index - 2) * rows : (index - 1) * rows, :] = part.astype(BF16)


def project_up(place, pieces, w_own, w_other, transposed, after):
    rows, width = pieces[0].shape
    depth = width // 2
    columns = w_own.shape[0 if transposed else 1]
    tile = min(TILE, columns)
    whole = [pl.BlockSpec(piece.shape, lambda n: (0, 0)) for piece in pieces]
    if transposed:
        weight = pl.BlockSpec((tile, depth), lambda n: (n, 0))
    else:
        weight = pl.BlockSpec((depth, tile), lambda n: (0, n))
    kept = pl.BlockSpec((RING * rows, depth), lambda n: (0, 0))
    outs = pl.pallas_call(
        functools.partial(up_kernel, transposed),
        grid=(columns // tile,),
        in_specs=[pl.BlockSpec(memory_space=pltpu.SMEM)] + whole + [weight] * 2 + [ANYWHERE],
        out_specs=[pl.BlockSpec((2 * rows, tile), lambda n: (0, n))] * 2 + [kept] * 2,
        out_shape=[jax.ShapeDtypeStruct((2 * rows, columns), dtype) for dtype in (F32, BF16)]
        + [jax.ShapeDtypeStruct((RING * rows, depth), BF16)] * 2,
        scratch_shapes=[pltpu.VMEM((RING * rows, tile), F32)],
        compiler_params=pltpu.CompilerParams(vmem_limit_bytes=LIMIT),
        cost_estimate=cost(RING * rows, width, columns, 2 * (width * columns + 2 * RING * rows * width)),
    )(place, *pieces, w_own, w_other, after)
    return outs


def down_kernel(transposed, place, near, far, w_own, w_other, after, later, y0, y1, y2, y3, kept):
    rows = near.shape[0] // 2
    step = pl.program_id(0)
    half = pl.num_programs(0) // 2

    @pl.when(step == 0)
    def _():
        for index in range(RING):
            piece = (near, far)[index // 2]
            start = pl.multiple_of(place[index] * rows, rows)
            kept[pl.ds(start, rows), :] = piece[(index % 2) * rows : (index % 2 + 1) * rows, :]

    def finish(weight):
        total = dot(kept[...], weight[...], transposed).astype(BF16)
        for index, out in enumerate((y0, y1, y2, y3)):
            out[...] = total[index * rows : (index + 1) * rows, :]

    @pl.when(step < half)
    def _():
        finish(w_own)

    @pl.when(step >= half)
    def _():
        finish(w_other)


def project_down(place, pieces, w_own, w_other, transposed, after):
    rows, depth = pieces[0].shape[0] // 2, pieces[0].shape[1]
    columns = w_own.shape[0 if transposed else 1]
    tile = min(TILE, columns)
    half = columns // tile
    whole = pl.BlockSpec((2 * rows, depth), lambda n: (0, 0))
    if transposed:
        own = pl.BlockSpec((tile, depth), lambda n: (jnp.minimum(n, half - 1), 0))
        other = pl.BlockSpec((tile, depth), lambda n: (jnp.maximum(n - half, 0), 0))
    else:
        own = pl.BlockSpec((depth, tile), lambda n: (0, jnp.minimum(n, half - 1)))
        other = pl.BlockSpec((depth, tile), lambda n: (0, jnp.maximum(n - half, 0)))
    outs = pl.pallas_call(
        functools.partial(down_kernel, transposed),
        grid=(2 * half,),
        in_specs=[pl.BlockSpec(memory_space=pltpu.SMEM)] + [whole] * 2 + [own, other, ANYWHERE, ANYWHERE],
        out_specs=[pl.BlockSpec((rows, tile), lambda n: (0, n))] * RING
        + [pl.BlockSpec((RING * rows, depth), lambda n: (0, 0))],
        out_shape=[jax.ShapeDtypeStruct((rows, 2 * columns), BF16)] * RING
        + [jax.ShapeDtypeStruct((RING * rows, depth), BF16)],
        compiler_params=pltpu.CompilerParams(vmem_limit_bytes=LIMIT),
        cost_estimate=cost(
            RING * rows, depth, 2 * columns, 2 * (2 * depth * columns + 2 * RING * rows * (depth + columns))
        ),
    )(place, *pieces, w_own, w_other, *after)
    return outs[:RING], outs[RING]


def weight_kernel(l_own, l_other, r_own, r_other, after, out):
    dims = (((0,), (0,)), ((), ()))
    total = lax.dot_general(l_own[...], r_own[...], dims, preferred_element_type=F32)
    total = total + lax.dot_general(l_other[...], r_other[...], dims, preferred_element_type=F32)
    out[...] = total.astype(BF16)


def weight_grad(l_own, l_other, r_own, r_other, after):
    tokens, rows = l_own.shape
    columns = r_own.shape[1]
    tile = min(TILE, rows)
    left = pl.BlockSpec((tokens, tile), lambda m: (0, m))
    right = pl.BlockSpec((tokens, columns), lambda m: (0, 0))
    return pl.pallas_call(
        weight_kernel,
        grid=(rows // tile,),
        in_specs=[left, left, right, right, ANYWHERE],
        out_specs=pl.BlockSpec((tile, columns), lambda m: (m, 0)),
        out_shape=jax.ShapeDtypeStruct((rows, columns), BF16),
        compiler_params=pltpu.CompilerParams(vmem_limit_bytes=LIMIT),
        cost_estimate=cost(rows, 2 * tokens, columns, 2 * (rows * columns + 2 * tokens * (rows + columns))),
    )(l_own, l_other, r_own, r_other, after)


def join_kernel(p0, p1, p2, p3, after, out):
    rows = p0.shape[0] // 2
    for index, piece in enumerate((p0, p1, p2, p3)):
        out[index * rows : (index + 1) * rows, :] = piece[rows:, :]


def join(parts, after):
    rows, width = parts[0].shape
    whole = pl.BlockSpec(memory_space=pltpu.VMEM)
    return pl.pallas_call(
        join_kernel,
        in_specs=[whole] * RING + [ANYWHERE],
        out_specs=whole,
        out_shape=jax.ShapeDtypeStruct((2 * rows, width), BF16),
        compiler_params=pltpu.CompilerParams(vmem_limit_bytes=SMALL),
        cost_estimate=cost(0, 0, 0, 4 * rows * width),
    )(*parts, after)


def add_kernel(p0, p1, p2, p3, first, z0, z1, z2, z3):
    total = p0[...].astype(F32) + p1[...].astype(F32) + p2[...].astype(F32) + p3[...].astype(F32)
    total = total.astype(BF16)
    rows = z0.shape[0] // 2
    for index, out in enumerate((z0, z1, z2, z3)):
        out[:rows, :] = first[index * rows : (index + 1) * rows, :]
        out[rows:, :] = total[index * rows : (index + 1) * rows, :]


def add_parts(parts, first):
    rows, width = parts[0].shape
    tile = min(1024, width)
    return pl.pallas_call(
        add_kernel,
        grid=(width // tile,),
        in_specs=[pl.BlockSpec((rows, tile), lambda n: (0, n))] * (RING + 1),
        out_specs=[pl.BlockSpec((rows // 2, tile), lambda n: (0, n))] * RING,
        out_shape=[jax.ShapeDtypeStruct((rows // 2, width), BF16)] * RING,
        compiler_params=pltpu.CompilerParams(vmem_limit_bytes=SMALL),
        cost_estimate=cost(0, 0, 0, 4 * rows * width),
    )(*parts, first)


def together(*values):
    return lax.optimization_barrier(values)


def total_of(blocks):
    total = blocks[0].astype(F32)
    for block in blocks[1:]:
        total = total + block.astype(F32)
    return total


def scatter_far(keep, got):
    rows = keep.shape[0] // 2
    total = keep + got.astype(F32)
    return lax.optimization_barrier((total[:rows], total[rows:].astype(BF16)))


def gather_near(block):
    return jnp.concatenate([block, send(block, flip=NEAR)])


def exchange(blocks, axis):
    return [blocks[0]] + [send(blocks[step], **{axis: step}) for step in range(1, RING)]


def local(inputs, w_in, w_out, cotangent):
    row = lax.axis_index("row")
    core = lax.rem(row, 2)
    level = lax.div(row, 2)
    far = jnp.where(core == 0, FAR[0], FAR[1])
    place = jnp.stack([level, level ^ far ^ 2, level ^ far, level ^ 2]).astype(jnp.int32)
    half, width = inputs.shape[0] // 2, inputs.shape[1]

    def halves(which):
        return [lax.dynamic_slice_in_dim(block, which * half, half) for block in (inputs, cotangent)]

    chip = jnp.concatenate([jnp.concatenate(halves(core)), swap(jnp.concatenate(halves(1 - core)))], axis=1)
    w_in_late, chip = together(w_in, chip)
    w_in_other = swap(w_in_late)

    parts = gather_ring(chip, "first")
    input_block, w_out_late, w_in_other = together(
        jnp.concatenate([part[:half] for part in parts]), w_out, w_in_other
    )
    w_out_other = swap(w_out_late)
    input_pieces = gather_ring(input_block, "second")
    cotangent_block, w_out_other = together(join(parts, input_pieces[1]), w_out_other)
    cotangent_pieces = gather_ring(cotangent_block, "second")

    keep, give, input_own, input_sent = project_up(place, input_pieces, w_in, w_in_other, False, cotangent_block)
    give, cotangent_pieces[1], cotangent_pieces[3] = together(give, cotangent_pieces[1], cotangent_pieces[3])
    hidden, passed = scatter_far(keep, send(give, flip=FAR))
    passed, input_got = together(passed, swap(input_sent))
    hidden_got = send(passed, flip=NEAR)
    keep, give, cotangent_own, cotangent_sent = project_up(
        place, cotangent_pieces, w_out, w_out_other, True, passed
    )
    give, hidden_got = together(give, hidden_got)

    hidden = hidden + hidden_got.astype(F32)
    hidden, activated = together(hidden, gelu_form(hidden).astype(BF16))
    grad_got, near = together(send(give, flip=FAR), gather_near(activated))
    activated = [near, send(near, flip=FAR)]
    grad_activated, passed = scatter_far(keep, grad_got)
    passed, cotangent_got = together(passed, swap(cotangent_sent))

    grad_activated = grad_activated + send(passed, flip=NEAR).astype(F32)
    grad_hidden = gelu_backward(hidden, grad_activated).astype(BF16)
    near = gather_near(grad_hidden)
    grad_hidden = [near, send(near, flip=FAR)]
    output_parts, activated_own = project_down(
        place, activated, w_out, w_out_other, False, (near, input_got)
    )
    activated_got = swap(activated_own)
    output_blocks = exchange(output_parts, "second")

    input_parts, grad_hidden_own = project_down(
        place, grad_hidden, w_in, w_in_other, True, (activated_own, place)
    )
    input_blocks = exchange(input_parts, "second")
    output_sum = total_of(output_blocks).astype(BF16)
    grad_w_out = weight_grad(activated_own, activated_got, cotangent_own, cotangent_got, output_sum)
    grad_w_in = weight_grad(input_own, input_got, grad_hidden_own, swap(grad_hidden_own), grad_w_out)
    *input_blocks, output_sum, grad_w_in = together(*input_blocks, output_sum, grad_w_in)
    both = scatter_ring(add_parts(input_blocks, output_sum), "first").astype(BF16)
    kept, got = both[:, :width], swap(both[:, width:])

    def whole(start):
        mine, theirs = kept[start : start + half], got[start : start + half]
        return jnp.where(core == 0, jnp.concatenate([mine, theirs]), jnp.concatenate([theirs, mine]))

    return (whole(0), whole(half), grad_w_in, grad_w_out)


def solution(mesh):
    in_specs = (P("col", "row"), P("row", "col"), P("col", "row"), P("col", "row"))
    out_specs = (P("col", "row"), P("col", "row"), P("row", "col"), P("col", "row"))
    return jax.shard_map(local, mesh=mesh, in_specs=in_specs, out_specs=out_specs, check_vma=False)
```

time: 231 us -> 205 us (0.89)
  starting transfers between devices: 78.6 us -> 42.4 us
  waiting for transfers between devices: 73.1 us -> 85.1 us
  local copies, waits for them, and re-layouts: 17.3 us -> 5.45 us
  Pallas kernels: 53.8 us -> 63.2 us
    ppermute x45 -> x34, starting transfers between devices: 78.6 us -> 42.4 us  [send(): return lax.ppermute(block, AXES, permutation(**where))]
    unnamed x38 -> x30, local copies, waits for them, and re-layouts: 17.2 us -> 3.09 us
    ppermute x45 -> x34, waiting for transfers between devices: 73.1 us -> 85.1 us  [send(): return lax.ppermute(block, AXES, permutation(**where))]
    pallas_call x2, Pallas kernels: 14.4 us -> 17.9 us  [weight_grad(): pl.pallas_call(weight_kernel, grid=(rows // tile,), in_specs=[left, left,...]
    convert_element_type x3 -> x4, other arithmetic: 1.12 us -> 4.07 us  [the longest x1 2.98 us: local(): output_sum = total_of(output_blocks).astype(BF16)]
    pallas_call x0 -> x2, Pallas kernels: none -> 2.72 us  [the longest x1 2.67 us: add_parts(): pl.pallas_call(add_kernel, grid=(width // tile,), in_specs=[pl.BlockSpec(...]
    pallas_call x2, Pallas kernels: 17 us -> 19.7 us  [project_up(): pl.pallas_call(functools.partial(up_kernel, transposed), grid=(columns //...]
  transfers between devices with their start and end apart: 45 -> 34, of which waited for: 18 -> 15; matrix products, arithmetic and copies ran while one was open for 2% -> 3% of each run, Pallas kernels for 20% -> 30%
where the time goes in v2:
time: 205 us
  waiting for transfers between devices  85.1 us (42%)
  Pallas kernels  63.2 us (31%)
  starting transfers between devices  42.4 us (21%)
  other arithmetic  7.54 us (4%)
  local copies, waits for them, and re-layouts  5.45 us (3%)
    ppermute x34, waiting for transfers between devices, send(): return lax.ppermute(block, AXES, permutation(**where))  85.1 us
    ppermute x34, starting transfers between devices, send(): return lax.ppermute(block, AXES, permutation(**where))  42.4 us
    pallas_call x2, Pallas kernels, project_down(): pl.pallas_call(functools.partial(down_kernel, transposed), grid=(2 * half...  22.8 us
    pallas_call x2, Pallas kernels, project_up(): pl.pallas_call(functools.partial(up_kernel, transposed), grid=(columns //...  19.7 us
    pallas_call x2, Pallas kernels, weight_grad(): pl.pallas_call(weight_kernel, grid=(rows // tile,), in_specs=[left, left,...  17.9 us
  transfers between devices with their start and end apart: 34, of which 15 were waited for; matrix products, arithmetic and copies ran while one was open for 3% of the time, Pallas kernels for 30%

profile of v2, /device:TPU:1, one launch (start us, length us, event | category | flops | bytes accessed | tf_op | source)
XLA Modules:
  0.0 204.7 jit_solution(5630172328239373978)
XLA Ops:
  0.6 1.0 constant_dynamic-slice_fusion.3
  1.6 1.1 constant_dynamic-slice_fusion.2
  2.8 1.5 collective-permute-start
  4.3 1.1 collective-permute-done
  5.4 0.5 collective-permute-start.4
  5.8 1.4 collective-permute-start.3
  7.2 2.6 %collective-permute-start.2 = (bf16[64,3072]{1,0:T(8,128)(2,1)S(1)}, bf16[64,3072]{1,0:T(8,128)(2,1)S(1)}, u32[]{:S(2)}, u32[]{:S(2)}) collective-permute-start(bf16[64,3072]{1,0:T(8,128)(2,1)S(1)} %pad_maximum_fusion.3.p0), channel_id=1, source_target_pairs={{0,8},{1,9},{2,10},{3,11},{4,12},{5,13},{6,14},{7,15},{8,0},{9,1},... | collective-permute-start | bytes 1179656 | tf_op jit(solution)/shard_map/ppermute | solution.py:44
  9.8 1.1 collective-permute-start.1
  10.9 3.2 %collective-permute-done.3.p3 = bf16[64,3072]{1,0:T(8,128)(2,1)S(1)} collective-permute-done((bf16[64,3072]{1,0:T(8,128)(2,1)S(1)}, bf16[64,3072]{1,0:T(8,128)(2,1)S(1)}, u32[]{:S(2)}, u32[]{:S(2)}) %collective-permute-start.3) | collective-permute-done | bytes 393248 | tf_op jit(solution)/shard_map/ppermute | solution.py:44
  14.1 5.4 %collective-permute-done.2.p2 = bf16[64,3072]{1,0:T(8,128)(2,1)S(1)} collective-permute-done((bf16[64,3072]{1,0:T(8,128)(2,1)S(1)}, bf16[64,3072]{1,0:T(8,128)(2,1)S(1)}, u32[]{:S(2)}, u32[]{:S(2)}) %collective-permute-start.2) | collective-permute-done | bytes 393248 | tf_op jit(solution)/shard_map/ppermute | solution.py:44
  19.6 0.8 collective-permute-start.6
  20.5 2.1 %collective-permute-start.5 = (bf16[128,3072]{1,0:T(8,128)(2,1)S(1)}, bf16[128,3072]{1,0:T(8,128)(2,1)S(1)}, u32[]{:S(2)}, u32[]{:S(2)}) collective-permute-start(bf16[128,3072]{1,0:T(8,128)(2,1)S(1)} %pad_maximum_fusion.p0), channel_id=1, source_target_pairs={{0,3},{1,0},{2,1},{3,2},{4,7},{5,4},{6,5},{7,6},{8,11},{9,8},{10,9... | collective-permute-start | bytes 2359304 | tf_op jit(solution)/shard_map/ppermute | solution.py:44
  22.6 1.9 collective-permute-start.7
  24.5 15.4 %collective-permute-done.5.after.p1 = bf16[128,3072]{1,0:T(8,128)(2,1)S(1)} collective-permute-done((bf16[128,3072]{1,0:T(8,128)(2,1)S(1)}, bf16[128,3072]{1,0:T(8,128)(2,1)S(1)}, u32[]{:S(2)}, u32[]{:S(2)}) %collective-permute-start.5) | collective-permute-done | bytes 786464 | tf_op jit(solution)/shard_map/ppermute | solution.py:44
  40.1 0.1 collective-permute-start.10
  40.1 2.2 %copy-done.12 = bf16[1536,1536]{1,0:T(8,128)(2,1)} copy-done((bf16[1536,1536]{1,0:T(8,128)(2,1)}, bf16[1536,1536]{1,0:T(8,128)(2,1)S(1)}, u32[]{:S(2)}) %copy-start.12) | copy-done | bytes 4718616
  42.3 3.5 %collective-permute-start.9 = (bf16[128,3072]{1,0:T(8,128)(2,1)S(1)}, bf16[128,3072]{1,0:T(8,128)(2,1)}, u32[]{:S(2)}, u32[]{:S(2)}) collective-permute-start(bf16[128,3072]{1,0:T(8,128)(2,1)S(1)} %shard_map.75.after.p0), channel_id=1, source_target_pairs={{0,3},{1,0},{2,1},{3,2},{4,7},{5,4},{6,5},{7,6},{8,11},{9,8},{10,9... | collective-permute-start | bytes 2359304 | tf_op jit(solution)/shard_map/ppermute | solution.py:44
  45.8 0.7 pad_add_fusion.place.later
  46.5 9.9 %shard_map.76 = (f32[256,1536]{1,0:T(8,128)}, bf16[256,1536]{1,0:T(8,128)(2,1)}, bf16[512,1536]{1,0:T(8,128)(2,1)}, bf16[512,1536]{1,0:T(8,128)(2,1)}) custom-call(s32[4]{0:T(128)} %pad_add_fusion.place.later, bf16[128,3072]{1,0:T(8,128)(2,1)} %copy-done.5, bf16[128,3072]{1,0:T(8,128)(2,1)} %copy-done.2, bf16[128,3072]{1,0:T(8,128)(2,1)} %collective-permute-done.7.p2, ...), custom_call_target="tpu_custom_call" | custom-call | flops 4831838208 | bytes 15728640 | tf_op jit(solution)/shard_map/pallas_call | solution.py:105
  56.4 1.7 collective-permute-start.13
  58.1 3.8 %collective-permute-start.12 = (bf16[256,1536]{1,0:T(8,128)(2,1)}, bf16[256,1536]{1,0:T(8,128)(2,1)S(1)}, u32[]{:S(2)}, u32[]{:S(2)}) collective-permute-start(bf16[256,1536]{1,0:T(8,128)(2,1)} %get-tuple-element.67), channel_id=1, source_target_pairs={{0,32},{1,33},{2,34},{3,35},{4,36},{5,37},{6,38},{7,39},{8,40},{9,... | collective-permute-start | bytes 2359304 | tf_op jit(solution)/shard_map/ppermute | solution.py:44
  61.8 2.6 %collective-permute-start.11 = (bf16[128,3072]{1,0:T(8,128)(2,1)}, bf16[128,3072]{1,0:T(8,128)(2,1)}, u32[]{:S(2)}, u32[]{:S(2)}) collective-permute-start(bf16[128,3072]{1,0:T(8,128)(2,1)} %copy-done.1), channel_id=1, source_target_pairs={{0,2},{1,3},{2,0},{3,1},{4,6},{5,7},{6,4},{7,5},{8,10},{9,11},{10,... | collective-permute-start | bytes 2359304 | tf_op jit(solution)/shard_map/ppermute | solution.py:44
  64.5 7.4 %collective-permute-done.12 = bf16[256,1536]{1,0:T(8,128)(2,1)S(1)} collective-permute-done((bf16[256,1536]{1,0:T(8,128)(2,1)}, bf16[256,1536]{1,0:T(8,128)(2,1)S(1)}, u32[]{:S(2)}, u32[]{:S(2)}) %collective-permute-start.12) | collective-permute-done | bytes 786464 | tf_op jit(solution)/shard_map/ppermute | solution.py:44
  71.8 1.6 convert_add_fusion.1
  73.6 0.1 collective-permute-start.14
  73.7 0.8 collective-permute-done.11.p2
  74.5 9.9 %shard_map.77 = (f32[256,1536]{1,0:T(8,128)}, bf16[256,1536]{1,0:T(8,128)(2,1)}, bf16[512,1536]{1,0:T(8,128)(2,1)}, bf16[512,1536]{1,0:T(8,128)(2,1)}) custom-call(s32[4]{0:T(128)} %pad_add_fusion.place.later, bf16[128,3072]{1,0:T(8,128)(2,1)} %copy-done.1, bf16[128,3072]{1,0:T(8,128)(2,1)} %collective-permute-done.9.p1, ...), custom_call_target="tpu_custom_call" | custom-call | flops 4831838208 | bytes 15728640 | tf_op jit(solution)/shard_map/pallas_call | solution.py:105
  84.4 1.8 collective-permute-start.17
  86.2 0.8 collective-permute-start.15
  86.9 0.3 fusion.14
  87.2 0.4 collective-permute-start.16
  87.6 10.8 %collective-permute-done.16 = bf16[128,1536]{1,0:T(8,128)(2,1)S(1)} collective-permute-done((bf16[128,1536]{1,0:T(8,128)(2,1)S(1)}, bf16[128,1536]{1,0:T(8,128)(2,1)S(1)}, u32[]{:S(2)}, u32[]{:S(2)}) %collective-permute-start.16) | collective-permute-done | bytes 393248 | tf_op jit(solution)/shard_map/ppermute | solution.py:44
  98.4 4.2 %collective-permute-done.15 = bf16[256,1536]{1,0:T(8,128)(2,1)S(1)} collective-permute-done((bf16[256,1536]{1,0:T(8,128)(2,1)}, bf16[256,1536]{1,0:T(8,128)(2,1)S(1)}, u32[]{:S(2)}, u32[]{:S(2)}) %collective-permute-start.15) | collective-permute-done | bytes 786464 | tf_op jit(solution)/shard_map/ppermute | solution.py:44
  102.6 0.2 convert_add_fusion
  103.0 0.1 collective-permute-start.18
  103.1 6.9 %collective-permute-done.18 = bf16[128,1536]{1,0:T(8,128)(2,1)S(1)} collective-permute-done((bf16[128,1536]{1,0:T(8,128)(2,1)S(1)}, bf16[128,1536]{1,0:T(8,128)(2,1)S(1)}, u32[]{:S(2)}, u32[]{:S(2)}) %collective-permute-start.18) | collective-permute-done | bytes 393248 | tf_op jit(solution)/shard_map/ppermute | solution.py:44
  110.0 0.6 fusion.6
  110.6 0.1 collective-permute-start.19
  110.7 0.8 collective-permute-start.21
  111.5 6.3 %collective-permute-done.19 = bf16[128,1536]{1,0:T(8,128)(2,1)S(1)} collective-permute-done((bf16[128,1536]{1,0:T(8,128)(2,1)S(1)}, bf16[128,1536]{1,0:T(8,128)(2,1)S(1)}, u32[]{:S(2)}, u32[]{:S(2)}) %collective-permute-start.19) | collective-permute-done | bytes 393248 | tf_op jit(solution)/shard_map/ppermute | solution.py:44
  117.9 0.8 collective-permute-start.20
  118.7 8.3 %collective-permute-done.21.far = bf16[256,1536]{1,0:T(8,128)(2,1)S(1)} collective-permute-done((bf16[256,1536]{1,0:T(8,128)(2,1)S(1)}, bf16[256,1536]{1,0:T(8,128)(2,1)S(1)}, u32[]{:S(2)}, u32[]{:S(2)}) %collective-permute-start.21) | collective-permute-done | bytes 786464 | tf_op jit(solution)/shard_map/ppermute | solution.py:44
  127.0 0.9 copy-done.14
  127.9 11.3 %shard_map.78 = (bf16[128,3072]{1,0:T(8,128)(2,1)}, bf16[128,3072]{1,0:T(8,128)(2,1)}, bf16[128,3072]{1,0:T(8,128)(2,1)}, bf16[128,3072]{1,0:T(8,128)(2,1)}, bf16[512,1536]{1,0:T(8,128)(2,1)}) custom-call(s32[4]{0:T(128)} %pad_add_fusion.place.later, bf16[256,1536]{1,0:T(8,128)(2,1)} %copy-done.6, bf16[256,1536]{1,0:T(8,128)(2,1)} %copy-done.14, ...), custom_call_target="tpu_custom_call" | custom-call | flops 4831838208 | bytes 15728640 | tf_op jit(solution)/shard_map/pallas_call | solution.py:157
  139.2 1.6 collective-permute-start.25
  140.8 1.8 collective-permute-start.26
  142.7 1.3 collective-permute-start.27
  144.0 11.5 %shard_map.79 = (bf16[128,3072]{1,0:T(8,128)(2,1)}, bf16[128,3072]{1,0:T(8,128)(2,1)}, bf16[128,3072]{1,0:T(8,128)(2,1)}, bf16[128,3072]{1,0:T(8,128)(2,1)}, bf16[512,1536]{1,0:T(8,128)(2,1)}) custom-call(s32[4]{0:T(128)} %pad_add_fusion.place.later, bf16[256,1536]{1,0:T(8,128)(2,1)} %copy-done.7, bf16[256,1536]{1,0:T(8,128)(2,1)} %collective-permute-done.20.far, ...), custom_call_target="tpu_custom_call" | custom-call | flops 4831838208 | bytes 15728640 | tf_op jit(solution)/shard_map/pallas_call | solution.py:157
  155.5 0.6 collective-permute-start.28
  156.0 0.4 collective-permute-start.22
  156.5 4.6 %collective-permute-done.26 = bf16[128,3072]{1,0:T(8,128)(2,1)} collective-permute-done((bf16[128,3072]{1,0:T(8,128)(2,1)}, bf16[128,3072]{1,0:T(8,128)(2,1)}, u32[]{:S(2)}, u32[]{:S(2)}) %collective-permute-start.26) | collective-permute-done | bytes 786464 | tf_op jit(solution)/shard_map/ppermute | solution.py:44
  161.1 1.2 collective-permute-start.23
  162.2 1.1 collective-permute-start.24
  163.3 3.0 %add_convert_fusion.after.first = bf16[128,3072]{1,0:T(8,128)(2,1)} fusion(bf16[128,3072]{1,0:T(8,128)(2,1)} %collective-permute-done.27, bf16[128,3072]{1,0:T(8,128)(2,1)} %collective-permute-done.26, bf16[128,3072]{1,0:T(8,128)(2,1)} %collective-permute-done.25, bf16[128,3072]{1,0:T(8,128)(2,1)S(1)} %copy-done.8), kind=kLoop, calls=%fused_computation | loop fusion | flops 3145728 | bytes 3932160 | tf_op jit(solution)/shard_map/convert_element_type | solution.py:319
  166.3 8.9 %shard_map.80.after = bf16[1536,1536]{1,0:T(8,128)(2,1)} custom-call(bf16[512,1536]{1,0:T(8,128)(2,1)} %get-tuple-element.85.after.l_own, bf16[512,1536]{1,0:T(8,128)(2,1)} %collective-permute-done.29.l_other, bf16[512,1536]{1,0:T(8,128)(2,1)} %get-tuple-element.96.r_own, bf16[512,1536]{1,0:T(8,128)(2,1)} %copy-done.13, ...), custom_call_target="tpu_custom_call" | custom-call | flops 4831838208 | bytes 11010048 | tf_op jit(solution)/shard_map/pallas_call | solution.py:186
  175.2 9.0 %shard_map.81 = bf16[1536,1536]{1,0:T(8,128)(2,1)} custom-call(bf16[512,1536]{1,0:T(8,128)(2,1)} %get-tuple-element.94.l_own, bf16[512,1536]{1,0:T(8,128)(2,1)} %collective-permute-done.13.later.l_other, bf16[512,1536]{1,0:T(8,128)(2,1)} %get-tuple-element.95.r_own, bf16[512,1536]{1,0:T(8,128)(2,1)} %collective-permute-done.28.r_other, ...), custom_call_target="tpu_custom_call" | custom-call | flops 4831838208 | bytes 11010048 | tf_op jit(solution)/shard_map/pallas_call | solution.py:186
  184.3 2.7 %shard_map.82 = (bf16[64,3072]{1,0:T(8,128)(2,1)S(1)}, bf16[64,3072]{1,0:T(8,128)(2,1)S(1)}, bf16[64,3072]{1,0:T(8,128)(2,1)S(1)}, bf16[64,3072]{1,0:T(8,128)(2,1)S(1)}) custom-call(bf16[128,3072]{1,0:T(8,128)(2,1)S(1)} %copy-done.3, bf16[128,3072]{1,0:T(8,128)(2,1)} %collective-permute-done.22.p1, bf16[128,3072]{1,0:T(8,128)(2,1)} %collective-permute-done.23.p2, ...), custom_call_target="tpu_custom_call" | custom-call | bytes 1572864 | tf_op jit(solution)/shard_map/pallas_call | solution.py:228
  187.0 3.5 %collective-permute-start.31 = (bf16[64,3072]{1,0:T(8,128)(2,1)S(1)}, bf16[64,3072]{1,0:T(8,128)(2,1)S(1)}, u32[]{:S(2)}, u32[]{:S(2)}) collective-permute-start(bf16[64,3072]{1,0:T(8,128)(2,1)S(1)} %get-tuple-element.105), channel_id=1, source_target_pairs={{0,8},{1,9},{2,10},{3,11},{4,12},{5,13},{6,14},{7,15},{8,0},{9,1},... | collective-permute-start | bytes 1179656 | tf_op jit(solution)/shard_map/ppermute | solution.py:44
  190.6 4.6 %collective-permute-done.30 = bf16[64,3072]{1,0:T(8,128)(2,1)S(1)} collective-permute-done((bf16[64,3072]{1,0:T(8,128)(2,1)S(1)}, bf16[64,3072]{1,0:T(8,128)(2,1)S(1)}, u32[]{:S(2)}, u32[]{:S(2)}) %collective-permute-start.30) | collective-permute-done | bytes 393248 | tf_op jit(solution)/shard_map/ppermute | solution.py:44
  195.2 5.1 %collective-permute-done.31 = bf16[64,3072]{1,0:T(8,128)(2,1)S(1)} collective-permute-done((bf16[64,3072]{1,0:T(8,128)(2,1)S(1)}, bf16[64,3072]{1,0:T(8,128)(2,1)S(1)}, u32[]{:S(2)}, u32[]{:S(2)}) %collective-permute-start.31) | collective-permute-done | bytes 393248 | tf_op jit(solution)/shard_map/ppermute | solution.py:44
  200.2 0.2 add_convert_fusion.1
  200.4 2.4 %collective-permute-start.33 = (bf16[64,1536]{1,0:T(8,128)(2,1)S(1)}, bf16[64,1536]{1,0:T(8,128)(2,1)S(1)}, u32[]{:S(2)}, u32[]{:S(2)}) collective-permute-start(bf16[64,1536]{1,0:T(8,128)(2,1)S(1)} %slice.65), channel_id=1, source_target_pairs={{0,16},{1,17},{2,18},{3,19},{4,20},{5,21},{6,22},{7,23},{8,24},{9,... | collective-permute-start | bytes 589832 | tf_op jit(solution)/shard_map/ppermute | solution.py:44
  202.8 1.1 collective-permute-done.33
  203.9 0.8 maximum_select_fusion
  (68 shorter events, 0.7 us)
Async XLA Ops:
  1.6 18.0 %copy-start.10 = (bf16[1536,1536]{1,0:T(8,128)(2,1)S(1)}, bf16[1536,1536]{1,0:T(8,128)(2,1)}, u32[]{:S(2)}) copy-start(bf16[1536,1536]{1,0:T(8,128)(2,1)} %w_own.6) | copy-start | bytes 14155780
  2.8 2.6 %collective-permute-start = (bf16[64,1536]{1,0:T(8,128)(2,1)S(1)}, bf16[64,1536]{1,0:T(8,128)(2,1)S(1)}, u32[]{:S(2)}, u32[]{:S(2)}) collective-permute-start(bf16[64,1536]{1,0:T(8,128)(2,1)S(1)} %pad_maximum_fusion.4), channel_id=1, source_target_pairs={{0,16},{1,17},{2,18},{3,19},{4,20},{5,21},{6,22},{7,23},{8,24},{9,... | collective-permute-start | bytes 589832 | tf_op jit(solution)/shard_map/ppermute | solution.py:44
  5.4 14.2 %collective-permute-start.4 = (bf16[1536,1536]{1,0:T(8,128)(2,1)}, bf16[1536,1536]{1,0:T(8,128)(2,1)S(1)}, u32[]{:S(2)}, u32[]{:S(2)}) collective-permute-start(bf16[1536,1536]{1,0:T(8,128)(2,1)} %w_own.7), channel_id=1, source_target_pairs={{0,16},{1,17},{2,18},{3,19},{4,20},{5,21},{6,22},{7,23},{8,24},{9,... | collective-permute-start | bytes 14155784 | tf_op jit(solution)/shard_map/ppermute | solution.py:44
  5.8 8.3 %collective-permute-start.3 = (bf16[64,3072]{1,0:T(8,128)(2,1)S(1)}, bf16[64,3072]{1,0:T(8,128)(2,1)S(1)}, u32[]{:S(2)}, u32[]{:S(2)}) collective-permute-start(bf16[64,3072]{1,0:T(8,128)(2,1)S(1)} %pad_maximum_fusion.3.p0), channel_id=1, source_target_pairs={{0,4},{1,5},{2,6},{3,7},{4,8},{5,9},{6,10},{7,11},{8,12},{9,13},{1... | collective-permute-start | bytes 1179656 | tf_op jit(solution)/shard_map/ppermute | solution.py:44
  7.2 12.3 %collective-permute-start.2 = (bf16[64,3072]{1,0:T(8,128)(2,1)S(1)}, bf16[64,3072]{1,0:T(8,128)(2,1)S(1)}, u32[]{:S(2)}, u32[]{:S(2)}) collective-permute-start(bf16[64,3072]{1,0:T(8,128)(2,1)S(1)} %pad_maximum_fusion.3.p0), channel_id=1, source_target_pairs={{0,8},{1,9},{2,10},{3,11},{4,12},{5,13},{6,14},{7,15},{8,0},{9,1},... | collective-permute-start | bytes 1179656 | tf_op jit(solution)/shard_map/ppermute | solution.py:44
  9.8 9.7 %collective-permute-start.1 = (bf16[64,3072]{1,0:T(8,128)(2,1)S(1)}, bf16[64,3072]{1,0:T(8,128)(2,1)S(1)}, u32[]{:S(2)}, u32[]{:S(2)}) collective-permute-start(bf16[64,3072]{1,0:T(8,128)(2,1)S(1)} %pad_maximum_fusion.3.p0), channel_id=1, source_target_pairs={{0,12},{1,13},{2,14},{3,15},{4,0},{5,1},{6,2},{7,3},{8,4},{9,5},{1... | collective-permute-start | bytes 1179656 | tf_op jit(solution)/shard_map/ppermute | solution.py:44
  19.6 26.2 %copy-start.5 = (bf16[128,3072]{1,0:T(8,128)(2,1)}, bf16[128,3072]{1,0:T(8,128)(2,1)S(1)}, u32[]{:S(2)}) copy-start(bf16[128,3072]{1,0:T(8,128)(2,1)S(1)} %pad_maximum_fusion.p0) | copy-start | bytes 2359300
  19.6 20.4 %copy-start.11 = (bf16[1536,1536]{1,0:T(8,128)(2,1)}, bf16[1536,1536]{1,0:T(8,128)(2,1)S(1)}, u32[]{:S(2)}) copy-start(bf16[1536,1536]{1,0:T(8,128)(2,1)S(1)} %collective-permute-done.4.w_other) | copy-start | bytes 14155780
  19.6 20.4 %collective-permute-start.6 = (bf16[1536,1536]{1,0:T(8,128)(2,1)S(1)}, bf16[1536,1536]{1,0:T(8,128)(2,1)S(1)}, u32[]{:S(2)}, u32[]{:S(2)}) collective-permute-start(bf16[1536,1536]{1,0:T(8,128)(2,1)S(1)} %copy-done.10), channel_id=1, source_target_pairs={{0,16},{1,17},{2,18},{3,19},{4,20},{5,21},{6,22},{7,23},{8,24},{9,... | collective-permute-start | bytes 14155784 | tf_op jit(solution)/shard_map/ppermute | solution.py:44
  20.5 19.5 %collective-permute-start.5 = (bf16[128,3072]{1,0:T(8,128)(2,1)S(1)}, bf16[128,3072]{1,0:T(8,128)(2,1)S(1)}, u32[]{:S(2)}, u32[]{:S(2)}) collective-permute-start(bf16[128,3072]{1,0:T(8,128)(2,1)S(1)} %pad_maximum_fusion.p0), channel_id=1, source_target_pairs={{0,3},{1,0},{2,1},{3,2},{4,7},{5,4},{6,5},{7,6},{8,11},{9,8},{10,9... | collective-permute-start | bytes 2359304 | tf_op jit(solution)/shard_map/ppermute | solution.py:44
  22.6 23.9 %collective-permute-start.8 = (bf16[128,3072]{1,0:T(8,128)(2,1)S(1)}, bf16[128,3072]{1,0:T(8,128)(2,1)}, u32[]{:S(2)}, u32[]{:S(2)}) collective-permute-start(bf16[128,3072]{1,0:T(8,128)(2,1)S(1)} %pad_maximum_fusion.p0), channel_id=1, source_target_pairs={{0,1},{1,2},{2,3},{3,0},{4,5},{5,6},{6,7},{7,4},{8,9},{9,10},{10,1... | collective-permute-start | bytes 2359304 | tf_op jit(solution)/shard_map/ppermute | solution.py:44
  22.6 23.9 %collective-permute-start.7 = (bf16[128,3072]{1,0:T(8,128)(2,1)S(1)}, bf16[128,3072]{1,0:T(8,128)(2,1)}, u32[]{:S(2)}, u32[]{:S(2)}) collective-permute-start(bf16[128,3072]{1,0:T(8,128)(2,1)S(1)} %pad_maximum_fusion.p0), channel_id=1, source_target_pairs={{0,2},{1,3},{2,0},{3,1},{4,6},{5,7},{6,4},{7,5},{8,10},{9,11},{10,... | collective-permute-start | bytes 2359304 | tf_op jit(solution)/shard_map/ppermute | solution.py:44
  40.0 5.9 %copy-start.2 = (bf16[128,3072]{1,0:T(8,128)(2,1)}, bf16[128,3072]{1,0:T(8,128)(2,1)S(1)}, u32[]{:S(2)}) copy-start(bf16[128,3072]{1,0:T(8,128)(2,1)S(1)} %collective-permute-done.5.after.p1) | copy-start | bytes 2359300
  40.0 6.5 %copy-start.1 = (bf16[128,3072]{1,0:T(8,128)(2,1)}, bf16[128,3072]{1,0:T(8,128)(2,1)S(1)}, u32[]{:S(2)}) copy-start(bf16[128,3072]{1,0:T(8,128)(2,1)S(1)} %shard_map.75.after.p0) | copy-start | bytes 2359300
  40.1 2.3 %copy-start.12 = (bf16[1536,1536]{1,0:T(8,128)(2,1)}, bf16[1536,1536]{1,0:T(8,128)(2,1)S(1)}, u32[]{:S(2)}) copy-start(bf16[1536,1536]{1,0:T(8,128)(2,1)S(1)} %collective-permute-done.6.w_other) | copy-start | bytes 14155780
  40.1 18.0 %collective-permute-start.10 = (bf16[128,3072]{1,0:T(8,128)(2,1)S(1)}, bf16[128,3072]{1,0:T(8,128)(2,1)}, u32[]{:S(2)}, u32[]{:S(2)}) collective-permute-start(bf16[128,3072]{1,0:T(8,128)(2,1)S(1)} %shard_map.75.after.p0), channel_id=1, source_target_pairs={{0,1},{1,2},{2,3},{3,0},{4,5},{5,6},{6,7},{7,4},{8,9},{9,10},{10,1... | collective-permute-start | bytes 2359304 | tf_op jit(solution)/shard_map/ppermute | solution.py:44
  42.3 15.8 %collective-permute-start.9 = (bf16[128,3072]{1,0:T(8,128)(2,1)S(1)}, bf16[128,3072]{1,0:T(8,128)(2,1)}, u32[]{:S(2)}, u32[]{:S(2)}) collective-permute-start(bf16[128,3072]{1,0:T(8,128)(2,1)S(1)} %shard_map.75.after.p0), channel_id=1, source_target_pairs={{0,3},{1,0},{2,1},{3,2},{4,7},{5,4},{6,5},{7,6},{8,11},{9,8},{10,9... | collective-permute-start | bytes 2359304 | tf_op jit(solution)/shard_map/ppermute | solution.py:44
  56.4 17.2 %collective-permute-start.13 = (bf16[512,1536]{1,0:T(8,128)(2,1)}, bf16[512,1536]{1,0:T(8,128)(2,1)}, u32[]{:S(2)}, u32[]{:S(2)}) collective-permute-start(bf16[512,1536]{1,0:T(8,128)(2,1)} %get-tuple-element.69), channel_id=1, source_target_pairs={{0,16},{1,17},{2,18},{3,19},{4,20},{5,21},{6,22},{7,23},{8,24},{9,... | collective-permute-start | bytes 4718600 | tf_op jit(solution)/shard_map/ppermute | solution.py:44
  58.1 13.7 %collective-permute-start.12 = (bf16[256,1536]{1,0:T(8,128)(2,1)}, bf16[256,1536]{1,0:T(8,128)(2,1)S(1)}, u32[]{:S(2)}, u32[]{:S(2)}) collective-permute-start(bf16[256,1536]{1,0:T(8,128)(2,1)} %get-tuple-element.67), channel_id=1, source_target_pairs={{0,32},{1,33},{2,34},{3,35},{4,36},{5,37},{6,38},{7,39},{8,40},{9,... | collective-permute-start | bytes 2359304 | tf_op jit(solution)/shard_map/ppermute | solution.py:44
  61.8 12.7 %collective-permute-start.11 = (bf16[128,3072]{1,0:T(8,128)(2,1)}, bf16[128,3072]{1,0:T(8,128)(2,1)}, u32[]{:S(2)}, u32[]{:S(2)}) collective-permute-start(bf16[128,3072]{1,0:T(8,128)(2,1)} %copy-done.1), channel_id=1, source_target_pairs={{0,2},{1,3},{2,0},{3,1},{4,6},{5,7},{6,4},{7,5},{8,10},{9,11},{10,... | collective-permute-start | bytes 2359304 | tf_op jit(solution)/shard_map/ppermute | solution.py:44
  73.5 1.0 copy-start.9
  73.6 12.6 %collective-permute-start.14 = (bf16[128,1536]{1,0:T(8,128)(2,1)S(1)}, bf16[128,1536]{1,0:T(8,128)(2,1)S(1)}, u32[]{:S(2)}, u32[]{:S(2)}) collective-permute-start(bf16[128,1536]{1,0:T(8,128)(2,1)S(1)} %slice.72.after), channel_id=1, source_target_pairs={{0,96},{1,97},{2,98},{3,99},{4,100},{5,101},{6,102},{7,103},{8,104... | collective-permute-start | bytes 1179656 | tf_op jit(solution)/shard_map/ppermute | solution.py:44
  84.4 18.6 %collective-permute-start.17 = (bf16[512,1536]{1,0:T(8,128)(2,1)}, bf16[512,1536]{1,0:T(8,128)(2,1)S(1)}, u32[]{:S(2)}, u32[]{:S(2)}) collective-permute-start(bf16[512,1536]{1,0:T(8,128)(2,1)} %get-tuple-element.80), channel_id=1, source_target_pairs={{0,16},{1,17},{2,18},{3,19},{4,20},{5,21},{6,22},{7,23},{8,24},{9,... | collective-permute-start | bytes 4718600 | tf_op jit(solution)/shard_map/ppermute | solution.py:44
  86.2 16.5 %copy-start.4 = (f32[256,1536]{1,0:T(8,128)S(1)}, f32[256,1536]{1,0:T(8,128)}, u32[]{:S(2)}) copy-start(f32[256,1536]{1,0:T(8,128)} %get-tuple-element.71) | copy-start | bytes 4718596
  86.2 16.5 %collective-permute-start.15 = (bf16[256,1536]{1,0:T(8,128)(2,1)}, bf16[256,1536]{1,0:T(8,128)(2,1)S(1)}, u32[]{:S(2)}, u32[]{:S(2)}) collective-permute-start(bf16[256,1536]{1,0:T(8,128)(2,1)} %get-tuple-element.73), channel_id=1, source_target_pairs={{0,32},{1,33},{2,34},{3,35},{4,36},{5,37},{6,38},{7,39},{8,40},{9,... | collective-permute-start | bytes 2359304 | tf_op jit(solution)/shard_map/ppermute | solution.py:44
  87.2 11.1 %collective-permute-start.16 = (bf16[128,1536]{1,0:T(8,128)(2,1)S(1)}, bf16[128,1536]{1,0:T(8,128)(2,1)S(1)}, u32[]{:S(2)}, u32[]{:S(2)}) collective-permute-start(bf16[128,1536]{1,0:T(8,128)(2,1)S(1)} %get-tuple-element.76), channel_id=1, source_target_pairs={{0,96},{1,97},{2,98},{3,99},{4,100},{5,101},{6,102},{7,103},{8,104... | collective-permute-start | bytes 1179656 | tf_op jit(solution)/shard_map/ppermute | solution.py:44
  98.4 12.2 %copy-start.6 = (bf16[256,1536]{1,0:T(8,128)(2,1)}, bf16[256,1536]{1,0:T(8,128)(2,1)S(1)}, u32[]{:S(2)}) copy-start(bf16[256,1536]{1,0:T(8,128)(2,1)S(1)} %pad_maximum_fusion.1.near) | copy-start | bytes 2359300
  103.0 14.9 %copy-start.13 = (bf16[512,1536]{1,0:T(8,128)(2,1)}, bf16[512,1536]{1,0:T(8,128)(2,1)S(1)}, u32[]{:S(2)}) copy-start(bf16[512,1536]{1,0:T(8,128)(2,1)S(1)} %collective-permute-done.17.r_other) | copy-start | bytes 4718596
  103.0 7.0 %collective-permute-start.18 = (bf16[128,1536]{1,0:T(8,128)(2,1)S(1)}, bf16[128,1536]{1,0:T(8,128)(2,1)S(1)}, u32[]{:S(2)}, u32[]{:S(2)}) collective-permute-start(bf16[128,1536]{1,0:T(8,128)(2,1)S(1)} %slice.71), channel_id=1, source_target_pairs={{0,96},{1,97},{2,98},{3,99},{4,100},{5,101},{6,102},{7,103},{8,104... | collective-permute-start | bytes 1179656 | tf_op jit(solution)/shard_map/ppermute | solution.py:44
  110.6 7.2 %collective-permute-start.19 = (bf16[128,1536]{1,0:T(8,128)(2,1)S(1)}, bf16[128,1536]{1,0:T(8,128)(2,1)S(1)}, u32[]{:S(2)}, u32[]{:S(2)}) collective-permute-start(bf16[128,1536]{1,0:T(8,128)(2,1)S(1)} %fusion.6), channel_id=1, source_target_pairs={{0,96},{1,97},{2,98},{3,99},{4,100},{5,101},{6,102},{7,103},{8,104... | collective-permute-start | bytes 1179656 | tf_op jit(solution)/shard_map/ppermute | solution.py:44
  110.7 16.3 %collective-permute-start.21 = (bf16[256,1536]{1,0:T(8,128)(2,1)S(1)}, bf16[256,1536]{1,0:T(8,128)(2,1)S(1)}, u32[]{:S(2)}, u32[]{:S(2)}) collective-permute-start(bf16[256,1536]{1,0:T(8,128)(2,1)S(1)} %pad_maximum_fusion.1.near), channel_id=1, source_target_pairs={{0,32},{1,33},{2,34},{3,35},{4,36},{5,37},{6,38},{7,39},{8,40},{9,... | collective-permute-start | bytes 2359304 | tf_op jit(solution)/shard_map/ppermute | solution.py:44
  117.9 9.2 %copy-start.7 = (bf16[256,1536]{1,0:T(8,128)(2,1)}, bf16[256,1536]{1,0:T(8,128)(2,1)S(1)}, u32[]{:S(2)}) copy-start(bf16[256,1536]{1,0:T(8,128)(2,1)S(1)} %pad_maximum_fusion.2.after.near) | copy-start | bytes 2359300
  117.9 26.1 %collective-permute-start.20 = (bf16[256,1536]{1,0:T(8,128)(2,1)S(1)}, bf16[256,1536]{1,0:T(8,128)(2,1)}, u32[]{:S(2)}, u32[]{:S(2)}) collective-permute-start(bf16[256,1536]{1,0:T(8,128)(2,1)S(1)} %pad_maximum_fusion.2.after.near), channel_id=1, source_target_pairs={{0,32},{1,33},{2,34},{3,35},{4,36},{5,37},{6,38},{7,39},{8,40},{9,... | collective-permute-start | bytes 2359304 | tf_op jit(solution)/shard_map/ppermute | solution.py:44
  127.0 0.9 copy-start.14
  139.2 16.9 %collective-permute-start.25 = (bf16[128,3072]{1,0:T(8,128)(2,1)}, bf16[128,3072]{1,0:T(8,128)(2,1)}, u32[]{:S(2)}, u32[]{:S(2)}) collective-permute-start(bf16[128,3072]{1,0:T(8,128)(2,1)} %get-tuple-element.91), channel_id=1, source_target_pairs={{0,1},{1,2},{2,3},{3,0},{4,5},{5,6},{6,7},{7,4},{8,9},{9,10},{10,1... | collective-permute-start | bytes 2359304 | tf_op jit(solution)/shard_map/ppermute | solution.py:44
  140.8 20.2 %collective-permute-start.26 = (bf16[128,3072]{1,0:T(8,128)(2,1)}, bf16[128,3072]{1,0:T(8,128)(2,1)}, u32[]{:S(2)}, u32[]{:S(2)}) collective-permute-start(bf16[128,3072]{1,0:T(8,128)(2,1)} %get-tuple-element.92), channel_id=1, source_target_pairs={{0,2},{1,3},{2,0},{3,1},{4,6},{5,7},{6,4},{7,5},{8,10},{9,11},{10,... | collective-permute-start | bytes 2359304 | tf_op jit(solution)/shard_map/ppermute | solution.py:44
  142.7 19.6 %collective-permute-start.27 = (bf16[128,3072]{1,0:T(8,128)(2,1)}, bf16[128,3072]{1,0:T(8,128)(2,1)}, u32[]{:S(2)}, u32[]{:S(2)}) collective-permute-start(bf16[128,3072]{1,0:T(8,128)(2,1)} %get-tuple-element.93), channel_id=1, source_target_pairs={{0,3},{1,0},{2,1},{3,2},{4,7},{5,4},{6,5},{7,6},{8,11},{9,8},{10,9... | collective-permute-start | bytes 2359304 | tf_op jit(solution)/shard_map/ppermute | solution.py:44
  144.0 19.4 %copy-start.8 = (bf16[128,3072]{1,0:T(8,128)(2,1)S(1)}, bf16[128,3072]{1,0:T(8,128)(2,1)}, u32[]{:S(2)}) copy-start(bf16[128,3072]{1,0:T(8,128)(2,1)} %get-tuple-element.90) | copy-start | bytes 2359300
  144.0 22.3 %collective-permute-start.29 = (bf16[512,1536]{1,0:T(8,128)(2,1)}, bf16[512,1536]{1,0:T(8,128)(2,1)}, u32[]{:S(2)}, u32[]{:S(2)}) collective-permute-start(bf16[512,1536]{1,0:T(8,128)(2,1)} %get-tuple-element.85.after.l_own), channel_id=1, source_target_pairs={{0,16},{1,17},{2,18},{3,19},{4,20},{5,21},{6,22},{7,23},{8,24},{9,... | collective-permute-start | bytes 4718600 | tf_op jit(solution)/shard_map/ppermute | solution.py:44
  155.5 19.8 %collective-permute-start.28 = (bf16[512,1536]{1,0:T(8,128)(2,1)}, bf16[512,1536]{1,0:T(8,128)(2,1)}, u32[]{:S(2)}, u32[]{:S(2)}) collective-permute-start(bf16[512,1536]{1,0:T(8,128)(2,1)} %get-tuple-element.95.r_own), channel_id=1, source_target_pairs={{0,16},{1,17},{2,18},{3,19},{4,20},{5,21},{6,22},{7,23},{8,24},{9,... | collective-permute-start | bytes 4718600 | tf_op jit(solution)/shard_map/ppermute | solution.py:44
  156.0 28.2 %collective-permute-start.22 = (bf16[128,3072]{1,0:T(8,128)(2,1)}, bf16[128,3072]{1,0:T(8,128)(2,1)}, u32[]{:S(2)}, u32[]{:S(2)}) collective-permute-start(bf16[128,3072]{1,0:T(8,128)(2,1)} %get-tuple-element.87), channel_id=1, source_target_pairs={{0,1},{1,2},{2,3},{3,0},{4,5},{5,6},{6,7},{7,4},{8,9},{9,10},{10,1... | collective-permute-start | bytes 2359304 | tf_op jit(solution)/shard_map/ppermute | solution.py:44
  161.1 23.2 %collective-permute-start.23 = (bf16[128,3072]{1,0:T(8,128)(2,1)}, bf16[128,3072]{1,0:T(8,128)(2,1)}, u32[]{:S(2)}, u32[]{:S(2)}) collective-permute-start(bf16[128,3072]{1,0:T(8,128)(2,1)} %get-tuple-element.88), channel_id=1, source_target_pairs={{0,2},{1,3},{2,0},{3,1},{4,6},{5,7},{6,4},{7,5},{8,10},{9,11},{10,... | collective-permute-start | bytes 2359304 | tf_op jit(solution)/shard_map/ppermute | solution.py:44
  162.2 22.0 %collective-permute-start.24 = (bf16[128,3072]{1,0:T(8,128)(2,1)}, bf16[128,3072]{1,0:T(8,128)(2,1)}, u32[]{:S(2)}, u32[]{:S(2)}) collective-permute-start(bf16[128,3072]{1,0:T(8,128)(2,1)} %get-tuple-element.89), channel_id=1, source_target_pairs={{0,3},{1,0},{2,1},{3,2},{4,7},{5,4},{6,5},{7,6},{8,11},{9,8},{10,9... | collective-permute-start | bytes 2359304 | tf_op jit(solution)/shard_map/ppermute | solution.py:44
  175.2 9.0 %copy-start = (bf16[128,3072]{1,0:T(8,128)(2,1)S(1)}, bf16[128,3072]{1,0:T(8,128)(2,1)}, u32[]{:S(2)}) copy-start(bf16[128,3072]{1,0:T(8,128)(2,1)} %add_convert_fusion.after.first) | copy-start | bytes 2359300
  175.2 9.1 %copy-start.3 = (bf16[128,3072]{1,0:T(8,128)(2,1)S(1)}, bf16[128,3072]{1,0:T(8,128)(2,1)}, u32[]{:S(2)}) copy-start(bf16[128,3072]{1,0:T(8,128)(2,1)} %get-tuple-element.98.p0) | copy-start | bytes 2359300
  187.0 8.2 %collective-permute-start.30 = (bf16[64,3072]{1,0:T(8,128)(2,1)S(1)}, bf16[64,3072]{1,0:T(8,128)(2,1)S(1)}, u32[]{:S(2)}, u32[]{:S(2)}) collective-permute-start(bf16[64,3072]{1,0:T(8,128)(2,1)S(1)} %get-tuple-element.104), channel_id=1, source_target_pairs={{0,4},{1,5},{2,6},{3,7},{4,8},{5,9},{6,10},{7,11},{8,12},{9,13},{1... | collective-permute-start | bytes 1179656 | tf_op jit(solution)/shard_map/ppermute | solution.py:44
  187.0 13.2 %collective-permute-start.31 = (bf16[64,3072]{1,0:T(8,128)(2,1)S(1)}, bf16[64,3072]{1,0:T(8,128)(2,1)S(1)}, u32[]{:S(2)}, u32[]{:S(2)}) collective-permute-start(bf16[64,3072]{1,0:T(8,128)(2,1)S(1)} %get-tuple-element.105), channel_id=1, source_target_pairs={{0,8},{1,9},{2,10},{3,11},{4,12},{5,13},{6,14},{7,15},{8,0},{9,1},... | collective-permute-start | bytes 1179656 | tf_op jit(solution)/shard_map/ppermute | solution.py:44
  190.6 9.7 %collective-permute-start.32 = (bf16[64,3072]{1,0:T(8,128)(2,1)S(1)}, bf16[64,3072]{1,0:T(8,128)(2,1)S(1)}, u32[]{:S(2)}, u32[]{:S(2)}) collective-permute-start(bf16[64,3072]{1,0:T(8,128)(2,1)S(1)} %get-tuple-element.106), channel_id=1, source_target_pairs={{0,12},{1,13},{2,14},{3,15},{4,0},{5,1},{6,2},{7,3},{8,4},{9,5},{1... | collective-permute-start | bytes 1179656 | tf_op jit(solution)/shard_map/ppermute | solution.py:44
  200.4 3.4 %collective-permute-start.33 = (bf16[64,1536]{1,0:T(8,128)(2,1)S(1)}, bf16[64,1536]{1,0:T(8,128)(2,1)S(1)}, u32[]{:S(2)}, u32[]{:S(2)}) collective-permute-start(bf16[64,1536]{1,0:T(8,128)(2,1)S(1)} %slice.65), channel_id=1, source_target_pairs={{0,16},{1,17},{2,18},{3,19},{4,20},{5,21},{6,22},{7,23},{8,24},{9,... | collective-permute-start | bytes 589832 | tf_op jit(solution)/shard_map/ppermute | solution.py:44

commit v3 on v2

--- a/solution.py
+++ b/solution.py
@@ -14,7 +14,7 @@
 NEAR = (3, 1)
 RING = 4
 TILE = 512
-LIMIT = 62 * 1024 * 1024
+LIMIT = 30 * 1024 * 1024
 SMALL = 16 * 1024 * 1024
 ANYWHERE = pl.BlockSpec(memory_space=pl.ANY)
 
@@ -68,12 +68,21 @@
     return lax.dot_general(left, right, (((1,), (1 if transposed else 0,)), ((), ())), preferred_element_type=F32)
 
 
-def up_kernel(transposed, place, p0, p1, p2, p3, w_own, w_other, after, keep, give, own, other, scratch):
+def up_kernel(transposed, place, p0, p1, p2, p3, w_own, w_other, after, keep, give, own, other, scratch, tiles, sems):
     rows = p0.shape[0]
     depth = own.shape[1]
-
-    @pl.when(pl.program_id(0) == 0)
+    step = pl.program_id(0)
+
+    def fetch(index):
+        width = scratch.shape[1]
+        part = pl.ds(pl.multiple_of(index * width, width), width)
+        source = w_own.at[part, :] if transposed else w_own.at[:, part]
+        return pltpu.make_async_copy(source, tiles.at[index], sems.at[index])
+
+    @pl.when(step == 0)
     def _():
+        for index in range(tiles.shape[0]):
+            fetch(index).start()
         start = 0
         for piece in (p0, p1, p2, p3):
             stop = start + piece.shape[0]
@@ -81,8 +90,9 @@
             other[start:stop, :] = piece[:, depth:]
             start = stop
 
-    total = dot(own[...], w_own[...], transposed) + dot(other[...], w_other[...], transposed)
-    scratch[...] = total
+    total = dot(other[...], w_other[...], transposed)
+    fetch(step).wait()
+    scratch[...] = total + dot(own[...], tiles[step], transposed)
     for index in range(RING):
         part = scratch[pl.ds(pl.multiple_of(place[index] * rows, rows), rows), :]
         if index < 2:
@@ -105,11 +115,15 @@
     outs = pl.pallas_call(
         functools.partial(up_kernel, transposed),
         grid=(columns // tile,),
-        in_specs=[pl.BlockSpec(memory_space=pltpu.SMEM)] + whole + [weight] * 2 + [ANYWHERE],
+        in_specs=[pl.BlockSpec(memory_space=pltpu.SMEM)] + whole + [pl.BlockSpec(memory_space=pltpu.HBM), weight, ANYWHERE],
         out_specs=[pl.BlockSpec((2 * rows, tile), lambda n: (0, n))] * 2 + [kept] * 2,
         out_shape=[jax.ShapeDtypeStruct((2 * rows, columns), dtype) for dtype in (F32, BF16)]
         + [jax.ShapeDtypeStruct((RING * rows, depth), BF16)] * 2,
-        scratch_shapes=[pltpu.VMEM((RING * rows, tile), F32)],
+        scratch_shapes=[
+            pltpu.VMEM((RING * rows, tile), F32),
+            pltpu.VMEM((columns // tile, tile, depth) if transposed else (columns // tile, depth, tile), BF16),
+            pltpu.SemaphoreType.DMA((columns // tile,)),
+        ],
         compiler_params=pltpu.CompilerParams(vmem_limit_bytes=LIMIT),
         cost_estimate=cost(RING * rows, width, columns, 2 * (width * columns + 2 * RING * rows * width)),
     )(place, *pieces, w_own, w_other, after)
@@ -277,12 +291,10 @@
     w_in_other = swap(w_in_late)
 
     parts = gather_ring(chip, "first")
-    input_block, w_out_late, w_in_other = together(
-        jnp.concatenate([part[:half] for part in parts]), w_out, w_in_other
-    )
+    input_block, w_out_late = together(jnp.concatenate([part[:half] for part in parts]), w_out)
     w_out_other = swap(w_out_late)
     input_pieces = gather_ring(input_block, "second")
-    cotangent_block, w_out_other = together(join(parts, input_pieces[1]), w_out_other)
+    cotangent_block = join(parts, input_pieces[1])
     cotangent_pieces = gather_ring(cotangent_block, "second")
 
     keep, give, input_own, input_sent = project_up(place, input_pieces, w_in, w_in_other, False, cotangent_block)
@@ -318,7 +330,8 @@
     input_blocks = exchange(input_parts, "second")
     output_sum = total_of(output_blocks).astype(BF16)
     grad_w_out = weight_grad(activated_own, activated_got, cotangent_own, cotangent_got, output_sum)
-    grad_w_in = weight_grad(input_own, input_got, grad_hidden_own, swap(grad_hidden_own), grad_w_out)
+    grad_hidden_got, grad_w_out = together(swap(grad_hidden_own), grad_w_out)
+    grad_w_in = weight_grad(input_own, input_got, grad_hidden_own, grad_hidden_got, place)
     *input_blocks, output_sum, grad_w_in = together(*input_blocks, output_sum, grad_w_in)
     both = scatter_ring(add_parts(input_blocks, output_sum), "first").astype(BF16)
     kept, got = both[:, :width], swap(both[:, width:])

time: 205 us -> 191 us (0.932)
  Pallas kernels: 63.2 us -> 50.5 us
  other arithmetic: 7.54 us -> 3.07 us
  waiting for transfers between devices: 85.1 us -> 88.8 us
    pallas_call x2, Pallas kernels: 22.8 us -> 17.7 us  [project_down(): pl.pallas_call(functools.partial(down_kernel, transposed), grid=(2 * half...]
    pallas_call x2, Pallas kernels: 17.9 us -> 13.9 us  [weight_grad(): pl.pallas_call(weight_kernel, grid=(rows // tile,), in_specs=[left, left,...]
    ppermute x34, waiting for transfers between devices: 85.1 us -> 88.8 us  [send(): return lax.ppermute(block, AXES, permutation(**where))]
    convert_element_type x1, other arithmetic: 2.98 us -> 0.49 us  [local(): output_sum = total_of(output_blocks).astype(BF16)]
    unnamed x30 -> x14, local copies, waits for them, and re-layouts: 3.09 us -> 4.37 us
  transfers between devices with their start and end apart: 34 -> 34, of which waited for: 15 -> 18; matrix products, arithmetic and copies ran while one was open for 3% -> 1% of each run, Pallas kernels for 30% -> 26%
where the time goes in v3:
time: 191 us
  waiting for transfers between devices  88.8 us (46%)
  Pallas kernels  50.5 us (26%)
  starting transfers between devices  40.7 us (21%)
  local copies, waits for them, and re-layouts  6.58 us (3%)
  other arithmetic  3.07 us (2%)
    ppermute x34, waiting for transfers between devices, send(): return lax.ppermute(block, AXES, permutation(**where))  88.8 us
    ppermute x34, starting transfers between devices, send(): return lax.ppermute(block, AXES, permutation(**where))  40.7 us
    pallas_call x2, Pallas kernels, project_up(): pl.pallas_call(functools.partial(up_kernel, transposed), grid=(columns //...  18 us
    pallas_call x2, Pallas kernels, project_down(): pl.pallas_call(functools.partial(down_kernel, transposed), grid=(2 * half...  17.7 us
    pallas_call x2, Pallas kernels, weight_grad(): pl.pallas_call(weight_kernel, grid=(rows // tile,), in_specs=[left, left,...  13.9 us
    unnamed x14, local copies, waits for them, and re-layouts  4.37 us
  transfers between devices with their start and end apart: 34, of which 18 were waited for; matrix products, arithmetic and copies ran while one was open for 1% of the time, Pallas kernels for 26%

profile of v3, /device:TPU:1, one launch (start us, length us, event | category | flops | bytes accessed | tf_op | source)
XLA Modules:
  0.0 190.6 jit_solution(9955419309712076018)
XLA Ops:
  0.6 1.0 constant_dynamic-slice_fusion.3
  1.6 1.0 constant_dynamic-slice_fusion.2
  2.6 1.5 collective-permute-start
  4.1 1.1 collective-permute-done
  5.2 0.5 collective-permute-start.7
  5.6 1.4 collective-permute-start.3
  7.0 2.6 %collective-permute-start.2 = (bf16[64,3072]{1,0:T(8,128)(2,1)S(1)}, bf16[64,3072]{1,0:T(8,128)(2,1)S(1)}, u32[]{:S(2)}, u32[]{:S(2)}) collective-permute-start(bf16[64,3072]{1,0:T(8,128)(2,1)S(1)} %pad_maximum_fusion.3.p0), channel_id=1, source_target_pairs={{0,8},{1,9},{2,10},{3,11},{4,12},{5,13},{6,14},{7,15},{8,0},{9,1},... | collective-permute-start | bytes 1179656 | tf_op jit(solution)/shard_map/ppermute | solution.py:44
  9.6 1.1 collective-permute-start.1
  10.7 3.2 %collective-permute-done.3.p3 = bf16[64,3072]{1,0:T(8,128)(2,1)S(1)} collective-permute-done((bf16[64,3072]{1,0:T(8,128)(2,1)S(1)}, bf16[64,3072]{1,0:T(8,128)(2,1)S(1)}, u32[]{:S(2)}, u32[]{:S(2)}) %collective-permute-start.3) | collective-permute-done | bytes 393248 | tf_op jit(solution)/shard_map/ppermute | solution.py:44
  13.9 5.4 %collective-permute-done.2.p2 = bf16[64,3072]{1,0:T(8,128)(2,1)S(1)} collective-permute-done((bf16[64,3072]{1,0:T(8,128)(2,1)S(1)}, bf16[64,3072]{1,0:T(8,128)(2,1)S(1)}, u32[]{:S(2)}, u32[]{:S(2)}) %collective-permute-start.2) | collective-permute-done | bytes 393248 | tf_op jit(solution)/shard_map/ppermute | solution.py:44
  19.4 0.8 collective-permute-start.11
  20.2 2.1 %collective-permute-start.4 = (bf16[128,3072]{1,0:T(8,128)(2,1)S(1)}, bf16[128,3072]{1,0:T(8,128)(2,1)S(1)}, u32[]{:S(2)}, u32[]{:S(2)}) collective-permute-start(bf16[128,3072]{1,0:T(8,128)(2,1)S(1)} %pad_maximum_fusion.p0), channel_id=1, source_target_pairs={{0,3},{1,0},{2,1},{3,2},{4,7},{5,4},{6,5},{7,6},{8,11},{9,8},{10,9... | collective-permute-start | bytes 2359304 | tf_op jit(solution)/shard_map/ppermute | solution.py:44
  22.4 1.9 %collective-permute-start.5 = (bf16[128,3072]{1,0:T(8,128)(2,1)S(1)}, bf16[128,3072]{1,0:T(8,128)(2,1)}, u32[]{:S(2)}, u32[]{:S(2)}) collective-permute-start(bf16[128,3072]{1,0:T(8,128)(2,1)S(1)} %pad_maximum_fusion.p0), channel_id=1, source_target_pairs={{0,2},{1,3},{2,0},{3,1},{4,6},{5,7},{6,4},{7,5},{8,10},{9,11},{10,... | collective-permute-start | bytes 2359304 | tf_op jit(solution)/shard_map/ppermute | solution.py:44
  24.3 15.4 %collective-permute-done.4.after.p1 = bf16[128,3072]{1,0:T(8,128)(2,1)S(1)} collective-permute-done((bf16[128,3072]{1,0:T(8,128)(2,1)S(1)}, bf16[128,3072]{1,0:T(8,128)(2,1)S(1)}, u32[]{:S(2)}, u32[]{:S(2)}) %collective-permute-start.4) | collective-permute-done | bytes 786464 | tf_op jit(solution)/shard_map/ppermute | solution.py:44
  39.9 3.4 %collective-permute-done.6.p3 = bf16[128,3072]{1,0:T(8,128)(2,1)S(1)} collective-permute-done((bf16[128,3072]{1,0:T(8,128)(2,1)S(1)}, bf16[128,3072]{1,0:T(8,128)(2,1)S(1)}, u32[]{:S(2)}, u32[]{:S(2)}) %collective-permute-start.6) | collective-permute-done | bytes 786464 | tf_op jit(solution)/shard_map/ppermute | solution.py:44
  43.3 0.9 copy-done.1
  44.2 0.2 collective-permute-start.8
  44.4 2.3 %copy-done = bf16[1536,1536]{1,0:T(8,128)(2,1)S(1)} copy-done((bf16[1536,1536]{1,0:T(8,128)(2,1)S(1)}, bf16[1536,1536]{1,0:T(8,128)(2,1)}, u32[]{:S(2)}) %copy-start) | copy-done | bytes 4718616
  46.7 1.1 copy-done.2
  47.9 8.6 %shard_map.76 = (f32[256,1536]{1,0:T(8,128)S(1)}, bf16[256,1536]{1,0:T(8,128)(2,1)S(1)}, bf16[512,1536]{1,0:T(8,128)(2,1)S(1)}, bf16[512,1536]{1,0:T(8,128)(2,1)S(1)}) custom-call(s32[4]{0:T(128)S(1)} %pad_add_fusion.place.later.after, bf16[128,3072]{1,0:T(8,128)(2,1)S(1)} %pad_maximum_fusion.p0, bf16[128,3072]{1,0:T(8,128)(2,1)S(1)} %collective-permute-done.4.after.p1, ...), custom_call_target="tpu_custom_call" | custom-call | flops 4831838208 | bytes 15728640 | tf_op jit(solution)/shard_map/pallas_call | solution.py:115
  56.4 1.8 collective-permute-start.13
  58.2 3.8 %collective-permute-start.12 = (bf16[256,1536]{1,0:T(8,128)(2,1)S(1)}, bf16[256,1536]{1,0:T(8,128)(2,1)S(1)}, u32[]{:S(2)}, u32[]{:S(2)}) collective-permute-start(bf16[256,1536]{1,0:T(8,128)(2,1)S(1)} %get-tuple-element.63), channel_id=1, source_target_pairs={{0,32},{1,33},{2,34},{3,35},{4,36},{5,37},{6,38},{7,39},{8,40},{9,... | collective-permute-start | bytes 2359304 | tf_op jit(solution)/shard_map/ppermute | solution.py:44
  62.0 2.6 %collective-permute-start.10 = (bf16[128,3072]{1,0:T(8,128)(2,1)S(1)}, bf16[128,3072]{1,0:T(8,128)(2,1)S(1)}, u32[]{:S(2)}, u32[]{:S(2)}) collective-permute-start(bf16[128,3072]{1,0:T(8,128)(2,1)S(1)} %shard_map.75.after.p0), channel_id=1, source_target_pairs={{0,2},{1,3},{2,0},{3,1},{4,6},{5,7},{6,4},{7,5},{8,10},{9,11},{10,... | collective-permute-start | bytes 2359304 | tf_op jit(solution)/shard_map/ppermute | solution.py:44
  64.6 7.0 %collective-permute-done.12 = bf16[256,1536]{1,0:T(8,128)(2,1)S(1)} collective-permute-done((bf16[256,1536]{1,0:T(8,128)(2,1)S(1)}, bf16[256,1536]{1,0:T(8,128)(2,1)S(1)}, u32[]{:S(2)}, u32[]{:S(2)}) %collective-permute-start.12) | collective-permute-done | bytes 786464 | tf_op jit(solution)/shard_map/ppermute | solution.py:44
  71.7 0.2 convert_add_fusion.1
  72.1 2.3 %collective-permute-done.10.p2 = bf16[128,3072]{1,0:T(8,128)(2,1)S(1)} collective-permute-done((bf16[128,3072]{1,0:T(8,128)(2,1)S(1)}, bf16[128,3072]{1,0:T(8,128)(2,1)S(1)}, u32[]{:S(2)}, u32[]{:S(2)}) %collective-permute-start.10) | collective-permute-done | bytes 786464 | tf_op jit(solution)/shard_map/ppermute | solution.py:44
  74.3 9.5 %shard_map.77 = (f32[256,1536]{1,0:T(8,128)S(1)}, bf16[256,1536]{1,0:T(8,128)(2,1)S(1)}, bf16[512,1536]{1,0:T(8,128)(2,1)S(1)}, bf16[512,1536]{1,0:T(8,128)(2,1)S(1)}) custom-call(s32[4]{0:T(128)S(1)} %pad_add_fusion.place.later.after, bf16[128,3072]{1,0:T(8,128)(2,1)S(1)} %shard_map.75.after.p0, bf16[128,3072]{1,0:T(8,128)(2,1)} %collective-permute-done.8.p1, ...), custom_call_target="tpu_custom_call" | custom-call | flops 4831838208 | bytes 15728640 | tf_op jit(solution)/shard_map/pallas_call | solution.py:115
  83.8 0.5 collective-permute-start.17
  84.3 1.2 collective-permute-start.15
  85.6 0.3 fusion.14
  85.9 0.8 collective-permute-start.16
  86.7 10.4 %collective-permute-done.16 = bf16[128,1536]{1,0:T(8,128)(2,1)S(1)} collective-permute-done((bf16[128,1536]{1,0:T(8,128)(2,1)S(1)}, bf16[128,1536]{1,0:T(8,128)(2,1)S(1)}, u32[]{:S(2)}, u32[]{:S(2)}) %collective-permute-start.16) | collective-permute-done | bytes 393248 | tf_op jit(solution)/shard_map/ppermute | solution.py:44
  97.1 3.5 %collective-permute-done.15 = bf16[256,1536]{1,0:T(8,128)(2,1)S(1)} collective-permute-done((bf16[256,1536]{1,0:T(8,128)(2,1)S(1)}, bf16[256,1536]{1,0:T(8,128)(2,1)S(1)}, u32[]{:S(2)}, u32[]{:S(2)}) %collective-permute-start.15) | collective-permute-done | bytes 786464 | tf_op jit(solution)/shard_map/ppermute | solution.py:44
  100.6 0.2 convert_add_fusion
  101.0 6.9 %collective-permute-done.18 = bf16[128,1536]{1,0:T(8,128)(2,1)S(1)} collective-permute-done((bf16[128,1536]{1,0:T(8,128)(2,1)S(1)}, bf16[128,1536]{1,0:T(8,128)(2,1)S(1)}, u32[]{:S(2)}, u32[]{:S(2)}) %collective-permute-start.18) | collective-permute-done | bytes 393248 | tf_op jit(solution)/shard_map/ppermute | solution.py:44
  107.9 0.6 fusion.6
  108.6 1.6 collective-permute-start.21
  110.3 5.4 %collective-permute-done.19 = bf16[128,1536]{1,0:T(8,128)(2,1)S(1)} collective-permute-done((bf16[128,1536]{1,0:T(8,128)(2,1)S(1)}, bf16[128,1536]{1,0:T(8,128)(2,1)S(1)}, u32[]{:S(2)}, u32[]{:S(2)}) %collective-permute-start.19) | collective-permute-done | bytes 393248 | tf_op jit(solution)/shard_map/ppermute | solution.py:44
  115.7 1.4 collective-permute-start.20
  117.1 7.9 %collective-permute-done.21.far = bf16[256,1536]{1,0:T(8,128)(2,1)S(1)} collective-permute-done((bf16[256,1536]{1,0:T(8,128)(2,1)S(1)}, bf16[256,1536]{1,0:T(8,128)(2,1)S(1)}, u32[]{:S(2)}, u32[]{:S(2)}) %collective-permute-start.21) | collective-permute-done | bytes 786464 | tf_op jit(solution)/shard_map/ppermute | solution.py:44
  125.0 9.2 %shard_map.78 = (bf16[128,3072]{1,0:T(8,128)(2,1)S(1)}, bf16[128,3072]{1,0:T(8,128)(2,1)S(1)}, bf16[128,3072]{1,0:T(8,128)(2,1)S(1)}, bf16[128,3072]{1,0:T(8,128)(2,1)S(1)}, bf16[512,1536]{1,0:T(8,128)(2,1)S(1)}) custom-call(s32[4]{0:T(128)S(1)} %pad_add_fusion.place.later.after, bf16[256,1536]{1,0:T(8,128)(2,1)S(1)} %pad_maximum_fusion.1.near, ...), custom_call_target="tpu_custom_call" | custom-call | flops 4831838208 | bytes 15728640 | tf_op jit(solution)/shard_map/pallas_call | solution.py:171
  134.2 1.7 collective-permute-start.25
  135.8 1.8 collective-permute-start.26
  137.6 1.3 collective-permute-start.27
  139.0 8.5 %shard_map.79 = (bf16[128,3072]{1,0:T(8,128)(2,1)S(1)}, bf16[128,3072]{1,0:T(8,128)(2,1)S(1)}, bf16[128,3072]{1,0:T(8,128)(2,1)S(1)}, bf16[128,3072]{1,0:T(8,128)(2,1)S(1)}, bf16[512,1536]{1,0:T(8,128)(2,1)S(1)}) custom-call(s32[4]{0:T(128)S(1)} %pad_add_fusion.place.later.after, bf16[256,1536]{1,0:T(8,128)(2,1)S(1)} %pad_maximum_fusion.2.after.near, ...), custom_call_target="tpu_custom_call" | custom-call | flops 4831838208 | bytes 15728640 | tf_op jit(solution)/shard_map/pallas_call | solution.py:171
  147.5 0.6 collective-permute-start.28
  148.1 0.7 collective-permute-start.22
  148.8 6.8 %collective-permute-done.26 = bf16[128,3072]{1,0:T(8,128)(2,1)S(1)} collective-permute-done((bf16[128,3072]{1,0:T(8,128)(2,1)S(1)}, bf16[128,3072]{1,0:T(8,128)(2,1)S(1)}, u32[]{:S(2)}, u32[]{:S(2)}) %collective-permute-start.26) | collective-permute-done | bytes 786464 | tf_op jit(solution)/shard_map/ppermute | solution.py:44
  155.6 1.4 collective-permute-start.23
  156.9 1.0 collective-permute-start.24
  158.0 0.5 add_convert_fusion.after.first
  158.5 6.9 %shard_map.80 = bf16[1536,1536]{1,0:T(8,128)(2,1)} custom-call(bf16[512,1536]{1,0:T(8,128)(2,1)S(1)} %get-tuple-element.81.after.l_own, bf16[512,1536]{1,0:T(8,128)(2,1)S(1)} %collective-permute-done.29.l_other, bf16[512,1536]{1,0:T(8,128)(2,1)S(1)} %get-tuple-element.92.r_own, bf16[512,1536]{1,0:T(8,128)(2,1)S(1)} %collective-permute-done.17.r_other, ...), custom_call_target="tpu_custom_call" | custom-call | flops 4831838208 | bytes 11010048 | tf_op jit(solution)/shard_map/pallas_call | solution.py:200
  165.4 7.0 %shard_map.81 = bf16[1536,1536]{1,0:T(8,128)(2,1)} custom-call(bf16[512,1536]{1,0:T(8,128)(2,1)S(1)} %copy-done.4, bf16[512,1536]{1,0:T(8,128)(2,1)S(1)} %collective-permute-done.13.later.l_other, bf16[512,1536]{1,0:T(8,128)(2,1)S(1)} %get-tuple-element.91.r_own, bf16[512,1536]{1,0:T(8,128)(2,1)S(1)} %collective-permute-done.28.r_other, ...), custom_call_target="tpu_custom_call" | custom-call | flops 4831838208 | bytes 11010048 | tf_op jit(solution)/shard_map/pallas_call | solution.py:200
  172.5 0.8 shard_map.82
  173.4 1.5 collective-permute-start.30
  174.8 1.5 collective-permute-start.31
  176.3 1.0 collective-permute-start.32
  177.3 4.2 %collective-permute-done.30 = bf16[64,3072]{1,0:T(8,128)(2,1)S(1)} collective-permute-done((bf16[64,3072]{1,0:T(8,128)(2,1)S(1)}, bf16[64,3072]{1,0:T(8,128)(2,1)S(1)}, u32[]{:S(2)}, u32[]{:S(2)}) %collective-permute-start.30) | collective-permute-done | bytes 393248 | tf_op jit(solution)/shard_map/ppermute | solution.py:44
  181.6 4.4 %collective-permute-done.31 = bf16[64,3072]{1,0:T(8,128)(2,1)S(1)} collective-permute-done((bf16[64,3072]{1,0:T(8,128)(2,1)S(1)}, bf16[64,3072]{1,0:T(8,128)(2,1)S(1)}, u32[]{:S(2)}, u32[]{:S(2)}) %collective-permute-start.31) | collective-permute-done | bytes 393248 | tf_op jit(solution)/shard_map/ppermute | solution.py:44
  186.0 0.4 collective-permute-done.32
  186.4 0.2 add_convert_fusion.1
  186.6 2.1 %collective-permute-start.33 = (bf16[64,1536]{1,0:T(8,128)(2,1)S(1)}, bf16[64,1536]{1,0:T(8,128)(2,1)S(1)}, u32[]{:S(2)}, u32[]{:S(2)}) collective-permute-start(bf16[64,1536]{1,0:T(8,128)(2,1)S(1)} %slice.65), channel_id=1, source_target_pairs={{0,16},{1,17},{2,18},{3,19},{4,20},{5,21},{6,22},{7,23},{8,24},{9,... | collective-permute-start | bytes 589832 | tf_op jit(solution)/shard_map/ppermute | solution.py:44
  188.7 1.1 collective-permute-done.33
  189.8 0.8 maximum_select_fusion
  (53 shorter events, 1.2 us)
Async XLA Ops:
  2.6 2.6 %collective-permute-start = (bf16[64,1536]{1,0:T(8,128)(2,1)S(1)}, bf16[64,1536]{1,0:T(8,128)(2,1)S(1)}, u32[]{:S(2)}, u32[]{:S(2)}) collective-permute-start(bf16[64,1536]{1,0:T(8,128)(2,1)S(1)} %pad_maximum_fusion.4), channel_id=1, source_target_pairs={{0,16},{1,17},{2,18},{3,19},{4,20},{5,21},{6,22},{7,23},{8,24},{9,... | collective-permute-start | bytes 589832 | tf_op jit(solution)/shard_map/ppermute | solution.py:44
  5.2 39.2 %collective-permute-start.7 = (bf16[1536,1536]{1,0:T(8,128)(2,1)}, bf16[1536,1536]{1,0:T(8,128)(2,1)}, u32[]{:S(2)}, u32[]{:S(2)}) collective-permute-start(bf16[1536,1536]{1,0:T(8,128)(2,1)} %w_own.7), channel_id=1, source_target_pairs={{0,16},{1,17},{2,18},{3,19},{4,20},{5,21},{6,22},{7,23},{8,24},{9,... | collective-permute-start | bytes 14155784 | tf_op jit(solution)/shard_map/ppermute | solution.py:44
  5.6 8.3 %collective-permute-start.3 = (bf16[64,3072]{1,0:T(8,128)(2,1)S(1)}, bf16[64,3072]{1,0:T(8,128)(2,1)S(1)}, u32[]{:S(2)}, u32[]{:S(2)}) collective-permute-start(bf16[64,3072]{1,0:T(8,128)(2,1)S(1)} %pad_maximum_fusion.3.p0), channel_id=1, source_target_pairs={{0,4},{1,5},{2,6},{3,7},{4,8},{5,9},{6,10},{7,11},{8,12},{9,13},{1... | collective-permute-start | bytes 1179656 | tf_op jit(solution)/shard_map/ppermute | solution.py:44
  7.0 12.3 %collective-permute-start.2 = (bf16[64,3072]{1,0:T(8,128)(2,1)S(1)}, bf16[64,3072]{1,0:T(8,128)(2,1)S(1)}, u32[]{:S(2)}, u32[]{:S(2)}) collective-permute-start(bf16[64,3072]{1,0:T(8,128)(2,1)S(1)} %pad_maximum_fusion.3.p0), channel_id=1, source_target_pairs={{0,8},{1,9},{2,10},{3,11},{4,12},{5,13},{6,14},{7,15},{8,0},{9,1},... | collective-permute-start | bytes 1179656 | tf_op jit(solution)/shard_map/ppermute | solution.py:44
  9.6 9.7 %collective-permute-start.1 = (bf16[64,3072]{1,0:T(8,128)(2,1)S(1)}, bf16[64,3072]{1,0:T(8,128)(2,1)S(1)}, u32[]{:S(2)}, u32[]{:S(2)}) collective-permute-start(bf16[64,3072]{1,0:T(8,128)(2,1)S(1)} %pad_maximum_fusion.3.p0), channel_id=1, source_target_pairs={{0,12},{1,13},{2,14},{3,15},{4,0},{5,1},{6,2},{7,3},{8,4},{9,5},{1... | collective-permute-start | bytes 1179656 | tf_op jit(solution)/shard_map/ppermute | solution.py:44
  19.4 54.9 %collective-permute-start.11 = (bf16[1536,1536]{1,0:T(8,128)(2,1)}, bf16[1536,1536]{1,0:T(8,128)(2,1)}, u32[]{:S(2)}, u32[]{:S(2)}) collective-permute-start(bf16[1536,1536]{1,0:T(8,128)(2,1)} %w_own.6), channel_id=1, source_target_pairs={{0,16},{1,17},{2,18},{3,19},{4,20},{5,21},{6,22},{7,23},{8,24},{9,... | collective-permute-start | bytes 14155784 | tf_op jit(solution)/shard_map/ppermute | solution.py:44
  20.2 19.5 %collective-permute-start.4 = (bf16[128,3072]{1,0:T(8,128)(2,1)S(1)}, bf16[128,3072]{1,0:T(8,128)(2,1)S(1)}, u32[]{:S(2)}, u32[]{:S(2)}) collective-permute-start(bf16[128,3072]{1,0:T(8,128)(2,1)S(1)} %pad_maximum_fusion.p0), channel_id=1, source_target_pairs={{0,3},{1,0},{2,1},{3,2},{4,7},{5,4},{6,5},{7,6},{8,11},{9,8},{10,9... | collective-permute-start | bytes 2359304 | tf_op jit(solution)/shard_map/ppermute | solution.py:44
  22.4 20.9 %collective-permute-start.6 = (bf16[128,3072]{1,0:T(8,128)(2,1)S(1)}, bf16[128,3072]{1,0:T(8,128)(2,1)S(1)}, u32[]{:S(2)}, u32[]{:S(2)}) collective-permute-start(bf16[128,3072]{1,0:T(8,128)(2,1)S(1)} %pad_maximum_fusion.p0), channel_id=1, source_target_pairs={{0,1},{1,2},{2,3},{3,0},{4,5},{5,6},{6,7},{7,4},{8,9},{9,10},{10,1... | collective-permute-start | bytes 2359304 | tf_op jit(solution)/shard_map/ppermute | solution.py:44
  22.4 22.0 %collective-permute-start.5 = (bf16[128,3072]{1,0:T(8,128)(2,1)S(1)}, bf16[128,3072]{1,0:T(8,128)(2,1)}, u32[]{:S(2)}, u32[]{:S(2)}) collective-permute-start(bf16[128,3072]{1,0:T(8,128)(2,1)S(1)} %pad_maximum_fusion.p0), channel_id=1, source_target_pairs={{0,2},{1,3},{2,0},{3,1},{4,6},{5,7},{6,4},{7,5},{8,10},{9,11},{10,... | collective-permute-start | bytes 2359304 | tf_op jit(solution)/shard_map/ppermute | solution.py:44
  39.8 18.4 %collective-permute-start.9 = (bf16[128,3072]{1,0:T(8,128)(2,1)S(1)}, bf16[128,3072]{1,0:T(8,128)(2,1)S(1)}, u32[]{:S(2)}, u32[]{:S(2)}) collective-permute-start(bf16[128,3072]{1,0:T(8,128)(2,1)S(1)} %shard_map.75.after.p0), channel_id=1, source_target_pairs={{0,1},{1,2},{2,3},{3,0},{4,5},{5,6},{6,7},{7,4},{8,9},{9,10},{10,1... | collective-permute-start | bytes 2359304 | tf_op jit(solution)/shard_map/ppermute | solution.py:44
  43.3 0.9 copy-start.1
  44.2 14.1 %collective-permute-start.8 = (bf16[128,3072]{1,0:T(8,128)(2,1)S(1)}, bf16[128,3072]{1,0:T(8,128)(2,1)}, u32[]{:S(2)}, u32[]{:S(2)}) collective-permute-start(bf16[128,3072]{1,0:T(8,128)(2,1)S(1)} %shard_map.75.after.p0), channel_id=1, source_target_pairs={{0,3},{1,0},{2,1},{3,2},{4,7},{5,4},{6,5},{7,6},{8,11},{9,8},{10,9... | collective-permute-start | bytes 2359304 | tf_op jit(solution)/shard_map/ppermute | solution.py:44
  44.4 2.3 %copy-start = (bf16[1536,1536]{1,0:T(8,128)(2,1)S(1)}, bf16[1536,1536]{1,0:T(8,128)(2,1)}, u32[]{:S(2)}) copy-start(bf16[1536,1536]{1,0:T(8,128)(2,1)} %w_own.7) | copy-start | bytes 14155780
  46.7 1.1 copy-start.2
  56.4 15.4 %copy-start.3 = (bf16[512,1536]{1,0:T(8,128)(2,1)}, bf16[512,1536]{1,0:T(8,128)(2,1)S(1)}, u32[]{:S(2)}) copy-start(bf16[512,1536]{1,0:T(8,128)(2,1)S(1)} %get-tuple-element.90.l_own) | copy-start | bytes 4718596
  56.4 15.5 %collective-permute-start.13 = (bf16[512,1536]{1,0:T(8,128)(2,1)S(1)}, bf16[512,1536]{1,0:T(8,128)(2,1)S(1)}, u32[]{:S(2)}, u32[]{:S(2)}) collective-permute-start(bf16[512,1536]{1,0:T(8,128)(2,1)S(1)} %get-tuple-element.65), channel_id=1, source_target_pairs={{0,16},{1,17},{2,18},{3,19},{4,20},{5,21},{6,22},{7,23},{8,24},{9,... | collective-permute-start | bytes 4718600 | tf_op jit(solution)/shard_map/ppermute | solution.py:44
  58.2 13.4 %collective-permute-start.12 = (bf16[256,1536]{1,0:T(8,128)(2,1)S(1)}, bf16[256,1536]{1,0:T(8,128)(2,1)S(1)}, u32[]{:S(2)}, u32[]{:S(2)}) collective-permute-start(bf16[256,1536]{1,0:T(8,128)(2,1)S(1)} %get-tuple-element.63), channel_id=1, source_target_pairs={{0,32},{1,33},{2,34},{3,35},{4,36},{5,37},{6,38},{7,39},{8,40},{9,... | collective-permute-start | bytes 2359304 | tf_op jit(solution)/shard_map/ppermute | solution.py:44
  62.0 12.3 %collective-permute-start.10 = (bf16[128,3072]{1,0:T(8,128)(2,1)S(1)}, bf16[128,3072]{1,0:T(8,128)(2,1)S(1)}, u32[]{:S(2)}, u32[]{:S(2)}) collective-permute-start(bf16[128,3072]{1,0:T(8,128)(2,1)S(1)} %shard_map.75.after.p0), channel_id=1, source_target_pairs={{0,2},{1,3},{2,0},{3,1},{4,6},{5,7},{6,4},{7,5},{8,10},{9,11},{10,... | collective-permute-start | bytes 2359304 | tf_op jit(solution)/shard_map/ppermute | solution.py:44
  72.0 12.3 %collective-permute-start.14 = (bf16[128,1536]{1,0:T(8,128)(2,1)S(1)}, bf16[128,1536]{1,0:T(8,128)(2,1)S(1)}, u32[]{:S(2)}, u32[]{:S(2)}) collective-permute-start(bf16[128,1536]{1,0:T(8,128)(2,1)S(1)} %slice.72.after), channel_id=1, source_target_pairs={{0,96},{1,97},{2,98},{3,99},{4,100},{5,101},{6,102},{7,103},{8,104... | collective-permute-start | bytes 1179656 | tf_op jit(solution)/shard_map/ppermute | solution.py:44
  83.8 17.1 %collective-permute-start.17 = (bf16[512,1536]{1,0:T(8,128)(2,1)S(1)}, bf16[512,1536]{1,0:T(8,128)(2,1)S(1)}, u32[]{:S(2)}, u32[]{:S(2)}) collective-permute-start(bf16[512,1536]{1,0:T(8,128)(2,1)S(1)} %get-tuple-element.76), channel_id=1, source_target_pairs={{0,16},{1,17},{2,18},{3,19},{4,20},{5,21},{6,22},{7,23},{8,24},{9,... | collective-permute-start | bytes 4718600 | tf_op jit(solution)/shard_map/ppermute | solution.py:44
  84.3 16.3 %collective-permute-start.15 = (bf16[256,1536]{1,0:T(8,128)(2,1)S(1)}, bf16[256,1536]{1,0:T(8,128)(2,1)S(1)}, u32[]{:S(2)}, u32[]{:S(2)}) collective-permute-start(bf16[256,1536]{1,0:T(8,128)(2,1)S(1)} %get-tuple-element.69), channel_id=1, source_target_pairs={{0,32},{1,33},{2,34},{3,35},{4,36},{5,37},{6,38},{7,39},{8,40},{9,... | collective-permute-start | bytes 2359304 | tf_op jit(solution)/shard_map/ppermute | solution.py:44
  85.9 11.2 %collective-permute-start.16 = (bf16[128,1536]{1,0:T(8,128)(2,1)S(1)}, bf16[128,1536]{1,0:T(8,128)(2,1)S(1)}, u32[]{:S(2)}, u32[]{:S(2)}) collective-permute-start(bf16[128,1536]{1,0:T(8,128)(2,1)S(1)} %get-tuple-element.72), channel_id=1, source_target_pairs={{0,96},{1,97},{2,98},{3,99},{4,100},{5,101},{6,102},{7,103},{8,104... | collective-permute-start | bytes 1179656 | tf_op jit(solution)/shard_map/ppermute | solution.py:44
  100.9 7.0 %collective-permute-start.18 = (bf16[128,1536]{1,0:T(8,128)(2,1)S(1)}, bf16[128,1536]{1,0:T(8,128)(2,1)S(1)}, u32[]{:S(2)}, u32[]{:S(2)}) collective-permute-start(bf16[128,1536]{1,0:T(8,128)(2,1)S(1)} %slice.71), channel_id=1, source_target_pairs={{0,96},{1,97},{2,98},{3,99},{4,100},{5,101},{6,102},{7,103},{8,104... | collective-permute-start | bytes 1179656 | tf_op jit(solution)/shard_map/ppermute | solution.py:44
  108.5 7.1 %collective-permute-start.19 = (bf16[128,1536]{1,0:T(8,128)(2,1)S(1)}, bf16[128,1536]{1,0:T(8,128)(2,1)S(1)}, u32[]{:S(2)}, u32[]{:S(2)}) collective-permute-start(bf16[128,1536]{1,0:T(8,128)(2,1)S(1)} %fusion.6), channel_id=1, source_target_pairs={{0,96},{1,97},{2,98},{3,99},{4,100},{5,101},{6,102},{7,103},{8,104... | collective-permute-start | bytes 1179656 | tf_op jit(solution)/shard_map/ppermute | solution.py:44
  108.6 16.3 %collective-permute-start.21 = (bf16[256,1536]{1,0:T(8,128)(2,1)S(1)}, bf16[256,1536]{1,0:T(8,128)(2,1)S(1)}, u32[]{:S(2)}, u32[]{:S(2)}) collective-permute-start(bf16[256,1536]{1,0:T(8,128)(2,1)S(1)} %pad_maximum_fusion.1.near), channel_id=1, source_target_pairs={{0,32},{1,33},{2,34},{3,35},{4,36},{5,37},{6,38},{7,39},{8,40},{9,... | collective-permute-start | bytes 2359304 | tf_op jit(solution)/shard_map/ppermute | solution.py:44
  115.6 23.3 %slice-start = ((s8[4718592]{0:T(1024)(128)(4,1)}), s8[4194304]{0:T(1024)(128)(4,1)S(1)}, s32[]{:S(2)}) async-start(s8[4718592]{0:T(1024)(128)(4,1)} %bitcast.4), calls=%async_computation | async-start | bytes 8388608
  115.7 23.3 %slice-start.1 = ((s8[4718592]{0:T(1024)(128)(4,1)}), s8[524288]{0:T(1024)(128)(4,1)S(1)}, s32[]{:S(2)}) async-start(s8[4718592]{0:T(1024)(128)(4,1)} %bitcast.4), calls=%async_computation.1 | async-start | bytes 1048576
  115.7 23.2 %collective-permute-start.20 = (bf16[256,1536]{1,0:T(8,128)(2,1)S(1)}, bf16[256,1536]{1,0:T(8,128)(2,1)S(1)}, u32[]{:S(2)}, u32[]{:S(2)}) collective-permute-start(bf16[256,1536]{1,0:T(8,128)(2,1)S(1)} %pad_maximum_fusion.2.after.near), channel_id=1, source_target_pairs={{0,32},{1,33},{2,34},{3,35},{4,36},{5,37},{6,38},{7,39},{8,40},{9,... | collective-permute-start | bytes 2359304 | tf_op jit(solution)/shard_map/ppermute | solution.py:44
  134.2 13.9 %collective-permute-start.25 = (bf16[128,3072]{1,0:T(8,128)(2,1)S(1)}, bf16[128,3072]{1,0:T(8,128)(2,1)S(1)}, u32[]{:S(2)}, u32[]{:S(2)}) collective-permute-start(bf16[128,3072]{1,0:T(8,128)(2,1)S(1)} %get-tuple-element.87), channel_id=1, source_target_pairs={{0,1},{1,2},{2,3},{3,0},{4,5},{5,6},{6,7},{7,4},{8,9},{9,10},{10,1... | collective-permute-start | bytes 2359304 | tf_op jit(solution)/shard_map/ppermute | solution.py:44
  135.8 19.7 %collective-permute-start.26 = (bf16[128,3072]{1,0:T(8,128)(2,1)S(1)}, bf16[128,3072]{1,0:T(8,128)(2,1)S(1)}, u32[]{:S(2)}, u32[]{:S(2)}) collective-permute-start(bf16[128,3072]{1,0:T(8,128)(2,1)S(1)} %get-tuple-element.88), channel_id=1, source_target_pairs={{0,2},{1,3},{2,0},{3,1},{4,6},{5,7},{6,4},{7,5},{8,10},{9,11},{10,... | collective-permute-start | bytes 2359304 | tf_op jit(solution)/shard_map/ppermute | solution.py:44
  137.6 19.3 %collective-permute-start.27 = (bf16[128,3072]{1,0:T(8,128)(2,1)S(1)}, bf16[128,3072]{1,0:T(8,128)(2,1)S(1)}, u32[]{:S(2)}, u32[]{:S(2)}) collective-permute-start(bf16[128,3072]{1,0:T(8,128)(2,1)S(1)} %get-tuple-element.89), channel_id=1, source_target_pairs={{0,3},{1,0},{2,1},{3,2},{4,7},{5,4},{6,5},{7,6},{8,11},{9,8},{10,9... | collective-permute-start | bytes 2359304 | tf_op jit(solution)/shard_map/ppermute | solution.py:44
  138.9 19.5 %collective-permute-start.29 = (bf16[512,1536]{1,0:T(8,128)(2,1)S(1)}, bf16[512,1536]{1,0:T(8,128)(2,1)S(1)}, u32[]{:S(2)}, u32[]{:S(2)}) collective-permute-start(bf16[512,1536]{1,0:T(8,128)(2,1)S(1)} %get-tuple-element.81.after.l_own), channel_id=1, source_target_pairs={{0,16},{1,17},{2,18},{3,19},{4,20},{5,21},{6,22},{7,23},{8,24},{9,... | collective-permute-start | bytes 4718600 | tf_op jit(solution)/shard_map/ppermute | solution.py:44
  147.5 17.9 %collective-permute-start.28 = (bf16[512,1536]{1,0:T(8,128)(2,1)S(1)}, bf16[512,1536]{1,0:T(8,128)(2,1)S(1)}, u32[]{:S(2)}, u32[]{:S(2)}) collective-permute-start(bf16[512,1536]{1,0:T(8,128)(2,1)S(1)} %get-tuple-element.91.r_own), channel_id=1, source_target_pairs={{0,16},{1,17},{2,18},{3,19},{4,20},{5,21},{6,22},{7,23},{8,24},{9,... | collective-permute-start | bytes 4718600 | tf_op jit(solution)/shard_map/ppermute | solution.py:44
  148.1 24.3 %collective-permute-start.22 = (bf16[128,3072]{1,0:T(8,128)(2,1)S(1)}, bf16[128,3072]{1,0:T(8,128)(2,1)S(1)}, u32[]{:S(2)}, u32[]{:S(2)}) collective-permute-start(bf16[128,3072]{1,0:T(8,128)(2,1)S(1)} %get-tuple-element.83), channel_id=1, source_target_pairs={{0,1},{1,2},{2,3},{3,0},{4,5},{5,6},{6,7},{7,4},{8,9},{9,10},{10,1... | collective-permute-start | bytes 2359304 | tf_op jit(solution)/shard_map/ppermute | solution.py:44
  155.6 16.8 %collective-permute-start.23 = (bf16[128,3072]{1,0:T(8,128)(2,1)S(1)}, bf16[128,3072]{1,0:T(8,128)(2,1)S(1)}, u32[]{:S(2)}, u32[]{:S(2)}) collective-permute-start(bf16[128,3072]{1,0:T(8,128)(2,1)S(1)} %get-tuple-element.84), channel_id=1, source_target_pairs={{0,2},{1,3},{2,0},{3,1},{4,6},{5,7},{6,4},{7,5},{8,10},{9,11},{10,... | collective-permute-start | bytes 2359304 | tf_op jit(solution)/shard_map/ppermute | solution.py:44
  156.9 15.6 %collective-permute-start.24 = (bf16[128,3072]{1,0:T(8,128)(2,1)S(1)}, bf16[128,3072]{1,0:T(8,128)(2,1)S(1)}, u32[]{:S(2)}, u32[]{:S(2)}) collective-permute-start(bf16[128,3072]{1,0:T(8,128)(2,1)S(1)} %get-tuple-element.85), channel_id=1, source_target_pairs={{0,3},{1,0},{2,1},{3,2},{4,7},{5,4},{6,5},{7,6},{8,11},{9,8},{10,9... | collective-permute-start | bytes 2359304 | tf_op jit(solution)/shard_map/ppermute | solution.py:44
  158.5 6.9 %copy-start.4 = (bf16[512,1536]{1,0:T(8,128)(2,1)S(1)}, bf16[512,1536]{1,0:T(8,128)(2,1)}, u32[]{:S(2)}) copy-start(bf16[512,1536]{1,0:T(8,128)(2,1)} %copy-done.3) | copy-start | bytes 4718596
  173.4 8.2 %collective-permute-start.30 = (bf16[64,3072]{1,0:T(8,128)(2,1)S(1)}, bf16[64,3072]{1,0:T(8,128)(2,1)S(1)}, u32[]{:S(2)}, u32[]{:S(2)}) collective-permute-start(bf16[64,3072]{1,0:T(8,128)(2,1)S(1)} %get-tuple-element.101), channel_id=1, source_target_pairs={{0,4},{1,5},{2,6},{3,7},{4,8},{5,9},{6,10},{7,11},{8,12},{9,13},{1... | collective-permute-start | bytes 1179656 | tf_op jit(solution)/shard_map/ppermute | solution.py:44
  174.8 11.2 %collective-permute-start.31 = (bf16[64,3072]{1,0:T(8,128)(2,1)S(1)}, bf16[64,3072]{1,0:T(8,128)(2,1)S(1)}, u32[]{:S(2)}, u32[]{:S(2)}) collective-permute-start(bf16[64,3072]{1,0:T(8,128)(2,1)S(1)} %get-tuple-element.102), channel_id=1, source_target_pairs={{0,8},{1,9},{2,10},{3,11},{4,12},{5,13},{6,14},{7,15},{8,0},{9,1},... | collective-permute-start | bytes 1179656 | tf_op jit(solution)/shard_map/ppermute | solution.py:44
  176.3 10.1 %collective-permute-start.32 = (bf16[64,3072]{1,0:T(8,128)(2,1)S(1)}, bf16[64,3072]{1,0:T(8,128)(2,1)S(1)}, u32[]{:S(2)}, u32[]{:S(2)}) collective-permute-start(bf16[64,3072]{1,0:T(8,128)(2,1)S(1)} %get-tuple-element.103), channel_id=1, source_target_pairs={{0,12},{1,13},{2,14},{3,15},{4,0},{5,1},{6,2},{7,3},{8,4},{9,5},{1... | collective-permute-start | bytes 1179656 | tf_op jit(solution)/shard_map/ppermute | solution.py:44
  186.6 3.2 %collective-permute-start.33 = (bf16[64,1536]{1,0:T(8,128)(2,1)S(1)}, bf16[64,1536]{1,0:T(8,128)(2,1)S(1)}, u32[]{:S(2)}, u32[]{:S(2)}) collective-permute-start(bf16[64,1536]{1,0:T(8,128)(2,1)S(1)} %slice.65), channel_id=1, source_target_pairs={{0,16},{1,17},{2,18},{3,19},{4,20},{5,21},{6,22},{7,23},{8,24},{9,... | collective-permute-start | bytes 589832 | tf_op jit(solution)/shard_map/ppermute | solution.py:44

commit v4 on v3

--- a/solution.py
+++ b/solution.py
@@ -283,10 +283,11 @@
     place = jnp.stack([level, level ^ far ^ 2, level ^ far, level ^ 2]).astype(jnp.int32)
     half, width = inputs.shape[0] // 2, inputs.shape[1]
 
-    def halves(which):
-        return [lax.dynamic_slice_in_dim(block, which * half, half) for block in (inputs, cotangent)]
-
-    chip = jnp.concatenate([jnp.concatenate(halves(core)), swap(jnp.concatenate(halves(1 - core)))], axis=1)
+    def halves(blocks, which):
+        return jnp.concatenate([lax.dynamic_slice_in_dim(block, which * half, half) for block in blocks])
+
+    theirs, inputs, cotangent = together(halves((inputs, cotangent), 1 - core), inputs, cotangent)
+    chip = jnp.concatenate([halves((inputs, cotangent), core), swap(theirs)], axis=1)
     w_in_late, chip = together(w_in, chip)
     w_in_other = swap(w_in_late)
 

time: 191 us -> 194 us (1.016)
  local copies, waits for them, and re-layouts: 6.58 us -> 11.8 us
    unnamed x14 -> x20, local copies, waits for them, and re-layouts: 4.37 us -> 9.66 us
  transfers between devices with their start and end apart: 34 -> 34, of which waited for: 18 -> 17; matrix products, arithmetic and copies ran while one was open for 1% -> 1% of each run, Pallas kernels for 26% -> 25%
where the time goes in v4:
time: 194 us; the launch traced here: 193 us
  waiting for transfers between devices  87.8 us (45%)
  Pallas kernels  48.9 us (25%)
  starting transfers between devices  40.8 us (21%)
  local copies, waits for them, and re-layouts  11.8 us (6%)
  other arithmetic  3.03 us (2%)
    ppermute x34, waiting for transfers between devices, send(): return lax.ppermute(block, AXES, permutation(**where))  87.8 us
    ppermute x34, starting transfers between devices, send(): return lax.ppermute(block, AXES, permutation(**where))  40.8 us
    pallas_call x2, Pallas kernels, project_up(): pl.pallas_call(functools.partial(up_kernel, transposed), grid=(columns //...  17.2 us
    pallas_call x2, Pallas kernels, project_down(): pl.pallas_call(functools.partial(down_kernel, transposed), grid=(2 * half...  17 us
    pallas_call x2, Pallas kernels, weight_grad(): pl.pallas_call(weight_kernel, grid=(rows // tile,), in_specs=[left, left,...  13.8 us
    unnamed x20, local copies, waits for them, and re-layouts  9.66 us
  transfers between devices with their start and end apart: 34, of which 17 were waited for; matrix products, arithmetic and copies ran while one was open for 1% of the time, Pallas kernels for 25%

profile of v4, /device:TPU:1, one launch (start us, length us, event | category | flops | bytes accessed | tf_op | source)
XLA Modules:
  0.0 193.2 jit_solution(11893354409733748927)
XLA Ops:
  0.7 0.9 copy-done
  1.6 0.9 constant_dynamic-slice_fusion.2
  2.5 1.5 collective-permute-start
  4.0 0.9 constant_dynamic-slice_fusion
  5.1 0.5 collective-permute-start.7
  5.5 1.4 collective-permute-start.3
  6.9 2.6 %collective-permute-start.2 = (bf16[64,3072]{1,0:T(8,128)(2,1)S(1)}, bf16[64,3072]{1,0:T(8,128)(2,1)S(1)}, u32[]{:S(2)}, u32[]{:S(2)}) collective-permute-start(bf16[64,3072]{1,0:T(8,128)(2,1)S(1)} %pad_maximum_fusion.3.p0), channel_id=1, source_target_pairs={{0,8},{1,9},{2,10},{3,11},{4,12},{5,13},{6,14},{7,15},{8,0},{9,1},... | collective-permute-start | bytes 1179656 | tf_op jit(solution)/shard_map/ppermute | solution.py:44
  9.5 1.1 collective-permute-start.1
  10.6 3.2 %collective-permute-done.3.p3 = bf16[64,3072]{1,0:T(8,128)(2,1)S(1)} collective-permute-done((bf16[64,3072]{1,0:T(8,128)(2,1)S(1)}, bf16[64,3072]{1,0:T(8,128)(2,1)S(1)}, u32[]{:S(2)}, u32[]{:S(2)}) %collective-permute-start.3) | collective-permute-done | bytes 393248 | tf_op jit(solution)/shard_map/ppermute | solution.py:44
  13.8 5.4 %collective-permute-done.2.p2 = bf16[64,3072]{1,0:T(8,128)(2,1)S(1)} collective-permute-done((bf16[64,3072]{1,0:T(8,128)(2,1)S(1)}, bf16[64,3072]{1,0:T(8,128)(2,1)S(1)}, u32[]{:S(2)}, u32[]{:S(2)}) %collective-permute-start.2) | collective-permute-done | bytes 393248 | tf_op jit(solution)/shard_map/ppermute | solution.py:44
  19.3 0.8 collective-permute-start.11
  20.1 2.1 %collective-permute-start.4 = (bf16[128,3072]{1,0:T(8,128)(2,1)S(1)}, bf16[128,3072]{1,0:T(8,128)(2,1)S(1)}, u32[]{:S(2)}, u32[]{:S(2)}) collective-permute-start(bf16[128,3072]{1,0:T(8,128)(2,1)S(1)} %pad_maximum_fusion.p0), channel_id=1, source_target_pairs={{0,3},{1,0},{2,1},{3,2},{4,7},{5,4},{6,5},{7,6},{8,11},{9,8},{10,9... | collective-permute-start | bytes 2359304 | tf_op jit(solution)/shard_map/ppermute | solution.py:44
  22.3 1.9 %collective-permute-start.5 = (bf16[128,3072]{1,0:T(8,128)(2,1)S(1)}, bf16[128,3072]{1,0:T(8,128)(2,1)}, u32[]{:S(2)}, u32[]{:S(2)}) collective-permute-start(bf16[128,3072]{1,0:T(8,128)(2,1)S(1)} %pad_maximum_fusion.p0), channel_id=1, source_target_pairs={{0,2},{1,3},{2,0},{3,1},{4,6},{5,7},{6,4},{7,5},{8,10},{9,11},{10,... | collective-permute-start | bytes 2359304 | tf_op jit(solution)/shard_map/ppermute | solution.py:44
  24.2 15.4 %collective-permute-done.4.after.p1 = bf16[128,3072]{1,0:T(8,128)(2,1)S(1)} collective-permute-done((bf16[128,3072]{1,0:T(8,128)(2,1)S(1)}, bf16[128,3072]{1,0:T(8,128)(2,1)S(1)}, u32[]{:S(2)}, u32[]{:S(2)}) %collective-permute-start.4) | collective-permute-done | bytes 786464 | tf_op jit(solution)/shard_map/ppermute | solution.py:44
  39.8 3.4 %collective-permute-done.6.p3 = bf16[128,3072]{1,0:T(8,128)(2,1)S(1)} collective-permute-done((bf16[128,3072]{1,0:T(8,128)(2,1)S(1)}, bf16[128,3072]{1,0:T(8,128)(2,1)S(1)}, u32[]{:S(2)}, u32[]{:S(2)}) %collective-permute-start.6) | collective-permute-done | bytes 786464 | tf_op jit(solution)/shard_map/ppermute | solution.py:44
  43.2 0.9 copy-done.4
  44.3 2.3 %copy-done.3 = bf16[1536,1536]{1,0:T(8,128)(2,1)S(1)} copy-done((bf16[1536,1536]{1,0:T(8,128)(2,1)S(1)}, bf16[1536,1536]{1,0:T(8,128)(2,1)}, u32[]{:S(2)}) %copy-start.3) | copy-done | bytes 4718616
  46.6 1.1 copy-done.5
  47.8 8.6 %shard_map.76 = (f32[256,1536]{1,0:T(8,128)S(1)}, bf16[256,1536]{1,0:T(8,128)(2,1)S(1)}, bf16[512,1536]{1,0:T(8,128)(2,1)S(1)}, bf16[512,1536]{1,0:T(8,128)(2,1)S(1)}) custom-call(s32[4]{0:T(128)S(1)} %pad_add_fusion.place.later.after, bf16[128,3072]{1,0:T(8,128)(2,1)S(1)} %pad_maximum_fusion.p0, bf16[128,3072]{1,0:T(8,128)(2,1)S(1)} %collective-permute-done.4.after.p1, ...), custom_call_target="tpu_custom_call" | custom-call | flops 4831838208 | bytes 15728640 | tf_op jit(solution)/shard_map/pallas_call | solution.py:115
  56.3 1.8 collective-permute-start.13
  58.1 3.8 %collective-permute-start.12 = (bf16[256,1536]{1,0:T(8,128)(2,1)S(1)}, bf16[256,1536]{1,0:T(8,128)(2,1)S(1)}, u32[]{:S(2)}, u32[]{:S(2)}) collective-permute-start(bf16[256,1536]{1,0:T(8,128)(2,1)S(1)} %get-tuple-element.69), channel_id=1, source_target_pairs={{0,32},{1,33},{2,34},{3,35},{4,36},{5,37},{6,38},{7,39},{8,40},{9,... | collective-permute-start | bytes 2359304 | tf_op jit(solution)/shard_map/ppermute | solution.py:44
  61.9 2.6 %collective-permute-start.10 = (bf16[128,3072]{1,0:T(8,128)(2,1)S(1)}, bf16[128,3072]{1,0:T(8,128)(2,1)S(1)}, u32[]{:S(2)}, u32[]{:S(2)}) collective-permute-start(bf16[128,3072]{1,0:T(8,128)(2,1)S(1)} %shard_map.75.after.p0), channel_id=1, source_target_pairs={{0,2},{1,3},{2,0},{3,1},{4,6},{5,7},{6,4},{7,5},{8,10},{9,11},{10,... | collective-permute-start | bytes 2359304 | tf_op jit(solution)/shard_map/ppermute | solution.py:44
  64.5 7.0 %collective-permute-done.12 = bf16[256,1536]{1,0:T(8,128)(2,1)S(1)} collective-permute-done((bf16[256,1536]{1,0:T(8,128)(2,1)S(1)}, bf16[256,1536]{1,0:T(8,128)(2,1)S(1)}, u32[]{:S(2)}, u32[]{:S(2)}) %collective-permute-start.12) | collective-permute-done | bytes 786464 | tf_op jit(solution)/shard_map/ppermute | solution.py:44
  72.0 2.3 %collective-permute-done.10.p2 = bf16[128,3072]{1,0:T(8,128)(2,1)S(1)} collective-permute-done((bf16[128,3072]{1,0:T(8,128)(2,1)S(1)}, bf16[128,3072]{1,0:T(8,128)(2,1)S(1)}, u32[]{:S(2)}, u32[]{:S(2)}) %collective-permute-start.10) | collective-permute-done | bytes 786464 | tf_op jit(solution)/shard_map/ppermute | solution.py:44
  74.2 2.3 %copy-done.2 = bf16[1536,1536]{1,0:T(8,128)(2,1)S(1)} copy-done((bf16[1536,1536]{1,0:T(8,128)(2,1)S(1)}, bf16[1536,1536]{1,0:T(8,128)(2,1)}, u32[]{:S(2)}) %copy-start.2) | copy-done | bytes 4718616
  76.6 8.6 %shard_map.77 = (f32[256,1536]{1,0:T(8,128)S(1)}, bf16[256,1536]{1,0:T(8,128)(2,1)S(1)}, bf16[512,1536]{1,0:T(8,128)(2,1)S(1)}, bf16[512,1536]{1,0:T(8,128)(2,1)S(1)}) custom-call(s32[4]{0:T(128)S(1)} %pad_add_fusion.place.later.after, bf16[128,3072]{1,0:T(8,128)(2,1)S(1)} %shard_map.75.after.p0, bf16[128,3072]{1,0:T(8,128)(2,1)} %collective-permute-done.8.p1, ...), custom_call_target="tpu_custom_call" | custom-call | flops 4831838208 | bytes 15728640 | tf_op jit(solution)/shard_map/pallas_call | solution.py:115
  85.2 1.1 copy-done.6
  86.4 0.4 collective-permute-start.17
  86.8 1.2 collective-permute-start.15
  88.0 0.3 fusion.14
  88.3 0.8 collective-permute-start.16
  89.1 10.4 %collective-permute-done.16 = bf16[128,1536]{1,0:T(8,128)(2,1)S(1)} collective-permute-done((bf16[128,1536]{1,0:T(8,128)(2,1)S(1)}, bf16[128,1536]{1,0:T(8,128)(2,1)S(1)}, u32[]{:S(2)}, u32[]{:S(2)}) %collective-permute-start.16) | collective-permute-done | bytes 393248 | tf_op jit(solution)/shard_map/ppermute | solution.py:44
  99.6 3.5 %collective-permute-done.15 = bf16[256,1536]{1,0:T(8,128)(2,1)S(1)} collective-permute-done((bf16[256,1536]{1,0:T(8,128)(2,1)S(1)}, bf16[256,1536]{1,0:T(8,128)(2,1)S(1)}, u32[]{:S(2)}, u32[]{:S(2)}) %collective-permute-start.15) | collective-permute-done | bytes 786464 | tf_op jit(solution)/shard_map/ppermute | solution.py:44
  103.5 6.9 %collective-permute-done.18 = bf16[128,1536]{1,0:T(8,128)(2,1)S(1)} collective-permute-done((bf16[128,1536]{1,0:T(8,128)(2,1)S(1)}, bf16[128,1536]{1,0:T(8,128)(2,1)S(1)}, u32[]{:S(2)}, u32[]{:S(2)}) %collective-permute-start.18) | collective-permute-done | bytes 393248 | tf_op jit(solution)/shard_map/ppermute | solution.py:44
  110.4 0.6 fusion.6
  111.1 1.6 collective-permute-start.21
  112.7 5.4 %collective-permute-done.19 = bf16[128,1536]{1,0:T(8,128)(2,1)S(1)} collective-permute-done((bf16[128,1536]{1,0:T(8,128)(2,1)S(1)}, bf16[128,1536]{1,0:T(8,128)(2,1)S(1)}, u32[]{:S(2)}, u32[]{:S(2)}) %collective-permute-start.19) | collective-permute-done | bytes 393248 | tf_op jit(solution)/shard_map/ppermute | solution.py:44
  118.2 1.3 collective-permute-start.20
  119.5 7.9 %collective-permute-done.21.far = bf16[256,1536]{1,0:T(8,128)(2,1)S(1)} collective-permute-done((bf16[256,1536]{1,0:T(8,128)(2,1)S(1)}, bf16[256,1536]{1,0:T(8,128)(2,1)S(1)}, u32[]{:S(2)}, u32[]{:S(2)}) %collective-permute-start.21) | collective-permute-done | bytes 786464 | tf_op jit(solution)/shard_map/ppermute | solution.py:44
  127.4 8.5 %shard_map.78 = (bf16[128,3072]{1,0:T(8,128)(2,1)S(1)}, bf16[128,3072]{1,0:T(8,128)(2,1)S(1)}, bf16[128,3072]{1,0:T(8,128)(2,1)S(1)}, bf16[128,3072]{1,0:T(8,128)(2,1)S(1)}, bf16[512,1536]{1,0:T(8,128)(2,1)S(1)}) custom-call(s32[4]{0:T(128)S(1)} %pad_add_fusion.place.later.after, bf16[256,1536]{1,0:T(8,128)(2,1)S(1)} %pad_maximum_fusion.1.near, ...), custom_call_target="tpu_custom_call" | custom-call | flops 4831838208 | bytes 15728640 | tf_op jit(solution)/shard_map/pallas_call | solution.py:171
  135.9 1.7 collective-permute-start.25
  137.6 1.8 collective-permute-start.26
  139.4 1.3 collective-permute-start.27
  140.7 8.5 %shard_map.79 = (bf16[128,3072]{1,0:T(8,128)(2,1)S(1)}, bf16[128,3072]{1,0:T(8,128)(2,1)S(1)}, bf16[128,3072]{1,0:T(8,128)(2,1)S(1)}, bf16[128,3072]{1,0:T(8,128)(2,1)S(1)}, bf16[512,1536]{1,0:T(8,128)(2,1)S(1)}) custom-call(s32[4]{0:T(128)S(1)} %pad_add_fusion.place.later.after, bf16[256,1536]{1,0:T(8,128)(2,1)S(1)} %pad_maximum_fusion.2.after.near, ...), custom_call_target="tpu_custom_call" | custom-call | flops 4831838208 | bytes 15728640 | tf_op jit(solution)/shard_map/pallas_call | solution.py:171
  149.3 0.6 collective-permute-start.28
  149.8 0.7 collective-permute-start.22
  150.6 6.8 %collective-permute-done.26 = bf16[128,3072]{1,0:T(8,128)(2,1)S(1)} collective-permute-done((bf16[128,3072]{1,0:T(8,128)(2,1)S(1)}, bf16[128,3072]{1,0:T(8,128)(2,1)S(1)}, u32[]{:S(2)}, u32[]{:S(2)}) %collective-permute-start.26) | collective-permute-done | bytes 786464 | tf_op jit(solution)/shard_map/ppermute | solution.py:44
  157.3 1.4 collective-permute-start.23
  158.7 1.0 collective-permute-start.24
  159.7 0.5 add_convert_fusion.after.first
  160.3 0.9 copy-done.7
  161.2 6.9 %shard_map.80 = bf16[1536,1536]{1,0:T(8,128)(2,1)} custom-call(bf16[512,1536]{1,0:T(8,128)(2,1)S(1)} %get-tuple-element.87.after.l_own, bf16[512,1536]{1,0:T(8,128)(2,1)S(1)} %collective-permute-done.29.l_other, bf16[512,1536]{1,0:T(8,128)(2,1)S(1)} %copy-done.7, bf16[512,1536]{1,0:T(8,128)(2,1)S(1)} %collective-permute-done.17.r_other, ...), custom_call_target="tpu_custom_call" | custom-call | flops 4831838208 | bytes 11010048 | tf_op jit(solution)/shard_map/pallas_call | solution.py:200
  168.0 6.9 %shard_map.81 = bf16[1536,1536]{1,0:T(8,128)(2,1)} custom-call(bf16[512,1536]{1,0:T(8,128)(2,1)S(1)} %get-tuple-element.96.l_own, bf16[512,1536]{1,0:T(8,128)(2,1)S(1)} %collective-permute-done.13.later.l_other, bf16[512,1536]{1,0:T(8,128)(2,1)S(1)} %get-tuple-element.97.r_own, bf16[512,1536]{1,0:T(8,128)(2,1)S(1)} %collective-permute-done.28.r_other, ...), custom_call_target="tpu_custom_call" | custom-call | flops 4831838208 | bytes 11010048 | tf_op jit(solution)/shard_map/pallas_call | solution.py:200
  174.9 0.8 shard_map.82
  175.8 1.5 collective-permute-start.30
  177.3 1.5 collective-permute-start.31
  178.8 1.0 collective-permute-start.32
  179.8 4.2 %collective-permute-done.30 = bf16[64,3072]{1,0:T(8,128)(2,1)S(1)} collective-permute-done((bf16[64,3072]{1,0:T(8,128)(2,1)S(1)}, bf16[64,3072]{1,0:T(8,128)(2,1)S(1)}, u32[]{:S(2)}, u32[]{:S(2)}) %collective-permute-start.30) | collective-permute-done | bytes 393248 | tf_op jit(solution)/shard_map/ppermute | solution.py:44
  184.0 4.4 %collective-permute-done.31 = bf16[64,3072]{1,0:T(8,128)(2,1)S(1)} collective-permute-done((bf16[64,3072]{1,0:T(8,128)(2,1)S(1)}, bf16[64,3072]{1,0:T(8,128)(2,1)S(1)}, u32[]{:S(2)}, u32[]{:S(2)}) %collective-permute-start.31) | collective-permute-done | bytes 393248 | tf_op jit(solution)/shard_map/ppermute | solution.py:44
  188.4 0.4 collective-permute-done.32
  188.8 0.2 add_convert_fusion.1
  189.1 2.2 %collective-permute-start.33 = (bf16[64,1536]{1,0:T(8,128)(2,1)S(1)}, bf16[64,1536]{1,0:T(8,128)(2,1)S(1)}, u32[]{:S(2)}, u32[]{:S(2)}) collective-permute-start(bf16[64,1536]{1,0:T(8,128)(2,1)S(1)} %slice.65), channel_id=1, source_target_pairs={{0,16},{1,17},{2,18},{3,19},{4,20},{5,21},{6,22},{7,23},{8,24},{9,... | collective-permute-start | bytes 589832 | tf_op jit(solution)/shard_map/ppermute | solution.py:44
  191.3 1.1 collective-permute-done.33
  192.4 0.8 maximum_select_fusion
  (61 shorter events, 1.7 us)
Async XLA Ops:
  0.6 0.9 copy-start
  2.5 2.6 %collective-permute-start = (bf16[64,1536]{1,0:T(8,128)(2,1)S(1)}, bf16[64,1536]{1,0:T(8,128)(2,1)S(1)}, u32[]{:S(2)}, u32[]{:S(2)}) collective-permute-start(bf16[64,1536]{1,0:T(8,128)(2,1)S(1)} %pad_maximum_fusion.4), channel_id=1, source_target_pairs={{0,16},{1,17},{2,18},{3,19},{4,20},{5,21},{6,22},{7,23},{8,24},{9,... | collective-permute-start | bytes 589832 | tf_op jit(solution)/shard_map/ppermute | solution.py:44
  5.1 39.2 %collective-permute-start.7 = (bf16[1536,1536]{1,0:T(8,128)(2,1)}, bf16[1536,1536]{1,0:T(8,128)(2,1)}, u32[]{:S(2)}, u32[]{:S(2)}) collective-permute-start(bf16[1536,1536]{1,0:T(8,128)(2,1)} %w_own.7), channel_id=1, source_target_pairs={{0,16},{1,17},{2,18},{3,19},{4,20},{5,21},{6,22},{7,23},{8,24},{9,... | collective-permute-start | bytes 14155784 | tf_op jit(solution)/shard_map/ppermute | solution.py:44
  5.5 8.3 %collective-permute-start.3 = (bf16[64,3072]{1,0:T(8,128)(2,1)S(1)}, bf16[64,3072]{1,0:T(8,128)(2,1)S(1)}, u32[]{:S(2)}, u32[]{:S(2)}) collective-permute-start(bf16[64,3072]{1,0:T(8,128)(2,1)S(1)} %pad_maximum_fusion.3.p0), channel_id=1, source_target_pairs={{0,4},{1,5},{2,6},{3,7},{4,8},{5,9},{6,10},{7,11},{8,12},{9,13},{1... | collective-permute-start | bytes 1179656 | tf_op jit(solution)/shard_map/ppermute | solution.py:44
  6.9 12.3 %collective-permute-start.2 = (bf16[64,3072]{1,0:T(8,128)(2,1)S(1)}, bf16[64,3072]{1,0:T(8,128)(2,1)S(1)}, u32[]{:S(2)}, u32[]{:S(2)}) collective-permute-start(bf16[64,3072]{1,0:T(8,128)(2,1)S(1)} %pad_maximum_fusion.3.p0), channel_id=1, source_target_pairs={{0,8},{1,9},{2,10},{3,11},{4,12},{5,13},{6,14},{7,15},{8,0},{9,1},... | collective-permute-start | bytes 1179656 | tf_op jit(solution)/shard_map/ppermute | solution.py:44
  9.5 9.7 %collective-permute-start.1 = (bf16[64,3072]{1,0:T(8,128)(2,1)S(1)}, bf16[64,3072]{1,0:T(8,128)(2,1)S(1)}, u32[]{:S(2)}, u32[]{:S(2)}) collective-permute-start(bf16[64,3072]{1,0:T(8,128)(2,1)S(1)} %pad_maximum_fusion.3.p0), channel_id=1, source_target_pairs={{0,12},{1,13},{2,14},{3,15},{4,0},{5,1},{6,2},{7,3},{8,4},{9,5},{1... | collective-permute-start | bytes 1179656 | tf_op jit(solution)/shard_map/ppermute | solution.py:44
  19.3 54.9 %collective-permute-start.11 = (bf16[1536,1536]{1,0:T(8,128)(2,1)}, bf16[1536,1536]{1,0:T(8,128)(2,1)}, u32[]{:S(2)}, u32[]{:S(2)}) collective-permute-start(bf16[1536,1536]{1,0:T(8,128)(2,1)} %w_own.6), channel_id=1, source_target_pairs={{0,16},{1,17},{2,18},{3,19},{4,20},{5,21},{6,22},{7,23},{8,24},{9,... | collective-permute-start | bytes 14155784 | tf_op jit(solution)/shard_map/ppermute | solution.py:44
  20.1 19.5 %collective-permute-start.4 = (bf16[128,3072]{1,0:T(8,128)(2,1)S(1)}, bf16[128,3072]{1,0:T(8,128)(2,1)S(1)}, u32[]{:S(2)}, u32[]{:S(2)}) collective-permute-start(bf16[128,3072]{1,0:T(8,128)(2,1)S(1)} %pad_maximum_fusion.p0), channel_id=1, source_target_pairs={{0,3},{1,0},{2,1},{3,2},{4,7},{5,4},{6,5},{7,6},{8,11},{9,8},{10,9... | collective-permute-start | bytes 2359304 | tf_op jit(solution)/shard_map/ppermute | solution.py:44
  22.3 20.9 %collective-permute-start.6 = (bf16[128,3072]{1,0:T(8,128)(2,1)S(1)}, bf16[128,3072]{1,0:T(8,128)(2,1)S(1)}, u32[]{:S(2)}, u32[]{:S(2)}) collective-permute-start(bf16[128,3072]{1,0:T(8,128)(2,1)S(1)} %pad_maximum_fusion.p0), channel_id=1, source_target_pairs={{0,1},{1,2},{2,3},{3,0},{4,5},{5,6},{6,7},{7,4},{8,9},{9,10},{10,1... | collective-permute-start | bytes 2359304 | tf_op jit(solution)/shard_map/ppermute | solution.py:44
  22.3 22.0 %collective-permute-start.5 = (bf16[128,3072]{1,0:T(8,128)(2,1)S(1)}, bf16[128,3072]{1,0:T(8,128)(2,1)}, u32[]{:S(2)}, u32[]{:S(2)}) collective-permute-start(bf16[128,3072]{1,0:T(8,128)(2,1)S(1)} %pad_maximum_fusion.p0), channel_id=1, source_target_pairs={{0,2},{1,3},{2,0},{3,1},{4,6},{5,7},{6,4},{7,5},{8,10},{9,11},{10,... | collective-permute-start | bytes 2359304 | tf_op jit(solution)/shard_map/ppermute | solution.py:44
  39.7 18.4 %collective-permute-start.9 = (bf16[128,3072]{1,0:T(8,128)(2,1)S(1)}, bf16[128,3072]{1,0:T(8,128)(2,1)S(1)}, u32[]{:S(2)}, u32[]{:S(2)}) collective-permute-start(bf16[128,3072]{1,0:T(8,128)(2,1)S(1)} %shard_map.75.after.p0), channel_id=1, source_target_pairs={{0,1},{1,2},{2,3},{3,0},{4,5},{5,6},{6,7},{7,4},{8,9},{9,10},{10,1... | collective-permute-start | bytes 2359304 | tf_op jit(solution)/shard_map/ppermute | solution.py:44
  43.2 0.9 copy-start.4
  44.1 14.1 %collective-permute-start.8 = (bf16[128,3072]{1,0:T(8,128)(2,1)S(1)}, bf16[128,3072]{1,0:T(8,128)(2,1)}, u32[]{:S(2)}, u32[]{:S(2)}) collective-permute-start(bf16[128,3072]{1,0:T(8,128)(2,1)S(1)} %shard_map.75.after.p0), channel_id=1, source_target_pairs={{0,3},{1,0},{2,1},{3,2},{4,7},{5,4},{6,5},{7,6},{8,11},{9,8},{10,9... | collective-permute-start | bytes 2359304 | tf_op jit(solution)/shard_map/ppermute | solution.py:44
  44.3 2.3 %copy-start.3 = (bf16[1536,1536]{1,0:T(8,128)(2,1)S(1)}, bf16[1536,1536]{1,0:T(8,128)(2,1)}, u32[]{:S(2)}) copy-start(bf16[1536,1536]{1,0:T(8,128)(2,1)} %w_own.7) | copy-start | bytes 14155780
  46.6 1.1 copy-start.5
  56.3 15.5 %collective-permute-start.13 = (bf16[512,1536]{1,0:T(8,128)(2,1)S(1)}, bf16[512,1536]{1,0:T(8,128)(2,1)S(1)}, u32[]{:S(2)}, u32[]{:S(2)}) collective-permute-start(bf16[512,1536]{1,0:T(8,128)(2,1)S(1)} %get-tuple-element.71), channel_id=1, source_target_pairs={{0,16},{1,17},{2,18},{3,19},{4,20},{5,21},{6,22},{7,23},{8,24},{9,... | collective-permute-start | bytes 4718600 | tf_op jit(solution)/shard_map/ppermute | solution.py:44
  58.1 13.4 %collective-permute-start.12 = (bf16[256,1536]{1,0:T(8,128)(2,1)S(1)}, bf16[256,1536]{1,0:T(8,128)(2,1)S(1)}, u32[]{:S(2)}, u32[]{:S(2)}) collective-permute-start(bf16[256,1536]{1,0:T(8,128)(2,1)S(1)} %get-tuple-element.69), channel_id=1, source_target_pairs={{0,32},{1,33},{2,34},{3,35},{4,36},{5,37},{6,38},{7,39},{8,40},{9,... | collective-permute-start | bytes 2359304 | tf_op jit(solution)/shard_map/ppermute | solution.py:44
  61.9 12.3 %collective-permute-start.10 = (bf16[128,3072]{1,0:T(8,128)(2,1)S(1)}, bf16[128,3072]{1,0:T(8,128)(2,1)S(1)}, u32[]{:S(2)}, u32[]{:S(2)}) collective-permute-start(bf16[128,3072]{1,0:T(8,128)(2,1)S(1)} %shard_map.75.after.p0), channel_id=1, source_target_pairs={{0,2},{1,3},{2,0},{3,1},{4,6},{5,7},{6,4},{7,5},{8,10},{9,11},{10,... | collective-permute-start | bytes 2359304 | tf_op jit(solution)/shard_map/ppermute | solution.py:44
  71.9 14.9 %collective-permute-start.14 = (bf16[128,1536]{1,0:T(8,128)(2,1)S(1)}, bf16[128,1536]{1,0:T(8,128)(2,1)S(1)}, u32[]{:S(2)}, u32[]{:S(2)}) collective-permute-start(bf16[128,1536]{1,0:T(8,128)(2,1)S(1)} %slice.72.after), channel_id=1, source_target_pairs={{0,96},{1,97},{2,98},{3,99},{4,100},{5,101},{6,102},{7,103},{8,104... | collective-permute-start | bytes 1179656 | tf_op jit(solution)/shard_map/ppermute | solution.py:44
  74.2 2.3 %copy-start.2 = (bf16[1536,1536]{1,0:T(8,128)(2,1)S(1)}, bf16[1536,1536]{1,0:T(8,128)(2,1)}, u32[]{:S(2)}) copy-start(bf16[1536,1536]{1,0:T(8,128)(2,1)} %w_own.6) | copy-start | bytes 14155780
  85.2 1.1 copy-start.6
  86.4 17.0 %collective-permute-start.17 = (bf16[512,1536]{1,0:T(8,128)(2,1)S(1)}, bf16[512,1536]{1,0:T(8,128)(2,1)S(1)}, u32[]{:S(2)}, u32[]{:S(2)}) collective-permute-start(bf16[512,1536]{1,0:T(8,128)(2,1)S(1)} %get-tuple-element.82), channel_id=1, source_target_pairs={{0,16},{1,17},{2,18},{3,19},{4,20},{5,21},{6,22},{7,23},{8,24},{9,... | collective-permute-start | bytes 4718600 | tf_op jit(solution)/shard_map/ppermute | solution.py:44
  86.8 16.3 %collective-permute-start.15 = (bf16[256,1536]{1,0:T(8,128)(2,1)S(1)}, bf16[256,1536]{1,0:T(8,128)(2,1)S(1)}, u32[]{:S(2)}, u32[]{:S(2)}) collective-permute-start(bf16[256,1536]{1,0:T(8,128)(2,1)S(1)} %get-tuple-element.75), channel_id=1, source_target_pairs={{0,32},{1,33},{2,34},{3,35},{4,36},{5,37},{6,38},{7,39},{8,40},{9,... | collective-permute-start | bytes 2359304 | tf_op jit(solution)/shard_map/ppermute | solution.py:44
  88.3 11.2 %collective-permute-start.16 = (bf16[128,1536]{1,0:T(8,128)(2,1)S(1)}, bf16[128,1536]{1,0:T(8,128)(2,1)S(1)}, u32[]{:S(2)}, u32[]{:S(2)}) collective-permute-start(bf16[128,1536]{1,0:T(8,128)(2,1)S(1)} %get-tuple-element.78), channel_id=1, source_target_pairs={{0,96},{1,97},{2,98},{3,99},{4,100},{5,101},{6,102},{7,103},{8,104... | collective-permute-start | bytes 1179656 | tf_op jit(solution)/shard_map/ppermute | solution.py:44
  103.4 7.0 %collective-permute-start.18 = (bf16[128,1536]{1,0:T(8,128)(2,1)S(1)}, bf16[128,1536]{1,0:T(8,128)(2,1)S(1)}, u32[]{:S(2)}, u32[]{:S(2)}) collective-permute-start(bf16[128,1536]{1,0:T(8,128)(2,1)S(1)} %slice.71), channel_id=1, source_target_pairs={{0,96},{1,97},{2,98},{3,99},{4,100},{5,101},{6,102},{7,103},{8,104... | collective-permute-start | bytes 1179656 | tf_op jit(solution)/shard_map/ppermute | solution.py:44
  111.0 7.2 %collective-permute-start.19 = (bf16[128,1536]{1,0:T(8,128)(2,1)S(1)}, bf16[128,1536]{1,0:T(8,128)(2,1)S(1)}, u32[]{:S(2)}, u32[]{:S(2)}) collective-permute-start(bf16[128,1536]{1,0:T(8,128)(2,1)S(1)} %fusion.6), channel_id=1, source_target_pairs={{0,96},{1,97},{2,98},{3,99},{4,100},{5,101},{6,102},{7,103},{8,104... | collective-permute-start | bytes 1179656 | tf_op jit(solution)/shard_map/ppermute | solution.py:44
  111.1 16.3 %collective-permute-start.21 = (bf16[256,1536]{1,0:T(8,128)(2,1)S(1)}, bf16[256,1536]{1,0:T(8,128)(2,1)S(1)}, u32[]{:S(2)}, u32[]{:S(2)}) collective-permute-start(bf16[256,1536]{1,0:T(8,128)(2,1)S(1)} %pad_maximum_fusion.1.near), channel_id=1, source_target_pairs={{0,32},{1,33},{2,34},{3,35},{4,36},{5,37},{6,38},{7,39},{8,40},{9,... | collective-permute-start | bytes 2359304 | tf_op jit(solution)/shard_map/ppermute | solution.py:44
  118.1 22.6 %slice-start = ((s8[4718592]{0:T(1024)(128)(4,1)}), s8[4194304]{0:T(1024)(128)(4,1)S(1)}, s32[]{:S(2)}) async-start(s8[4718592]{0:T(1024)(128)(4,1)} %bitcast.4), calls=%async_computation | async-start | bytes 8388608
  118.2 22.5 %slice-start.1 = ((s8[4718592]{0:T(1024)(128)(4,1)}), s8[524288]{0:T(1024)(128)(4,1)S(1)}, s32[]{:S(2)}) async-start(s8[4718592]{0:T(1024)(128)(4,1)} %bitcast.4), calls=%async_computation.1 | async-start | bytes 1048576
  118.2 22.5 %collective-permute-start.20 = (bf16[256,1536]{1,0:T(8,128)(2,1)S(1)}, bf16[256,1536]{1,0:T(8,128)(2,1)S(1)}, u32[]{:S(2)}, u32[]{:S(2)}) collective-permute-start(bf16[256,1536]{1,0:T(8,128)(2,1)S(1)} %pad_maximum_fusion.2.after.near), channel_id=1, source_target_pairs={{0,32},{1,33},{2,34},{3,35},{4,36},{5,37},{6,38},{7,39},{8,40},{9,... | collective-permute-start | bytes 2359304 | tf_op jit(solution)/shard_map/ppermute | solution.py:44
  135.9 13.9 %collective-permute-start.25 = (bf16[128,3072]{1,0:T(8,128)(2,1)S(1)}, bf16[128,3072]{1,0:T(8,128)(2,1)S(1)}, u32[]{:S(2)}, u32[]{:S(2)}) collective-permute-start(bf16[128,3072]{1,0:T(8,128)(2,1)S(1)} %get-tuple-element.93), channel_id=1, source_target_pairs={{0,1},{1,2},{2,3},{3,0},{4,5},{5,6},{6,7},{7,4},{8,9},{9,10},{10,1... | collective-permute-start | bytes 2359304 | tf_op jit(solution)/shard_map/ppermute | solution.py:44
  137.6 19.7 %collective-permute-start.26 = (bf16[128,3072]{1,0:T(8,128)(2,1)S(1)}, bf16[128,3072]{1,0:T(8,128)(2,1)S(1)}, u32[]{:S(2)}, u32[]{:S(2)}) collective-permute-start(bf16[128,3072]{1,0:T(8,128)(2,1)S(1)} %get-tuple-element.94), channel_id=1, source_target_pairs={{0,2},{1,3},{2,0},{3,1},{4,6},{5,7},{6,4},{7,5},{8,10},{9,11},{10,... | collective-permute-start | bytes 2359304 | tf_op jit(solution)/shard_map/ppermute | solution.py:44
  139.4 19.3 %collective-permute-start.27 = (bf16[128,3072]{1,0:T(8,128)(2,1)S(1)}, bf16[128,3072]{1,0:T(8,128)(2,1)S(1)}, u32[]{:S(2)}, u32[]{:S(2)}) collective-permute-start(bf16[128,3072]{1,0:T(8,128)(2,1)S(1)} %get-tuple-element.95), channel_id=1, source_target_pairs={{0,3},{1,0},{2,1},{3,2},{4,7},{5,4},{6,5},{7,6},{8,11},{9,8},{10,9... | collective-permute-start | bytes 2359304 | tf_op jit(solution)/shard_map/ppermute | solution.py:44
  140.7 19.5 %collective-permute-start.29 = (bf16[512,1536]{1,0:T(8,128)(2,1)S(1)}, bf16[512,1536]{1,0:T(8,128)(2,1)S(1)}, u32[]{:S(2)}, u32[]{:S(2)}) collective-permute-start(bf16[512,1536]{1,0:T(8,128)(2,1)S(1)} %get-tuple-element.87.after.l_own), channel_id=1, source_target_pairs={{0,16},{1,17},{2,18},{3,19},{4,20},{5,21},{6,22},{7,23},{8,24},{9,... | collective-permute-start | bytes 4718600 | tf_op jit(solution)/shard_map/ppermute | solution.py:44
  149.3 18.8 %collective-permute-start.28 = (bf16[512,1536]{1,0:T(8,128)(2,1)S(1)}, bf16[512,1536]{1,0:T(8,128)(2,1)S(1)}, u32[]{:S(2)}, u32[]{:S(2)}) collective-permute-start(bf16[512,1536]{1,0:T(8,128)(2,1)S(1)} %get-tuple-element.97.r_own), channel_id=1, source_target_pairs={{0,16},{1,17},{2,18},{3,19},{4,20},{5,21},{6,22},{7,23},{8,24},{9,... | collective-permute-start | bytes 4718600 | tf_op jit(solution)/shard_map/ppermute | solution.py:44
  149.8 25.1 %collective-permute-start.22 = (bf16[128,3072]{1,0:T(8,128)(2,1)S(1)}, bf16[128,3072]{1,0:T(8,128)(2,1)S(1)}, u32[]{:S(2)}, u32[]{:S(2)}) collective-permute-start(bf16[128,3072]{1,0:T(8,128)(2,1)S(1)} %get-tuple-element.89), channel_id=1, source_target_pairs={{0,1},{1,2},{2,3},{3,0},{4,5},{5,6},{6,7},{7,4},{8,9},{9,10},{10,1... | collective-permute-start | bytes 2359304 | tf_op jit(solution)/shard_map/ppermute | solution.py:44
  157.3 17.6 %collective-permute-start.23 = (bf16[128,3072]{1,0:T(8,128)(2,1)S(1)}, bf16[128,3072]{1,0:T(8,128)(2,1)S(1)}, u32[]{:S(2)}, u32[]{:S(2)}) collective-permute-start(bf16[128,3072]{1,0:T(8,128)(2,1)S(1)} %get-tuple-element.90), channel_id=1, source_target_pairs={{0,2},{1,3},{2,0},{3,1},{4,6},{5,7},{6,4},{7,5},{8,10},{9,11},{10,... | collective-permute-start | bytes 2359304 | tf_op jit(solution)/shard_map/ppermute | solution.py:44
  158.7 16.2 %collective-permute-start.24 = (bf16[128,3072]{1,0:T(8,128)(2,1)S(1)}, bf16[128,3072]{1,0:T(8,128)(2,1)S(1)}, u32[]{:S(2)}, u32[]{:S(2)}) collective-permute-start(bf16[128,3072]{1,0:T(8,128)(2,1)S(1)} %get-tuple-element.91), channel_id=1, source_target_pairs={{0,3},{1,0},{2,1},{3,2},{4,7},{5,4},{6,5},{7,6},{8,11},{9,8},{10,9... | collective-permute-start | bytes 2359304 | tf_op jit(solution)/shard_map/ppermute | solution.py:44
  159.7 1.4 copy-start.7
  175.8 8.2 %collective-permute-start.30 = (bf16[64,3072]{1,0:T(8,128)(2,1)S(1)}, bf16[64,3072]{1,0:T(8,128)(2,1)S(1)}, u32[]{:S(2)}, u32[]{:S(2)}) collective-permute-start(bf16[64,3072]{1,0:T(8,128)(2,1)S(1)} %get-tuple-element.107), channel_id=1, source_target_pairs={{0,4},{1,5},{2,6},{3,7},{4,8},{5,9},{6,10},{7,11},{8,12},{9,13},{1... | collective-permute-start | bytes 1179656 | tf_op jit(solution)/shard_map/ppermute | solution.py:44
  177.3 11.2 %collective-permute-start.31 = (bf16[64,3072]{1,0:T(8,128)(2,1)S(1)}, bf16[64,3072]{1,0:T(8,128)(2,1)S(1)}, u32[]{:S(2)}, u32[]{:S(2)}) collective-permute-start(bf16[64,3072]{1,0:T(8,128)(2,1)S(1)} %get-tuple-element.108), channel_id=1, source_target_pairs={{0,8},{1,9},{2,10},{3,11},{4,12},{5,13},{6,14},{7,15},{8,0},{9,1},... | collective-permute-start | bytes 1179656 | tf_op jit(solution)/shard_map/ppermute | solution.py:44
  178.8 10.1 %collective-permute-start.32 = (bf16[64,3072]{1,0:T(8,128)(2,1)S(1)}, bf16[64,3072]{1,0:T(8,128)(2,1)S(1)}, u32[]{:S(2)}, u32[]{:S(2)}) collective-permute-start(bf16[64,3072]{1,0:T(8,128)(2,1)S(1)} %get-tuple-element.109), channel_id=1, source_target_pairs={{0,12},{1,13},{2,14},{3,15},{4,0},{5,1},{6,2},{7,3},{8,4},{9,5},{1... | collective-permute-start | bytes 1179656 | tf_op jit(solution)/shard_map/ppermute | solution.py:44
  188.8 4.4 %copy-start.1 = (bf16[64,1536]{1,0:T(8,128)(2,1)S(1)}, bf16[64,1536]{1,0:T(8,128)(2,1)}, u32[]{:S(2)}) copy-start(bf16[64,1536]{1,0:T(8,128)(2,1)} %param.4) | copy-start | bytes 589828
  189.1 3.3 %collective-permute-start.33 = (bf16[64,1536]{1,0:T(8,128)(2,1)S(1)}, bf16[64,1536]{1,0:T(8,128)(2,1)S(1)}, u32[]{:S(2)}, u32[]{:S(2)}) collective-permute-start(bf16[64,1536]{1,0:T(8,128)(2,1)S(1)} %slice.65), channel_id=1, source_target_pairs={{0,16},{1,17},{2,18},{3,19},{4,20},{5,21},{6,22},{7,23},{8,24},{9,... | collective-permute-start | bytes 589832 | tf_op jit(solution)/shard_map/ppermute | solution.py:44
